TPU v7x, 32 devices: a whole 2x2x4 slice. The times are simulated.
32 devices in a mesh: doc: 8 (over z, y), ctx: 4 (over x, core).
Axes of the slice: x: 2, y: 2, z: 4, core: 2. Of those that a mesh axis runs over, the one named last changes fastest.
Arguments:
- tokens: bfloat16 [8, 1024, 5120], P('doc', 'ctx'), may hold values from -640 to 640
- latents: float32 [16, 512], replicated, may hold values from -6 to 6
- w_keys: bfloat16 [5120, 512], replicated, may hold values from -0.078125 to 0.078125
- w_values: bfloat16 [5120, 512], replicated, may hold values from -0.078125 to 0.078125
- w_out: bfloat16 [512, 512], replicated, may hold values from -0.25 to 0.25
- latent_gain: float32 [512], replicated, may hold values from 0.1 to 1.9
- heads_down: bfloat16 [32, 512, 5120], P(('doc', 'ctx')), may hold values from -0.25 to 0.25
- heads_up: bfloat16 [32, 512, 5120], P(('doc', 'ctx')), may hold values from -0.25 to 0.25
- owner: int32 [32], replicated, may hold values from 0 to 31, each once
- requests: bfloat16 [6144, 5120], P(('doc', 'ctx')), may hold values from -6 to 6
- req_doc: int32 [6144], P(('doc', 'ctx')), may hold values from 0 to 7
- req_module: int32 [6144, 1], P(('doc', 'ctx')), may hold values from 0 to 31; in each aligned block of 192 rows (0 to 191, 192 to 383, ...) at most 7 rows name the same one
Outputs:
- adapted: bfloat16 [6144, 5120], P(('doc', 'ctx'))
Inputs may be any that keep to these rules, and one draw needn't show every extreme that they name: Module m's heads are head slot owner[m]; every slot is named once. `req_module`: the 192 request rows of one device name any one module at most 7 times, and in every draw some device names some module exactly 7 times.
All inputs are finite; a program needn't handle non-finite values.
Results may differ from a plain program's by a relative error of at most 0.012.
The roundings to bfloat16 on the way count: a program that leaves them out, or rounds other values in their place, can miss the bound.
Values may be sent and summed in bfloat16 or wider, within the bound.
No kernel may reach another device: no remote copies, remote signals or barrier semaphores. Data moves between devices by JAX's collectives and lax.ppermute only.
A program may use at most 128 MiB of HBM per device.

v0:
```python
import math

import jax
import jax.numpy as jnp
from jax import lax
from jax.sharding import PartitionSpec as P

D = 5120
HEADS = 4


def combined_all(part, axis, combine):
    gathered = jax.tree.map(lambda a: lax.all_gather(a, axis), part)

    def take(source):
        return jax.tree.map(lambda a: lax.dynamic_index_in_dim(a, source, 0, False), gathered)

    return lax.fori_loop(
        1, lax.axis_size(axis), lambda source, state: combine(state, take(source)), take(0)
    )


def combine_pieces(first, second):
    peak_first, total_first, weighted_first = first
    peak_second, total_second, weighted_second = second
    summit = jnp.maximum(peak_first, peak_second)
    ratio_first = jnp.exp(peak_first - summit)
    ratio_second = jnp.exp(peak_second - summit)
    return (
        summit,
        total_first * ratio_first + total_second * ratio_second,
        weighted_first * ratio_first[..., None] + weighted_second * ratio_second[..., None],
    )


def apply_rows(picked_rows, tags, down_factor, up_factor, latent_count):
    coeff = lax.dot_general(
        picked_rows, down_factor, (((1,), (1,)), ((), ())), preferred_element_type=jnp.float32
    ) / math.sqrt(D)
    column_doc = jnp.arange(down_factor.shape[0], dtype=jnp.int32) // latent_count
    matched = tags[:, None] - 1 == column_doc[None, :]
    coeff = jnp.where(matched, coeff, 0.0).astype(jnp.bfloat16)
    return (
        jnp.dot(coeff, up_factor, preferred_element_type=jnp.float32) / math.sqrt(latent_count)
    ).astype(jnp.bfloat16)


def on_device(
    tokens,
    latents,
    w_keys,
    w_values,
    w_out,
    latent_gain,
    heads_down,
    heads_up,
    owner,
    requests,
    req_doc,
    req_module,
):
    local_tokens = tokens[0]
    latent_count, width = latents.shape
    head_dim = width // HEADS
    key_rows = jnp.dot(local_tokens, w_keys, preferred_element_type=jnp.float32).astype(
        jnp.bfloat16
    )
    value_rows = jnp.dot(local_tokens, w_values, preferred_element_type=jnp.float32).astype(
        jnp.bfloat16
    )
    queries = latents.astype(jnp.bfloat16).reshape(latent_count, HEADS, head_dim)
    scores = jnp.einsum(
        "ihe,the->hit",
        queries,
        key_rows.reshape(-1, HEADS, head_dim),
        preferred_element_type=jnp.float32,
    ) / math.sqrt(head_dim)
    score_peak = jnp.max(scores, axis=-1)
    expo = jnp.exp(scores - score_peak[..., None])
    weight_sum = jnp.sum(expo, axis=-1)
    weighted = jnp.einsum(
        "hit,the->hie",
        expo,
        value_rows.astype(jnp.float32).reshape(-1, HEADS, head_dim),
        precision=lax.Precision.HIGHEST,
    )
    score_peak, weight_sum, weighted = combined_all(
        (score_peak, weight_sum, weighted), "ctx", combine_pieces
    )
    attended = (
        (weighted / weight_sum[..., None])
        .transpose(1, 0, 2)
        .reshape(latent_count, width)
        .astype(jnp.bfloat16)
    )
    mixed_state = latents + jnp.dot(attended, w_out, preferred_element_type=jnp.float32)
    summary = (
        mixed_state
        * lax.rsqrt(jnp.mean(mixed_state * mixed_state, axis=-1, keepdims=True) + 1e-06)
        * latent_gain
    )
    summary = summary.astype(jnp.bfloat16)
    summaries = lax.all_gather(summary[None], "doc", axis=0, tiled=True).reshape(-1, width)
    down_factor = jnp.dot(summaries, heads_down[0], preferred_element_type=jnp.float32).astype(
        jnp.bfloat16
    )
    up_factor = jnp.dot(summaries, heads_up[0], preferred_element_type=jnp.float32).astype(
        jnp.bfloat16
    )
    doc_count = lax.axis_size("doc")
    ctx_count = lax.axis_size("ctx")
    device_count = doc_count * ctx_count
    req_rows = requests.shape[0]
    model_width = requests.shape[1]
    capacity = max(2, req_rows // device_count + 1)
    modules_row = req_module[:, 0]
    module_ids = jnp.arange(device_count, dtype=jnp.int32)
    target_dev = jnp.sum(
        jnp.where(modules_row[:, None] == module_ids[None, :], owner[None, :], 0), axis=1
    )
    row_ids = jnp.arange(req_rows, dtype=jnp.int32)
    earlier = (modules_row[:, None] == modules_row[None, :]) & (row_ids[None, :] < row_ids[:, None])
    slot_index = target_dev * capacity + jnp.sum(earlier.astype(jnp.int32), axis=1)
    placed = slot_index[None, :] == jnp.arange(device_count * capacity, dtype=jnp.int32)[:, None]
    placer = placed.astype(jnp.bfloat16)
    sent_rows = jnp.dot(placer, requests, preferred_element_type=jnp.float32).astype(jnp.bfloat16)
    sent_rows = sent_rows.reshape(device_count, capacity, model_width)
    sent_tags = jnp.sum(jnp.where(placed, req_doc[None, :] + 1, 0), axis=1).reshape(
        device_count, capacity
    )
    arrived_rows = lax.all_to_all(
        sent_rows, ("doc", "ctx"), split_axis=0, concat_axis=0, tiled=True
    )
    arrived_tags = lax.all_to_all(
        sent_tags, ("doc", "ctx"), split_axis=0, concat_axis=0, tiled=True
    )
    sources, items = arrived_tags.shape
    update = apply_rows(
        arrived_rows.reshape(sources * items, model_width),
        arrived_tags.reshape(-1),
        down_factor,
        up_factor,
        latent_count,
    )
    update = update.reshape(sources, items, model_width)
    returned_rows = lax.all_to_all(update, ("doc", "ctx"), split_axis=0, concat_axis=0, tiled=True)
    returned_rows = returned_rows.reshape(device_count * capacity, model_width)
    gathered = lax.dot_general(
        placer, returned_rows, (((0,), (0,)), ((), ())), preferred_element_type=jnp.float32
    )
    return (requests.astype(jnp.float32) + gathered).astype(jnp.bfloat16)


def solution(mesh):
    in_specs = (
        P("doc", "ctx", None),
        P(),
        P(),
        P(),
        P(),
        P(),
        P(("doc", "ctx"), None, None),
        P(("doc", "ctx"), None, None),
        P(),
        P(("doc", "ctx"), None),
        P(("doc", "ctx")),
        P(("doc", "ctx"), None),
    )
    out_specs = P(("doc", "ctx"), None)
    return jax.shard_map(
        on_device, mesh=mesh, in_specs=in_specs, out_specs=out_specs, check_vma=False
    )
```

profile of v0, /device:TPU:0, one launch (start us, length us, event | category | flops | bytes accessed | tf_op | source)
XLA Modules:
  0.0 196.0 jit_solution(2362889515427439343)
XLA Ops:
  0.0 1.0 convert_reduce_fusion
  1.0 0.8 select_reduce_fusion.1
  1.8 0.7 multiply_add_fusion
  2.5 0.1 select_reduce_fusion
  2.6 0.7 all_to_all.12
  3.4 7.3 %all-to-all-start = ((s32[32,1,7]{2,1,0:T(1,128)}), s32[32,1,7]{2,1,0:T(1,128)S(1)}, u32[]{:S(2)}, u32[]{:S(2)}) async-start(s32[32,1,7]{2,1,0:T(1,128)} %bitcast.4), calls=%async_computation | async-start | bytes 32768 | tf_op jit(solution)/shard_map/all_to_all | solution.py:134
  10.7 3.8 %convolution_convert_fusion = bf16[224,5120]{1,0:T(8,128)(2,1)} fusion(bf16[192,5120]{1,0:T(8,128)(2,1)} %param.23, s32[192]{0:T(256)S(1)} %get-tuple-element.206), kind=kOutput, calls=%fused_computation.11 | convolution fusion | flops 441591808 | bytes 4260608 | tf_op jit(solution)/shard_map/dot_general | solution.py:126
  14.5 4.2 %reshape.76 = bf16[32,7,5120]{2,1,0:T(8,128)(2,1)} reshape(bf16[224,5120]{1,0:T(8,128)(2,1)} %convolution_convert_fusion) | data formatting | bytes 4587520 | tf_op jit(solution)/shard_map/reshape | solution.py:127
  18.7 5.9 %all-to-all-start.1 = ((bf16[32,7,5120]{2,1,0:T(8,128)(2,1)}), bf16[32,7,5120]{2,1,0:T(8,128)(2,1)}, u32[]{:S(2)}, u32[]{:S(2)}) async-start(bf16[32,7,5120]{2,1,0:T(8,128)(2,1)} %reshape.76), calls=%async_computation.1 | async-start | bytes 5242880 | tf_op jit(solution)/shard_map/all_to_all | solution.py:131
  24.7 4.0 %fusion.25 = bf16[32,4,8,128]{3,2,1,0:T(8,128)(2,1)S(1)} fusion(bf16[5120,512]{1,0:T(8,128)(2,1)} %param.16, bf16[1,256,5120]{2,1,0:T(8,128)(2,1)S(1)} %copy-done), kind=kOutput, calls=%fused_computation.25 | convolution fusion | flops 1342308352 | bytes 8126464 | tf_op jit(solution)/shard_map/dot_general | solution.py:65
  28.7 0.2 fusion.54
  29.0 4.1 %fusion.22 = bf16[32,4,8,128]{3,2,1,0:T(8,128)(2,1)S(1)} fusion(bf16[5120,512]{1,0:T(8,128)(2,1)} %param.17, bf16[1,256,5120]{2,1,0:T(8,128)(2,1)S(1)} %copy-done), kind=kOutput, calls=%fused_computation.24 | convolution fusion | flops 1342308352 | bytes 8126464 | tf_op jit(solution)/shard_map/dot_general | solution.py:68
  33.1 0.3 fusion.38
  33.3 11.3 %all-gather.2 = f32[16,16,128]{2,1,0:T(8,128)S(1)} all-gather(f32[4,16,128]{2,1,0:T(8,128)S(1)} %fusion.38), channel_id=4, replica_groups=mesh['doc'=8,'ctx'=4] {'ctx'}, dimensions={0}, use_global_device_ids=true | all-gather | bytes 163840 | tf_op jit(solution)/shard_map/all_gather | solution.py:13
  44.7 5.1 %all-gather.4 = f32[4,4,16]{2,1,0:T(4,128)S(1)} all-gather(f32[1,4,16]{2,1,0:T(4,128)S(1)} %bitcast.100), channel_id=2, replica_groups=mesh['doc'=8,'ctx'=4] {'ctx'}, dimensions={0}, use_global_device_ids=true | all-gather | bytes 1280 | tf_op jit(solution)/shard_map/all_gather | solution.py:13
  49.8 0.2 fusion.46
  50.0 5.3 %all-gather.5 = f32[4,4,16]{2,1,0:T(4,128)S(1)} all-gather(f32[1,4,16]{2,1,0:T(4,128)S(1)} %bitcast.103), channel_id=3, replica_groups=mesh['doc'=8,'ctx'=4] {'ctx'}, dimensions={0}, use_global_device_ids=true | all-gather | bytes 1280 | tf_op jit(solution)/shard_map/all_gather | solution.py:13
  55.3 0.4 while.19
  55.4 0.1 fusion.69
  55.5 0.1 fusion.69
  55.6 0.1 fusion.69
  55.7 0.3 multiply_reduce_fusion
  56.1 0.1 multiply_convert_fusion
  56.2 48.4 %all-gather.3 = bf16[128,512]{1,0:T(8,128)(2,1)S(1)} all-gather(bf16[16,512]{1,0:T(8,128)(2,1)S(1)} %multiply_convert_fusion), channel_id=5, replica_groups=mesh['doc'=8,'ctx'=4] {'doc'}, dimensions={0}, use_global_device_ids=true | all-gather | bytes 147456 | tf_op jit(solution)/shard_map/all_gather | solution.py:103
  104.7 0.1 sub.41
  104.8 4.3 %reshape.77 = bf16[224,5120]{1,0:T(8,128)(2,1)} reshape(bf16[32,7,5120]{2,1,0:T(8,128)(2,1)} %all-to-all-done.1) | data formatting | bytes 4587520 | tf_op jit(solution)/shard_map/reshape | solution.py:139
  109.0 4.6 %fusion.34 = bf16[224,128]{1,0:T(8,128)(2,1)S(1)} fusion(bf16[224,5120]{1,0:T(8,128)(2,1)} %reshape.77, bf16[128,512]{1,0:T(8,128)(2,1)S(1)} %all-gather.3, bf16[1,512,5120]{2,1,0:T(8,128)(2,1)} %param.20, s32[128]{0:T(128)S(1)} %and_select_fusion, s32[224]{0:T(256)S(1)} %sub.41), kind=kOutput, calls=%fused_computation.28 | convolution fusion | flops 965459968 | bytes 7726464 | tf_op jit(solution)/shard_map/dot_general | solution.py:37
  113.7 5.3 %fusion.3 = bf16[224,5120]{1,0:T(8,128)(2,1)} fusion(bf16[224,128]{1,0:T(8,128)(2,1)S(1)} %fusion.34, bf16[128,512]{1,0:T(8,128)(2,1)S(1)} %all-gather.3, bf16[1,512,5120]{2,1,0:T(8,128)(2,1)} %param.21), kind=kOutput, calls=%fused_computation.10 | convolution fusion | flops 967639040 | bytes 7725056 | tf_op jit(solution)/shard_map/dot_general | solution.py:44
  119.0 4.2 %reshape.82 = bf16[32,7,5120]{2,1,0:T(8,128)(2,1)} reshape(bf16[224,5120]{1,0:T(8,128)(2,1)} %fusion.3) | data formatting | bytes 4587520 | tf_op jit(solution)/shard_map/reshape | solution.py:145
  123.3 64.3 %all_to_all.19 = bf16[32,7,5120]{2,1,0:T(8,128)(2,1)} all-to-all(bf16[32,7,5120]{2,1,0:T(8,128)(2,1)} %reshape.82), channel_id=1, replica_groups=mesh['doc'=8,'ctx'=4] {'doc','ctx'}, dimensions={0} | all-to-all | bytes 4587520 | tf_op jit(solution)/shard_map/all_to_all | solution.py:146
  187.5 4.3 %reshape.83 = bf16[224,5120]{1,0:T(8,128)(2,1)} reshape(bf16[32,7,5120]{2,1,0:T(8,128)(2,1)} %all_to_all.19) | data formatting | bytes 4587520 | tf_op jit(solution)/shard_map/reshape | solution.py:147
  191.8 4.2 %fusion.4 = bf16[192,5120]{1,0:T(8,128)(2,1)} fusion(bf16[224,5120]{1,0:T(8,128)(2,1)} %reshape.83, bf16[192,5120]{1,0:T(8,128)(2,1)} %param.23, s32[192]{0:T(256)S(1)} %get-tuple-element.206), kind=kOutput, calls=%fused_computation.12 | convolution fusion | flops 443394048 | bytes 6226688 | tf_op jit(solution)/shard_map/dot_general | solution.py:148
  (19 shorter events, 0.2 us)
Async XLA Ops:
  0.0 24.7 %copy-start = (bf16[1,256,5120]{2,1,0:T(8,128)(2,1)S(1)}, bf16[1,256,5120]{2,1,0:T(8,128)(2,1)}, u32[]{:S(2)}) copy-start(bf16[1,256,5120]{2,1,0:T(8,128)(2,1)} %param.14) | copy-start | bytes 7864324
  3.4 15.4 %all-to-all-start = ((s32[32,1,7]{2,1,0:T(1,128)}), s32[32,1,7]{2,1,0:T(1,128)S(1)}, u32[]{:S(2)}, u32[]{:S(2)}) async-start(s32[32,1,7]{2,1,0:T(1,128)} %bitcast.4), calls=%async_computation | async-start | bytes 32768 | tf_op jit(solution)/shard_map/all_to_all | solution.py:134
  18.7 86.1 %all-to-all-start.1 = ((bf16[32,7,5120]{2,1,0:T(8,128)(2,1)}), bf16[32,7,5120]{2,1,0:T(8,128)(2,1)}, u32[]{:S(2)}, u32[]{:S(2)}) async-start(bf16[32,7,5120]{2,1,0:T(8,128)(2,1)} %reshape.76), calls=%async_computation.1 | async-start | bytes 5242880 | tf_op jit(solution)/shard_map/all_to_all | solution.py:131
  24.7 4.0 %copy-start.2 = (f32[16,512]{1,0:T(8,128)S(1)}, f32[16,512]{1,0:T(8,128)}, u32[]{:S(2)}) copy-start(f32[16,512]{1,0:T(8,128)} %param.15) | copy-start | bytes 98308
  29.0 26.8 %copy-start.1 = (bf16[512,512]{1,0:T(8,128)(2,1)S(1)}, bf16[512,512]{1,0:T(8,128)(2,1)}, u32[]{:S(2)}) copy-start(bf16[512,512]{1,0:T(8,128)(2,1)} %param.18) | copy-start | bytes 1572868
  29.0 27.1 %copy-start.3 = (f32[512]{0:T(512)S(1)}, f32[512]{0:T(512)}, u32[]{:S(2)}) copy-start(f32[512]{0:T(512)} %param.19) | copy-start | bytes 6148
where the time goes:
time: 197 us; the launch traced here: 196 us
  blocking collectives  135 us (69%)
  matrix products  26.9 us (14%)
  local copies, waits for them, and re-layouts  17.8 us (9%)
  starting transfers between devices  13.2 us (7%)
  other arithmetic  3.26 us (2%)
    all_to_all x1, blocking collectives, on_device(): lax.all_to_all(update, ('doc', 'ctx'), split_axis=0, concat_axis=0, tiled...  64.3 us
    all_gather x1, blocking collectives, on_device(): lax.all_gather(summary[None], 'doc', axis=0, tiled=True).reshape(-1, width)  48.4 us
    all_gather x3, blocking collectives, combined_all(): gathered = jax.tree.map(lambda a: lax.all_gather(a, axis), part)  21.8 us
    all_to_all x1, starting transfers between devices, on_device(): lax.all_to_all(sent_tags, ('doc', 'ctx'), split_axis=0, concat_axis=0, ti...  7.3 us
    all_to_all x1, starting transfers between devices, on_device(): lax.all_to_all(sent_rows, ('doc', 'ctx'), split_axis=0, concat_axis=0, ti...  5.95 us
    dot_general x1, matrix products, apply_rows(): jnp.dot(coeff, up_factor, preferred_element_type=jnp.float32)  5.34 us
    dot_general x1, matrix products, apply_rows(): lax.dot_general(picked_rows, down_factor, (((1,), (1,)), ((), ())), prefe...  4.64 us
    reshape x1, local copies, waits for them, and re-layouts, on_device(): arrived_rows.reshape(sources * items, model_width)  4.26 us
  transfers between devices with their start and end apart: 2, of which 0 were waited for; matrix products, arithmetic and copies ran while one was open for 9% of the time, Pallas kernels for 0%

commit v1 on v0

v1 whole, which is shorter than its diff:
```python
import functools
import math

import jax
import jax.numpy as jnp
from jax import lax
from jax.experimental import pallas as pl
from jax.experimental.pallas import tpu as pltpu
from jax.sharding import PartitionSpec as P

HEADS = 4
SUB = 8
LANES = 128
ALL = ("doc", "ctx")


def compiler_params():
    return pltpu.CompilerParams(vmem_limit_bytes=48 * 1024 * 1024)


def scatter_pieces(stage, piece_index, values, blocks, capacity, piece):
    for slot in range(capacity):
        for lane in range(piece // LANES):
            stage[
                slot * (piece // LANES) + lane, pl.ds(piece_index, blocks, stride=SUB), :
            ] = values[slot * blocks : (slot + 1) * blocks, lane * LANES : (lane + 1) * LANES]


def gather_pieces(stage, piece_index, blocks, capacity, piece):
    return jnp.concatenate(
        [
            jnp.concatenate(
                [
                    stage[slot * (piece // LANES) + lane, pl.ds(piece_index, blocks, stride=SUB), :]
                    for lane in range(piece // LANES)
                ],
                axis=1,
            ).astype(jnp.bfloat16)
            for slot in range(capacity)
        ],
        axis=0,
    )


def fill_stage(stage, source):
    for lane in range(stage.shape[0]):
        stage[lane] = source[:, lane * LANES : (lane + 1) * LANES].astype(jnp.float32)


def drain_stage(stage, target):
    for lane in range(stage.shape[0]):
        target[:, lane * LANES : (lane + 1) * LANES] = stage[lane].astype(target.dtype)


def slot_of_rows(module_column, module_row, owner_column, blocks):
    rows = module_row.shape[1]
    module_ids = lax.broadcasted_iota(jnp.int32, (blocks, rows), 0)
    target = jnp.sum(
        jnp.where(module_ids == module_row, owner_column, 0), axis=0, keepdims=True
    )
    first = lax.broadcasted_iota(jnp.int32, (rows, rows), 0)
    second = lax.broadcasted_iota(jnp.int32, (rows, rows), 1)
    earlier = (module_column == module_row) & (first < second)
    rank = jnp.sum(earlier.astype(jnp.int32), axis=0, keepdims=True)
    return rank * blocks + target


def place_kernel(
    blocks, capacity, module_column, module_row, owner_column, doc_row, requests, sent, tags, slots, stage
):
    rows, width = requests.shape
    piece = width // SUB
    slot_row = slot_of_rows(module_column[...], module_row[...], owner_column[...], blocks)
    slots[...] = slot_row
    placed = lax.broadcasted_iota(jnp.int32, (capacity * blocks, rows), 0) == slot_row
    tags[...] = jnp.sum(
        jnp.where(placed, doc_row[...] + 1, 0), axis=1, keepdims=True
    )
    placer = placed.astype(jnp.float32).astype(jnp.bfloat16)
    for index in range(SUB):
        moved = jnp.dot(
            placer,
            requests[:, index * piece : (index + 1) * piece],
            preferred_element_type=jnp.float32,
        )
        scatter_pieces(stage, index, moved, blocks, capacity, piece)
    drain_stage(stage, sent)


def apply_kernel(blocks, capacity, latent_count, arrived, tags, column_doc, down, up, update, stage):
    width = down.shape[1]
    piece = width // SUB
    fill_stage(stage, arrived)
    coeff = None
    for index in range(SUB):
        part = lax.dot_general(
            gather_pieces(stage, index, blocks, capacity, piece),
            down[:, index * piece : (index + 1) * piece],
            (((1,), (1,)), ((), ())),
            preferred_element_type=jnp.float32,
        )
        coeff = part if coeff is None else coeff + part
    matched = tags[...] - 1 == column_doc[...]
    coeff = jnp.where(matched, coeff * (1.0 / math.sqrt(width)), 0.0).astype(jnp.bfloat16)
    for index in range(SUB):
        moved = jnp.dot(
            coeff, up[:, index * piece : (index + 1) * piece], preferred_element_type=jnp.float32
        ) * (1.0 / math.sqrt(latent_count))
        scatter_pieces(stage, index, moved, blocks, capacity, piece)
    drain_stage(stage, update)


def finish_kernel(blocks, capacity, returned, slots, requests, adapted, stage):
    rows, width = requests.shape
    piece = width // SUB
    fill_stage(stage, returned)
    placed = lax.broadcasted_iota(jnp.int32, (capacity * blocks, rows), 0) == slots[...]
    placer = placed.astype(jnp.float32).astype(jnp.bfloat16)
    for index in range(SUB):
        gathered = lax.dot_general(
            placer,
            gather_pieces(stage, index, blocks, capacity, piece),
            (((0,), (0,)), ((), ())),
            preferred_element_type=jnp.float32,
        )
        columns = slice(index * piece, (index + 1) * piece)
        adapted[:, columns] = (requests[:, columns].astype(jnp.float32) + gathered).astype(
            adapted.dtype
        )


def on_device(
    tokens,
    latents,
    w_keys,
    w_values,
    w_out,
    latent_gain,
    heads_down,
    heads_up,
    owner,
    requests,
    req_doc,
    req_module,
):
    doc_count = lax.axis_size("doc")
    ctx_count = lax.axis_size("ctx")
    blocks = doc_count * ctx_count
    rows, width = requests.shape
    capacity = max(2, rows // blocks + 1)
    piece = width // SUB
    latent_count, latent_width = latents.shape
    head_dim = latent_width // HEADS
    my_doc = lax.axis_index("doc")
    my_ctx = lax.axis_index("ctx")
    stage = pltpu.VMEM((capacity * piece // LANES, blocks * SUB, LANES), jnp.float32)
    block_shape = jax.ShapeDtypeStruct((blocks * SUB, capacity * piece), jnp.bfloat16)

    def exchange(values):
        return lax.all_to_all(
            values.reshape(blocks, SUB, capacity * piece), ALL, split_axis=0, concat_axis=0, tiled=True
        ).reshape(blocks * SUB, capacity * piece)

    sent, tags, slots = pl.pallas_call(
        functools.partial(place_kernel, blocks, capacity),
        out_shape=(
            block_shape,
            jax.ShapeDtypeStruct((capacity * blocks, 1), jnp.int32),
            jax.ShapeDtypeStruct((1, rows), jnp.int32),
        ),
        scratch_shapes=[stage],
        compiler_params=compiler_params(),
        name="place_rows",
    )(req_module, req_module.reshape(1, rows), owner.reshape(blocks, 1), req_doc.reshape(1, rows), requests)
    arrived = exchange(sent)

    local_tokens = tokens[0]
    key_rows = jnp.dot(local_tokens, w_keys, preferred_element_type=jnp.float32).astype(jnp.bfloat16)
    value_rows = jnp.dot(local_tokens, w_values, preferred_element_type=jnp.float32).astype(
        jnp.bfloat16
    )
    queries = latents.astype(jnp.bfloat16).reshape(latent_count, HEADS, head_dim)
    scores = jnp.einsum(
        "ihe,the->hit",
        queries,
        key_rows.reshape(-1, HEADS, head_dim),
        preferred_element_type=jnp.float32,
    ) / math.sqrt(head_dim)
    score_peak = jnp.max(scores, axis=-1)
    expo = jnp.exp(scores - score_peak[..., None])
    weight_sum = jnp.sum(expo, axis=-1)
    weighted = jnp.einsum(
        "hit,the->hie",
        expo,
        value_rows.astype(jnp.float32).reshape(-1, HEADS, head_dim),
        precision=lax.Precision.HIGHEST,
    )
    entries = HEADS * latent_count
    tag_count = capacity * blocks
    extra = jnp.concatenate(
        [score_peak.reshape(-1), weight_sum.reshape(-1), tags[:, 0].astype(jnp.float32)]
    )
    extra_rows = -(-extra.shape[0] // head_dim)
    extra = jnp.pad(extra, (0, extra_rows * head_dim - extra.shape[0])).reshape(extra_rows, head_dim)
    mine = jnp.concatenate([weighted.reshape(entries, head_dim), extra], axis=0)
    pieces = lax.all_gather(mine, "ctx")
    weighted = pieces[:, :entries]
    extra = pieces[:, entries:].reshape(ctx_count, -1)
    score_peak = extra[:, :entries]
    weight_sum = extra[:, entries : 2 * entries]
    ctx_tags = extra[:, 2 * entries : 2 * entries + tag_count]
    ratio = jnp.exp(score_peak - jnp.max(score_peak, axis=0, keepdims=True))
    total = jnp.sum(weight_sum * ratio, axis=0)
    weighted = jnp.sum(weighted * ratio[..., None], axis=0)
    attended = (
        (weighted / total[:, None])
        .reshape(HEADS, latent_count, head_dim)
        .transpose(1, 0, 2)
        .reshape(latent_count, latent_width)
        .astype(jnp.bfloat16)
    )
    mixed_state = latents + jnp.dot(attended, w_out, preferred_element_type=jnp.float32)
    summary = (
        mixed_state
        * lax.rsqrt(jnp.mean(mixed_state * mixed_state, axis=-1, keepdims=True) + 1e-06)
        * latent_gain
    ).astype(jnp.bfloat16)

    tag_rows = -(-(ctx_count * tag_count) // latent_width)
    flat_tags = ctx_tags.astype(jnp.bfloat16).reshape(-1)
    flat_tags = jnp.pad(flat_tags, (0, tag_rows * latent_width - flat_tags.shape[0]))
    packet = jnp.concatenate([summary, flat_tags.reshape(tag_rows, latent_width)], axis=0)
    share = doc_count // ctx_count
    fetched = []
    for turn in range(share):
        pairs = [
            (doc * ctx_count + ctx, (doc ^ (ctx * share + turn)) * ctx_count + ctx)
            for doc in range(doc_count)
            for ctx in range(ctx_count)
        ]
        fetched.append(lax.ppermute(packet, ALL, pairs))
    everyone = lax.all_gather(jnp.stack(fetched), "ctx").reshape(
        doc_count, latent_count + tag_rows, latent_width
    )
    summaries = everyone[:, :latent_count].reshape(doc_count * latent_count, latent_width)
    column_doc = (
        jnp.arange(doc_count * latent_count, dtype=jnp.int32)[None, :] // latent_count
    ) ^ my_doc
    all_tags = everyone[:, latent_count:].reshape(doc_count, -1)[:, : ctx_count * tag_count]
    all_tags = all_tags.reshape(doc_count, ctx_count, capacity, blocks)
    me = my_doc * ctx_count + my_ctx
    my_tags = jnp.sum(
        jnp.where(jnp.arange(blocks) == me, all_tags.astype(jnp.float32), 0.0), axis=-1
    )
    by_doc = jnp.arange(doc_count, dtype=jnp.int32)
    unmix = (by_doc[:, None] ^ my_doc) == by_doc[None, :]
    my_tags = jnp.sum(jnp.where(unmix[:, :, None, None], my_tags[None], 0.0), axis=1)
    my_tags = my_tags.transpose(2, 0, 1).reshape(tag_count, 1).astype(jnp.int32)

    down_factor = jnp.dot(summaries, heads_down[0], preferred_element_type=jnp.float32).astype(
        jnp.bfloat16
    )
    up_factor = jnp.dot(summaries, heads_up[0], preferred_element_type=jnp.float32).astype(
        jnp.bfloat16
    )
    update = pl.pallas_call(
        functools.partial(apply_kernel, blocks, capacity, latent_count),
        out_shape=block_shape,
        scratch_shapes=[stage],
        compiler_params=compiler_params(),
        name="apply_rows",
    )(arrived, my_tags, column_doc, down_factor, up_factor)
    returned = exchange(update)
    return pl.pallas_call(
        functools.partial(finish_kernel, blocks, capacity),
        out_shape=jax.ShapeDtypeStruct((rows, width), jnp.bfloat16),
        scratch_shapes=[stage],
        compiler_params=compiler_params(),
        name="finish_rows",
    )(returned, slots, requests)


def solution(mesh):
    in_specs = (
        P("doc", "ctx", None),
        P(),
        P(),
        P(),
        P(),
        P(),
        P(ALL, None, None),
        P(ALL, None, None),
        P(),
        P(ALL, None),
        P(ALL),
        P(ALL, None),
    )
    return jax.shard_map(
        on_device, mesh=mesh, in_specs=in_specs, out_specs=P(ALL, None), check_vma=False
    )
```

time: 197 us -> 155 us (0.79)
  blocking collectives: 135 us -> 104 us
  Pallas kernels: 0 us -> 9.36 us
  local copies, waits for them, and re-layouts: 17.8 us -> 9.37 us
  matrix products: 26.9 us -> 18.5 us
  starting transfers between devices: 13.2 us -> 8.15 us
  waiting for transfers between devices: 0.01 us -> 3.08 us
  other arithmetic: 3.26 us -> 1.03 us
    all_gather x4 -> x2, blocking collectives: 70.3 us -> 46.2 us  [the longest x1 36.7 us: on_device(): lax.all_gather(jnp.stack(fetched), 'ctx')]
    reshape x4 -> x5, local copies, waits for them, and re-layouts: 17 us -> 1.15 us  [the longest x1 0.89 us: on_device(): owner.reshape(blocks, 1)]
    pallas_call x0 -> x3, Pallas kernels: none -> 9.36 us  [the longest x1 4.58 us: on_device(): pl.pallas_call(functools.partial(apply_kernel, blocks, capacity, latent_c...]
    dot_general x4 -> x2, matrix products: 18 us -> 8.84 us  [the longest x1 4.44 us: on_device(): jnp.dot(summaries, heads_up[0], preferred_element_type=jnp.float32)]
    unnamed x8 -> x27, local copies, waits for them, and re-layouts: 0.02 us -> 7.72 us
    all_to_all x1, blocking collectives: 64.3 us -> 58 us  [exchange(): lax.all_to_all(values.reshape(blocks, SUB, capacity * piece), ALL, split_...]
    all_to_all x2 -> x1, starting transfers between devices: 13.2 us -> 7.41 us  [exchange(): lax.all_to_all(values.reshape(blocks, SUB, capacity * piece), ALL, split_...]
    ppermute x0 -> x2, waiting for transfers between devices: none -> 3.08 us  [on_device(): fetched.append(lax.ppermute(packet, ALL, pairs))]
  transfers between devices with their start and end apart: 2 -> 3, of which waited for: 0 -> 1; matrix products, arithmetic and copies ran while one was open for 9% -> 13% of each run, Pallas kernels for 0% -> 0%
where the time goes in v1:
time: 155 us; the launch traced here: 154 us
  blocking collectives  104 us (67%)
  matrix products  18.5 us (12%)
  local copies, waits for them, and re-layouts  9.37 us (6%)
  Pallas kernels  9.36 us (6%)
  starting transfers between devices  8.15 us (5%)
  waiting for transfers between devices  3.08 us (2%)
    all_to_all x1, blocking collectives, exchange(): lax.all_to_all(values.reshape(blocks, SUB, capacity * piece), ALL, split_...  58 us
    all_gather x1, blocking collectives, on_device(): lax.all_gather(jnp.stack(fetched), 'ctx')  36.7 us
    all_gather x1, blocking collectives, on_device(): pieces = lax.all_gather(mine, 'ctx')  9.41 us
    unnamed x27, local copies, waits for them, and re-layouts  7.72 us
    all_to_all x1, starting transfers between devices, exchange(): lax.all_to_all(values.reshape(blocks, SUB, capacity * piece), ALL, split_...  7.41 us
    pallas_call x1, Pallas kernels, on_device(): pl.pallas_call(functools.partial(apply_kernel, blocks, capacity, latent_c...  4.58 us
    dot_general x1, matrix products, on_device(): jnp.dot(summaries, heads_up[0], preferred_element_type=jnp.float32)  4.44 us
    dot_general x1, matrix products, on_device(): jnp.dot(summaries, heads_down[0], preferred_element_type=jnp.float32)  4.4 us
  transfers between devices with their start and end apart: 3, of which 1 were waited for; matrix products, arithmetic and copies ran while one was open for 13% of the time, Pallas kernels for 0%

profile of v1, /device:TPU:0, one launch (start us, length us, event | category | flops | bytes accessed | tf_op | source)
XLA Modules:
  0.0 153.9 jit_solution(4479705960615828397)
XLA Ops:
  0.0 0.9 copy.50.owner_column
  0.9 0.8 copy.49.module_column
  1.7 1.5 copy-done.1
  3.2 0.7 copy-done.6
  3.9 0.7 copy-done.7
  4.6 1.8 %place_rows.1 = (bf16[256,4480]{1,0:T(8,128)(2,1)S(1)}, s32[224,1]{1,0:T(8,128)S(1)}, s32[1,192]{1,0:T(1,128)S(1)}) custom-call(s32[192,1]{1,0:T(8,128)S(1)} %copy.49.module_column, s32[1,192]{1,0:T(1,128)S(1)} %bitcast.86, s32[32,1]{1,0:T(8,128)S(1)} %copy.50.owner_column, s32[1,192]{1,0:T(1,128)S(1)} %bitcast.87, bf16[192,5120]{1,0:T(8,128)(2,1)S(1)} %copy-done.1), custom_call_target="tpu_custom_call" | custom-call | tf_op jit(solution)/shard_map/place_rows/pallas_call | solution.py:164
  6.4 1.3 copy-done.5
  7.7 7.4 %all-to-all-start = ((bf16[32,8,4480]{2,1,0:T(8,128)(2,1)}), bf16[32,8,4480]{2,1,0:T(8,128)(2,1)}, u32[]{:S(2)}, u32[]{:S(2)}) async-start(bf16[32,8,4480]{2,1,0:T(8,128)(2,1)} %bitcast.85), calls=%async_computation | async-start | bytes 4587520 | tf_op jit(solution)/shard_map/all_to_all | solution.py:160
  15.2 4.0 %fusion.15 = bf16[32,4,8,128]{3,2,1,0:T(8,128)(2,1)S(1)} fusion(bf16[5120,512]{1,0:T(8,128)(2,1)} %param.14, bf16[1,256,5120]{2,1,0:T(8,128)(2,1)S(1)} %copy-done), kind=kOutput, calls=%fused_computation.11 | convolution fusion | flops 1342308352 | bytes 8126464 | tf_op jit(solution)/shard_map/dot_general | solution.py:178
  19.2 4.1 %fusion.12 = bf16[32,4,8,128]{3,2,1,0:T(8,128)(2,1)S(1)} fusion(bf16[5120,512]{1,0:T(8,128)(2,1)} %param.15, bf16[1,256,5120]{2,1,0:T(8,128)(2,1)S(1)} %copy-done), kind=kOutput, calls=%fused_computation.10 | convolution fusion | flops 1342308352 | bytes 8126464 | tf_op jit(solution)/shard_map/dot_general | solution.py:179
  23.3 0.1 convert_reduce_fusion
  23.4 0.2 fusion.35
  23.6 0.2 fusion.25
  24.1 0.3 fusion.19
  24.4 9.4 %all-gather.2 = f32[4,67,128]{2,1,0:T(8,128)S(1)} all-gather(f32[1,67,128]{2,1,0:T(8,128)S(1)} %maximum_bitcast_fusion), channel_id=2, replica_groups=mesh['doc'=8,'ctx'=4] {'ctx'}, dimensions={0}, use_global_device_ids=true | all-gather | bytes 171520 | tf_op jit(solution)/shard_map/all_gather | solution.py:206
  34.1 0.1 fusion.24
  34.2 1.1 multiply_reduce_fusion
  35.5 0.7 collective-permute-start
  36.3 3.1 %collective-permute-done.1 = bf16[18,512]{1,0:T(8,128)(2,1)S(1)} collective-permute-done((bf16[18,512]{1,0:T(8,128)(2,1)S(1)}, bf16[18,512]{1,0:T(8,128)(2,1)S(1)}, u32[]{:S(2)}, u32[]{:S(2)}) %collective-permute-start.1) | collective-permute-done | bytes 18464 | tf_op jit(solution)/shard_map/ppermute | solution.py:241
  39.4 36.7 %all-gather.1 = bf16[8,18,512]{2,1,0:T(8,128)(2,1)S(1)} all-gather(bf16[2,18,512]{2,1,0:T(8,128)(2,1)S(1)} %pad_maximum_fusion), channel_id=3, replica_groups=mesh['doc'=8,'ctx'=4] {'ctx'}, dimensions={0}, use_global_device_ids=true | all-gather | bytes 184320 | tf_op jit(solution)/shard_map/all_gather | solution.py:242
  76.2 0.1 reshape.208
  76.3 0.1 select_reduce_fusion
  76.4 0.1 copy.55
  76.5 0.1 select_reduce_fusion.1
  76.6 0.1 copy.56
  76.8 4.4 %convolution_convert_fusion.up = bf16[128,5120]{1,0:T(8,128)(2,1)} fusion(bf16[128,512]{1,0:T(8,128)(2,1)S(1)} %bitcast.88, bf16[1,512,5120]{2,1,0:T(8,128)(2,1)} %param.19), kind=kOutput, calls=%fused_computation | convolution fusion | flops 671744000 | bytes 6684672 | tf_op jit(solution)/shard_map/dot_general | solution.py:263
  81.3 4.4 %convolution_convert_fusion.1.down = bf16[128,5120]{1,0:T(8,128)(2,1)} fusion(bf16[128,512]{1,0:T(8,128)(2,1)S(1)} %bitcast.89, bf16[1,512,5120]{2,1,0:T(8,128)(2,1)} %param.18), kind=kOutput, calls=%fused_computation.1 | convolution fusion | flops 671744000 | bytes 6684672 | tf_op jit(solution)/shard_map/dot_general | solution.py:260
  85.7 1.3 copy-done.3
  87.0 1.3 copy-done.4
  88.3 4.6 %apply_rows.1 = bf16[256,4480]{1,0:T(8,128)(2,1)S(1)} custom-call(bf16[256,4480]{1,0:T(8,128)(2,1)} %bitcast.4.arrived, s32[224,1]{1,0:T(8,128)S(1)} %convert_element_type.69.tags, s32[1,128]{1,0:T(1,128)S(1)} %fusion.34.column_doc, bf16[128,5120]{1,0:T(8,128)(2,1)S(1)} %copy-done.4, bf16[128,5120]{1,0:T(8,128)(2,1)S(1)} %copy-done.3), custom_call_target="tpu_custom_call" | custom-call | tf_op jit(solution)/shard_map/apply_rows/pallas_call | solution.py:266
  92.9 58.0 %all_to_all.10 = bf16[32,8,4480]{2,1,0:T(8,128)(2,1)S(1)} all-to-all(bf16[32,8,4480]{2,1,0:T(8,128)(2,1)S(1)} %bitcast.84), channel_id=1, replica_groups=mesh['doc'=8,'ctx'=4] {'doc','ctx'}, dimensions={0} | all-to-all | bytes 4587520 | tf_op jit(solution)/shard_map/all_to_all | solution.py:160
  150.9 3.0 %finish_rows.1 = bf16[192,5120]{1,0:T(8,128)(2,1)} custom-call(bf16[256,4480]{1,0:T(8,128)(2,1)S(1)} %bitcast.83, s32[1,192]{1,0:T(1,128)S(1)} %get-tuple-element.10.slots, bf16[192,5120]{1,0:T(8,128)(2,1)S(1)} %copy-done.2), custom_call_target="tpu_custom_call" | custom-call | tf_op jit(solution)/shard_map/finish_rows/pallas_call | solution.py:274
  (46 shorter events, 1.0 us)
Async XLA Ops:
  0.0 15.1 %copy-start = (bf16[1,256,5120]{2,1,0:T(8,128)(2,1)S(1)}, bf16[1,256,5120]{2,1,0:T(8,128)(2,1)}, u32[]{:S(2)}) copy-start(bf16[1,256,5120]{2,1,0:T(8,128)(2,1)} %param.12) | copy-start | bytes 7864324
  1.7 1.6 %copy-start.1 = (bf16[192,5120]{1,0:T(8,128)(2,1)S(1)}, bf16[192,5120]{1,0:T(8,128)(2,1)}, u32[]{:S(2)}) copy-start(bf16[192,5120]{1,0:T(8,128)(2,1)} %requests.3) | copy-start | bytes 5898244
  3.2 0.7 copy-start.6
  3.9 0.7 copy-start.7
  6.4 1.4 copy-start.5
  7.7 78.0 %all-to-all-start = ((bf16[32,8,4480]{2,1,0:T(8,128)(2,1)}), bf16[32,8,4480]{2,1,0:T(8,128)(2,1)}, u32[]{:S(2)}, u32[]{:S(2)}) async-start(bf16[32,8,4480]{2,1,0:T(8,128)(2,1)} %bitcast.85), calls=%async_computation | async-start | bytes 4587520 | tf_op jit(solution)/shard_map/all_to_all | solution.py:160
  19.2 4.2 %copy-start.9 = (f32[16,512]{1,0:T(8,128)S(1)}, f32[16,512]{1,0:T(8,128)}, u32[]{:S(2)}) copy-start(f32[16,512]{1,0:T(8,128)} %param.13) | copy-start | bytes 98308
  19.2 15.0 %copy-start.8 = (bf16[512,512]{1,0:T(8,128)(2,1)S(1)}, bf16[512,512]{1,0:T(8,128)(2,1)}, u32[]{:S(2)}) copy-start(bf16[512,512]{1,0:T(8,128)(2,1)} %param.16) | copy-start | bytes 1572868
  19.2 16.1 %copy-start.10 = (f32[512]{0:T(512)S(1)}, f32[512]{0:T(512)}, u32[]{:S(2)}) copy-start(f32[512]{0:T(512)} %param.17) | copy-start | bytes 6148
  35.4 3.9 %collective-permute-start.1 = (bf16[18,512]{1,0:T(8,128)(2,1)S(1)}, bf16[18,512]{1,0:T(8,128)(2,1)S(1)}, u32[]{:S(2)}, u32[]{:S(2)}) collective-permute-start(bf16[18,512]{1,0:T(8,128)(2,1)S(1)} %pad_maximum_fusion.1), channel_id=1, source_target_pairs={{0,4},{1,13},{2,22},{3,31},{4,0},{5,9},{6,18},{7,27},{8,12},{9,5},... | collective-permute-start | bytes 55304 | tf_op jit(solution)/shard_map/ppermute | solution.py:241
  35.5 3.9 %collective-permute-start = (bf16[18,512]{1,0:T(8,128)(2,1)S(1)}, bf16[18,512]{1,0:T(8,128)(2,1)S(1)}, u32[]{:S(2)}, u32[]{:S(2)}) collective-permute-start(bf16[18,512]{1,0:T(8,128)(2,1)S(1)} %pad_maximum_fusion.1), channel_id=1, source_target_pairs={{0,0},{1,9},{2,18},{3,27},{4,4},{5,13},{6,22},{7,31},{8,8},{9,1},{... | collective-permute-start | bytes 55304 | tf_op jit(solution)/shard_map/ppermute | solution.py:241
  85.7 1.3 copy-start.3
  87.0 1.3 copy-start.4
  92.9 58.0 %copy-start.2 = (bf16[192,5120]{1,0:T(8,128)(2,1)S(1)}, bf16[192,5120]{1,0:T(8,128)(2,1)}, u32[]{:S(2)}) copy-start(bf16[192,5120]{1,0:T(8,128)(2,1)} %requests.3) | copy-start | bytes 5898244

commit v2 on v1

v2 whole, which is shorter than its diff:
```python
import functools
import math

import jax
import jax.numpy as jnp
from jax import lax
from jax.experimental import pallas as pl
from jax.experimental.pallas import tpu as pltpu
from jax.sharding import PartitionSpec as P

HEADS = 4
SUB = 8
LANES = 128
VMEM_LIMIT = 60 * 1024 * 1024
ALL = ("doc", "ctx")


def call(kernel, name, **options):
    return pl.pallas_call(
        kernel,
        name=name,
        compiler_params=pltpu.CompilerParams(vmem_limit_bytes=VMEM_LIMIT),
        **options,
    )


def scatter_pieces(stage, piece_index, values, blocks, capacity, piece):
    for slot in range(capacity):
        for lane in range(piece // LANES):
            stage[
                slot * (piece // LANES) + lane, pl.ds(piece_index, blocks, stride=SUB), :
            ] = values[slot * blocks : (slot + 1) * blocks, lane * LANES : (lane + 1) * LANES]


def gather_pieces(stage, piece_index, blocks, capacity, piece):
    return jnp.concatenate(
        [
            jnp.concatenate(
                [
                    stage[slot * (piece // LANES) + lane, pl.ds(piece_index, blocks, stride=SUB), :]
                    for lane in range(piece // LANES)
                ],
                axis=1,
            ).astype(jnp.bfloat16)
            for slot in range(capacity)
        ],
        axis=0,
    )


def fill_stage(stage, sources):
    start = 0
    for source in sources:
        for lane in range(source.shape[1] // LANES):
            stage[start] = source[:, lane * LANES : (lane + 1) * LANES].astype(jnp.float32)
            start += 1


def drain_stage(stage, targets):
    start = 0
    for target in targets:
        for lane in range(target.shape[1] // LANES):
            target[:, lane * LANES : (lane + 1) * LANES] = stage[start].astype(target.dtype)
            start += 1


def as_column(row):
    n = row.shape[1]
    on_diagonal = lax.broadcasted_iota(jnp.int32, (n, n), 0) == lax.broadcasted_iota(
        jnp.int32, (n, n), 1
    )
    return jnp.sum(jnp.where(on_diagonal, row, jnp.zeros_like(row)), axis=1, keepdims=True)


def as_row(column):
    n = column.shape[0]
    on_diagonal = lax.broadcasted_iota(jnp.int32, (n, n), 0) == lax.broadcasted_iota(
        jnp.int32, (n, n), 1
    )
    return jnp.sum(jnp.where(on_diagonal, column, jnp.zeros_like(column)), axis=0, keepdims=True)


def place_kernel(
    blocks, capacity, owner_row, module_row, doc_row, requests, first_sent, second_sent, tags, slots, stage
):
    rows, width = requests.shape
    piece = width // SUB
    modules = module_row[...]
    owners = as_column(owner_row[...])
    named = lax.broadcasted_iota(jnp.int32, (blocks, rows), 0) == modules
    target = jnp.sum(jnp.where(named, owners, 0), axis=0, keepdims=True)
    first = lax.broadcasted_iota(jnp.int32, (rows, rows), 0)
    second = lax.broadcasted_iota(jnp.int32, (rows, rows), 1)
    ahead = (as_column(modules) == modules) & (first < second)
    rank = jnp.sum(ahead.astype(jnp.int32), axis=0, keepdims=True)
    slot_row = rank * blocks + target
    slots[...] = slot_row
    slot_column = as_column(slot_row)
    documents = as_column(doc_row[...] + 1)
    for part in range(tags.shape[0]):
        lanes = lax.broadcasted_iota(jnp.int32, (rows, LANES), 1) + part * LANES
        tags[part : part + 1, :] = jnp.sum(
            jnp.where(lanes == slot_column, documents, 0), axis=0, keepdims=True
        ).astype(jnp.float32)
    slot_ids = lax.broadcasted_iota(jnp.int32, (capacity * blocks, rows), 0)
    placer = (slot_ids == slot_row).astype(jnp.float32).astype(jnp.bfloat16)
    for index in range(SUB):
        moved = jnp.dot(
            placer,
            requests[:, index * piece : (index + 1) * piece],
            preferred_element_type=jnp.float32,
        )
        scatter_pieces(stage, index, moved, blocks, capacity, piece)
    drain_stage(stage, (first_sent, second_sent))


def attend_kernel(
    chunks, tokens, w_keys, w_values, latents, tags, partial, tokens_in, keys_in, values_in, done
):
    depth = w_keys.shape[0] // chunks
    copies = []
    for chunk in range(chunks):
        part = pl.ds(chunk * depth, depth)
        copies.append(
            [
                pltpu.make_async_copy(
                    tokens.at[0, :, part], tokens_in.at[chunk], done.at[chunk, 0]
                ),
                pltpu.make_async_copy(w_keys.at[part, :], keys_in.at[chunk], done.at[chunk, 1]),
                pltpu.make_async_copy(w_values.at[part, :], values_in.at[chunk], done.at[chunk, 2]),
            ]
        )
    for group in copies:
        for copy in group:
            copy.start()
    keys = values = 0.0
    for chunk in range(chunks):
        for copy in copies[chunk]:
            copy.wait()
        keys = keys + jnp.dot(
            tokens_in[chunk], keys_in[chunk], preferred_element_type=jnp.float32
        )
        values = values + jnp.dot(
            tokens_in[chunk], values_in[chunk], preferred_element_type=jnp.float32
        )
    latent_count, width = latents.shape
    head_dim = width // HEADS
    queries = latents[...].astype(jnp.bfloat16)
    key_rows = keys.astype(jnp.bfloat16)
    value_rows = values.astype(jnp.bfloat16).astype(jnp.float32)
    peaks, sums = [], []
    for head in range(HEADS):
        lanes = slice(head * head_dim, (head + 1) * head_dim)
        scores = lax.dot_general(
            queries[:, lanes],
            key_rows[:, lanes],
            (((1,), (1,)), ((), ())),
            preferred_element_type=jnp.float32,
        ) / math.sqrt(head_dim)
        peak = jnp.max(scores, axis=1, keepdims=True)
        expo = jnp.exp(scores - peak)
        peaks.append(peak)
        sums.append(jnp.sum(expo, axis=1, keepdims=True))
        partial[head * latent_count : (head + 1) * latent_count, :] = jnp.dot(
            expo,
            value_rows[:, lanes],
            precision=lax.Precision.HIGHEST,
            preferred_element_type=jnp.float32,
        )
    entries = HEADS * latent_count
    partial[entries:, :] = jnp.zeros_like(partial[entries:, :])
    partial[entries : entries + 1, :entries] = as_row(jnp.concatenate(peaks, axis=0))
    partial[entries + 1 : entries + 2, :entries] = as_row(jnp.concatenate(sums, axis=0))
    partial[entries + 2 : entries + 2 + tags.shape[0], :] = tags[...]


def summary_kernel(tag_parts, pieces, latents, w_out, gain, packet):
    members = pieces.shape[0]
    latent_count, width = latents.shape
    entries = HEADS * latent_count
    peaks = [as_column(pieces[c, entries : entries + 1, :entries]) for c in range(members)]
    summit = functools.reduce(jnp.maximum, peaks)
    total, weighted = 0.0, 0.0
    for c in range(members):
        ratio = jnp.exp(peaks[c] - summit)
        total = total + as_column(pieces[c, entries + 1 : entries + 2, :entries]) * ratio
        weighted = weighted + pieces[c, :entries, :] * ratio
    attended = weighted / total
    attended = jnp.concatenate(
        [attended[h * latent_count : (h + 1) * latent_count] for h in range(HEADS)], axis=1
    ).astype(jnp.bfloat16)
    mixed = latents[...] + jnp.dot(attended, w_out[...], preferred_element_type=jnp.float32)
    summary = (
        mixed
        * lax.rsqrt(jnp.mean(mixed * mixed, axis=1, keepdims=True) + 1e-06)
        * gain[...]
    )
    packet[:latent_count, :] = summary.astype(jnp.bfloat16)
    tag_rows = [
        jnp.concatenate(
            [pieces[c, entries + 2 + part : entries + 3 + part, :] for part in range(tag_parts)],
            axis=1,
        )
        for c in range(members)
    ]
    block = jnp.concatenate(tag_rows, axis=0)
    block = jnp.pad(
        block,
        ((0, packet.shape[0] - latent_count - members), (0, width - tag_parts * LANES)),
    )
    packet[latent_count:, :] = block.astype(jnp.bfloat16)


def factor_kernel(
    blocks,
    capacity,
    early,
    latent_count,
    chunks,
    me,
    everyone,
    heads_down,
    heads_up,
    down,
    up,
    tags_first,
    tags_second,
    heads_in,
    factors_out,
    arrived,
    left,
):
    depth = down.shape[1] // chunks
    jobs = []
    for chunk in range(chunks):
        part = pl.ds(chunk * depth, depth)
        for side, (heads, factor) in enumerate(((heads_down, down), (heads_up, up))):
            jobs.append(
                (
                    chunk,
                    side,
                    pltpu.make_async_copy(
                        heads.at[0, :, part], heads_in.at[chunk, side], arrived.at[chunk, side]
                    ),
                    pltpu.make_async_copy(
                        factors_out.at[chunk, side], factor.at[:, part], left.at[chunk, side]
                    ),
                )
            )
    for job in jobs:
        job[2].start()
    documents = everyone.shape[0]
    members = blocks // documents
    summaries = jnp.concatenate([everyone[x, :latent_count, :] for x in range(documents)], axis=0)
    device = me[0, 0]
    my_doc = device // members
    by_entry = jnp.concatenate(
        [everyone[x, latent_count:, :].astype(jnp.float32)[:members] for x in range(documents)],
        axis=0,
    ).astype(jnp.bfloat16)
    source = lax.broadcasted_iota(jnp.int32, (blocks, blocks), 0)
    entry = lax.broadcasted_iota(jnp.int32, (blocks, blocks), 1)
    sorter = source == ((entry // members) ^ my_doc) * members + entry % members
    sorter = sorter.astype(jnp.float32).astype(jnp.bfloat16)
    arranged = jnp.dot(sorter, by_entry, preferred_element_type=jnp.float32)
    lanes = lax.broadcasted_iota(jnp.int32, arranged.shape, 1)
    for slot in range(capacity):
        column = jnp.sum(
            jnp.where(lanes == slot * blocks + device, arranged, 0.0), axis=1, keepdims=True
        ).astype(jnp.int32)
        target, position = (tags_first, slot) if slot < early else (tags_second, slot - early)
        target[position * blocks : (position + 1) * blocks, :] = column
    for chunk, side, arriving, leaving in jobs:
        arriving.wait()
        factors_out[chunk, side] = jnp.dot(
            summaries, heads_in[chunk, side], preferred_element_type=jnp.float32
        ).astype(jnp.bfloat16)
        leaving.start()
    for job in jobs:
        job[3].wait()


def apply_kernel(blocks, capacity, latent_count, members, me, tags, down, up, arrived, *refs):
    *ready, update, stage = refs
    width = down.shape[1]
    piece = width // SUB
    fill_stage(stage, (arrived,))
    coeff = None
    for index in range(SUB):
        part = lax.dot_general(
            gather_pieces(stage, index, blocks, capacity, piece),
            down[:, index * piece : (index + 1) * piece],
            (((1,), (1,)), ((), ())),
            preferred_element_type=jnp.float32,
        )
        coeff = part if coeff is None else coeff + part
    column_doc = (
        lax.broadcasted_iota(jnp.int32, coeff.shape, 1) // latent_count
    ) ^ (me[0, 0] // members)
    matched = tags[...] - 1 == column_doc
    coeff = jnp.where(matched, coeff / math.sqrt(width), 0.0).astype(jnp.bfloat16)
    for index in range(SUB):
        moved = jnp.dot(
            coeff, up[:, index * piece : (index + 1) * piece], preferred_element_type=jnp.float32
        ) * (1.0 / math.sqrt(latent_count))
        scatter_pieces(stage, index, moved, blocks, capacity, piece)
    start = 0
    for part in ready:
        start = part.shape[1]
        update[:, :start] = part[...]
    drain_stage(stage, (update.at[:, start:],))


def finish_kernel(blocks, capacity, returned, slots, requests, adapted, stage):
    rows, width = requests.shape
    piece = width // SUB
    fill_stage(stage, (returned,))
    placed = lax.broadcasted_iota(jnp.int32, (capacity * blocks, rows), 0) == slots[...]
    placer = placed.astype(jnp.float32).astype(jnp.bfloat16)
    for index in range(SUB):
        gathered = lax.dot_general(
            placer,
            gather_pieces(stage, index, blocks, capacity, piece),
            (((0,), (0,)), ((), ())),
            preferred_element_type=jnp.float32,
        )
        columns = slice(index * piece, (index + 1) * piece)
        adapted[:, columns] = (requests[:, columns].astype(jnp.float32) + gathered).astype(
            adapted.dtype
        )


def on_device(
    tokens,
    latents,
    w_keys,
    w_values,
    w_out,
    latent_gain,
    heads_down,
    heads_up,
    owner,
    requests,
    req_doc,
    req_module,
):
    doc_count = lax.axis_size("doc")
    ctx_count = lax.axis_size("ctx")
    blocks = doc_count * ctx_count
    rows, width = requests.shape
    capacity = max(2, rows // blocks + 1)
    piece = width // SUB
    latent_count, latent_width = latents.shape
    head_dim = latent_width // HEADS
    my_doc = lax.axis_index("doc")
    my_ctx = lax.axis_index("ctx")
    early = max(1, (capacity - 1) // 2)
    late = capacity - early
    tag_parts = -(-(capacity * blocks) // LANES)
    me = (my_doc * ctx_count + my_ctx).astype(jnp.int32).reshape(1, 1)
    in_smem = pl.BlockSpec(memory_space=pltpu.SMEM)
    in_vmem = pl.BlockSpec(memory_space=pltpu.VMEM)
    in_hbm = pl.BlockSpec(memory_space=pl.ANY)

    def after(values, *others):
        return lax.optimization_barrier((values, *others))[0]

    def block_type(slot_count):
        return jax.ShapeDtypeStruct((blocks * SUB, slot_count * piece), jnp.bfloat16)

    def stage_type(slot_count):
        return pltpu.VMEM((slot_count * piece // LANES, blocks * SUB, LANES), jnp.float32)

    def exchange(values):
        return lax.all_to_all(
            values.reshape(blocks, SUB, -1), ALL, split_axis=0, concat_axis=0, tiled=True
        ).reshape(values.shape)

    first_sent, second_sent, tags, slots = call(
        functools.partial(place_kernel, blocks, capacity),
        "place_rows",
        out_shape=(
            block_type(early),
            block_type(late),
            jax.ShapeDtypeStruct((tag_parts, LANES), jnp.float32),
            jax.ShapeDtypeStruct((1, rows), jnp.int32),
        ),
        scratch_shapes=[stage_type(capacity)],
    )(
        owner.reshape(1, blocks),
        req_module.reshape(1, rows),
        req_doc.reshape(1, rows),
        requests,
    )
    first_arrived = exchange(first_sent)

    token_count = tokens.shape[1]
    entries = HEADS * latent_count
    partial_rows = -(-(entries + 2 + tag_parts) // SUB) * SUB
    chunks = width // (SUB * LANES)
    depth = width // chunks
    partial = call(
        functools.partial(attend_kernel, chunks),
        "attend",
        in_specs=[in_hbm] * 3 + [in_vmem] * 2,
        out_shape=jax.ShapeDtypeStruct((partial_rows, head_dim), jnp.float32),
        scratch_shapes=[
            pltpu.VMEM((chunks, token_count, depth), jnp.bfloat16),
            pltpu.VMEM((chunks, depth, latent_width), jnp.bfloat16),
            pltpu.VMEM((chunks, depth, latent_width), jnp.bfloat16),
            pltpu.SemaphoreType.DMA((chunks, 3)),
        ],
    )(tokens, w_keys, w_values, latents, tags)
    packet_rows = latent_count + 16
    packet = call(
        functools.partial(summary_kernel, tag_parts),
        "summarize",
        out_shape=jax.ShapeDtypeStruct((packet_rows, latent_width), jnp.bfloat16),
    )(lax.all_gather(partial, "ctx"), latents, w_out, latent_gain.reshape(1, latent_width))

    share = doc_count // ctx_count
    fetched = []
    for turn in range(share):
        pairs = [
            (doc * ctx_count + ctx, (doc ^ (ctx * share + turn)) * ctx_count + ctx)
            for doc in range(doc_count)
            for ctx in range(ctx_count)
        ]
        fetched.append(lax.ppermute(packet, ALL, pairs))
    second_arrived = exchange(after(second_sent, *fetched))
    everyone = lax.all_gather(jnp.stack(fetched), "ctx").reshape(
        doc_count, packet_rows, latent_width
    )

    def tag_type(slot_count):
        return jax.ShapeDtypeStruct((slot_count * blocks, 1), jnp.int32)

    factor_type = jax.ShapeDtypeStruct((doc_count * latent_count, width), jnp.bfloat16)
    down_factor, up_factor, first_tags, second_tags = call(
        functools.partial(factor_kernel, blocks, capacity, early, latent_count, chunks),
        "factors",
        in_specs=[in_smem, in_vmem, in_hbm, in_hbm],
        out_specs=(in_hbm, in_hbm, in_vmem, in_vmem),
        out_shape=(factor_type, factor_type, tag_type(early), tag_type(late)),
        scratch_shapes=[
            pltpu.VMEM((chunks, 2, latent_width, depth), jnp.bfloat16),
            pltpu.VMEM((chunks, 2, doc_count * latent_count, depth), jnp.bfloat16),
            pltpu.SemaphoreType.DMA((chunks, 2)),
            pltpu.SemaphoreType.DMA((chunks, 2)),
        ],
    )(me, everyone, heads_down, heads_up)

    def apply(tag_column, slot_count, arrived, *ready):
        total = slot_count + sum(part.shape[1] for part in ready) // piece
        return call(
            functools.partial(apply_kernel, blocks, slot_count, latent_count, ctx_count),
            "apply_rows",
            in_specs=[in_smem] + [in_vmem] * (4 + len(ready)),
            out_shape=block_type(total),
            scratch_shapes=[stage_type(slot_count)],
        )(me, tag_column, down_factor, up_factor, arrived, *ready)

    first_update = apply(first_tags, early, first_arrived)
    update = apply(second_tags, late, after(second_arrived, first_update), first_update)
    returned = exchange(update)
    return call(
        functools.partial(finish_kernel, blocks, capacity),
        "finish_rows",
        out_shape=jax.ShapeDtypeStruct((rows, width), jnp.bfloat16),
        scratch_shapes=[stage_type(capacity)],
    )(returned, slots, requests)


def solution(mesh):
    in_specs = (
        P("doc", "ctx", None),
        P(),
        P(),
        P(),
        P(),
        P(),
        P(ALL, None, None),
        P(ALL, None, None),
        P(),
        P(ALL, None),
        P(ALL),
        P(ALL, None),
    )
    return jax.shard_map(
        on_device, mesh=mesh, in_specs=in_specs, out_specs=P(ALL, None), check_vma=False
    )
```

time: 155 us -> 146 us (0.942)
  Pallas kernels: 9.36 us -> 37.6 us
  blocking collectives: 104 us -> 79.7 us
  matrix products: 18.5 us -> 0 us
  starting transfers between devices: 8.15 us -> 16.6 us
  local copies, waits for them, and re-layouts: 9.37 us -> 1.06 us
  waiting for transfers between devices: 3.08 us -> 10.4 us
    pallas_call x3 -> x7, Pallas kernels: 9.36 us -> 37.6 us  [the longest x2 10 us: apply(): call(functools.partial(apply_kernel, blocks, slot_count, latent_count, ct...]
    all_gather x1, blocking collectives: 36.7 us -> 13.8 us  [on_device(): lax.all_gather(jnp.stack(fetched), 'ctx')]
    dot_general x7 -> x0, matrix products: 18.5 us -> none  [the longest x1 4.44 us: on_device(): jnp.dot(summaries, heads_up[0], preferred_element_type=jnp.float32)]
    all_to_all x1 -> x2, waiting for transfers between devices: 0.01 us -> 8.61 us  [exchange(): lax.all_to_all(values.reshape(blocks, SUB, -1), ALL, split_axis=0, concat...]
    unnamed x27 -> x4, local copies, waits for them, and re-layouts: 7.72 us -> 1.06 us
    all_to_all x1 -> x2, starting transfers between devices: 7.41 us -> 13.7 us  [exchange(): lax.all_to_all(values.reshape(blocks, SUB, -1), ALL, split_axis=0, concat...]
    ppermute x2, starting transfers between devices: 0.73 us -> 2.83 us  [on_device(): fetched.append(lax.ppermute(packet, ALL, pairs))]
    all_gather x1, blocking collectives: 9.41 us -> 7.79 us  [on_device(): lax.all_gather(partial, 'ctx')]
  transfers between devices with their start and end apart: 3 -> 4, of which waited for: 1 -> 3; matrix products, arithmetic and copies ran while one was open for 13% -> 0% of each run, Pallas kernels for 0% -> 15%
where the time goes in v2:
time: 146 us; the launch traced here: 145 us
  blocking collectives  79.7 us (55%)
  Pallas kernels  37.6 us (26%)
  starting transfers between devices  16.6 us (11%)
  waiting for transfers between devices  10.4 us (7%)
    all_to_all x1, blocking collectives, exchange(): lax.all_to_all(values.reshape(blocks, SUB, -1), ALL, split_axis=0, concat...  58.1 us
    all_gather x1, blocking collectives, on_device(): lax.all_gather(jnp.stack(fetched), 'ctx')  13.8 us
    all_to_all x2, starting transfers between devices, exchange(): lax.all_to_all(values.reshape(blocks, SUB, -1), ALL, split_axis=0, concat...  13.7 us
    pallas_call x2, Pallas kernels, apply(): call(functools.partial(apply_kernel, blocks, slot_count, latent_count, ct...  10 us
    all_to_all x2, waiting for transfers between devices, exchange(): lax.all_to_all(values.reshape(blocks, SUB, -1), ALL, split_axis=0, concat...  8.61 us
    pallas_call x1, Pallas kernels, on_device(): call(functools.partial(attend_kernel, chunks), 'attend', in_specs=[in_hbm...  8.16 us
    all_gather x1, blocking collectives, on_device(): lax.all_gather(partial, 'ctx')  7.79 us
    pallas_call x1, Pallas kernels, on_device(): call(functools.partial(factor_kernel, blocks, capacity, early, latent_cou...  7.41 us
  transfers between devices with their start and end apart: 4, of which 3 were waited for; matrix products, arithmetic and copies ran while one was open for 0% of the time, Pallas kernels for 15%

profile of v2, /device:TPU:0, one launch (start us, length us, event | category | flops | bytes accessed | tf_op | source)
XLA Modules:
  0.0 145.4 jit_solution(8857708947659943552)
XLA Ops:
  0.0 4.7 %place_rows.1 = (bf16[256,1920]{1,0:T(8,128)(2,1)}, bf16[256,2560]{1,0:T(8,128)(2,1)}, f32[2,128]{1,0:T(2,128)}, s32[1,192]{1,0:T(1,128)}) custom-call(s32[1,32]{1,0:T(1,128)} %bitcast.26, s32[1,192]{1,0:T(1,128)} %bitcast.24, s32[1,192]{1,0:T(1,128)} %bitcast.25, bf16[192,5120]{1,0:T(8,128)(2,1)} %requests.3), custom_call_target="tpu_custom_call" | custom-call | tf_op jit(solution)/shard_map/place_rows/pallas_call | solution.py:379
  4.7 7.3 %all-to-all-start.1 = ((bf16[32,8,1920]{2,1,0:T(8,128)(2,1)}), bf16[32,8,1920]{2,1,0:T(8,128)(2,1)S(1)}, u32[]{:S(2)}, u32[]{:S(2)}) async-start(bf16[32,8,1920]{2,1,0:T(8,128)(2,1)} %bitcast.19), calls=%async_computation.1 | async-start | bytes 1966080 | tf_op jit(solution)/shard_map/all_to_all | solution.py:375
  12.0 8.2 %attend.1 = f32[72,128]{1,0:T(8,128)} custom-call(bf16[1,256,5120]{2,1,0:T(8,128)(2,1)} %tokens.1, bf16[5120,512]{1,0:T(8,128)(2,1)} %w_keys.1, bf16[5120,512]{1,0:T(8,128)(2,1)} %w_values.1, f32[16,512]{1,0:T(8,128)} %latents.3, f32[2,128]{1,0:T(2,128)} %get-tuple-element.15.tags), custom_call_target="tpu_custom_call" | custom-call | tf_op jit(solution)/shard_map/attend/pallas_call | solution.py:402
  20.1 7.8 %all-gather = f32[288,128]{1,0:T(8,128)} all-gather(f32[72,128]{1,0:T(8,128)} %attend.1), channel_id=2, replica_groups=mesh['doc'=8,'ctx'=4] {'ctx'}, dimensions={0}, use_global_device_ids=true | all-gather | bytes 184320 | tf_op jit(solution)/shard_map/all_gather | solution.py:419
  27.9 2.1 %summarize.1 = bf16[32,512]{1,0:T(8,128)(2,1)} custom-call(f32[4,72,128]{2,1,0:T(8,128)} %bitcast.20, f32[16,512]{1,0:T(8,128)} %latents.3, bf16[512,512]{1,0:T(8,128)(2,1)} %w_out.1, f32[1,512]{1,0:T(1,128)} %bitcast.23), custom_call_target="tpu_custom_call" | custom-call | tf_op jit(solution)/shard_map/summarize/pallas_call | solution.py:415
  30.0 1.4 collective-permute-start.1
  31.5 1.4 collective-permute-start
  32.9 1.8 %collective-permute-done.1 = bf16[32,512]{1,0:T(8,128)(2,1)S(1)} collective-permute-done((bf16[32,512]{1,0:T(8,128)(2,1)}, bf16[32,512]{1,0:T(8,128)(2,1)S(1)}, u32[]{:S(2)}, u32[]{:S(2)}) %collective-permute-start.1) | collective-permute-done | bytes 32800 | tf_op jit(solution)/shard_map/ppermute | solution.py:429
  34.7 0.0 collective-permute-done
  34.7 2.1 %all-to-all-done.1 = bf16[32,8,1920]{2,1,0:T(8,128)(2,1)S(1)} async-done(((bf16[32,8,1920]{2,1,0:T(8,128)(2,1)}), bf16[32,8,1920]{2,1,0:T(8,128)(2,1)S(1)}, u32[]{:S(2)}, u32[]{:S(2)}) %all-to-all-start.1) | async-done | bytes 983072 | tf_op jit(solution)/shard_map/all_to_all | solution.py:375
  36.8 0.0 copy-start.1
  36.8 6.4 %all-to-all-start = ((bf16[32,8,2560]{2,1,0:T(8,128)(2,1)}), bf16[32,8,2560]{2,1,0:T(8,128)(2,1)S(1)}, u32[]{:S(2)}, u32[]{:S(2)}) async-start(bf16[32,8,2560]{2,1,0:T(8,128)(2,1)} %bitcast.18), calls=%async_computation | async-start | bytes 2621440 | tf_op jit(solution)/shard_map/all_to_all | solution.py:375
  43.3 13.8 %all-gather.1.everyone = bf16[8,32,512]{2,1,0:T(8,128)(2,1)} all-gather(bf16[2,32,512]{2,1,0:T(8,128)(2,1)S(1)} %pad_maximum_fusion), channel_id=3, replica_groups=mesh['doc'=8,'ctx'=4] {'ctx'}, dimensions={0}, use_global_device_ids=true | all-gather | bytes 327680 | tf_op jit(solution)/shard_map/all_gather | solution.py:431
  57.0 7.4 %factors.1 = (bf16[128,5120]{1,0:T(8,128)(2,1)}, bf16[128,5120]{1,0:T(8,128)(2,1)}, s32[96,1]{1,0:T(8,128)}, s32[128,1]{1,0:T(8,128)}) custom-call(s32[1,1]{1,0:T(1,128)} %bitcast.me, bf16[8,32,512]{2,1,0:T(8,128)(2,1)} %all-gather.1.everyone, bf16[1,512,5120]{2,1,0:T(8,128)(2,1)} %heads_down.1, bf16[1,512,5120]{2,1,0:T(8,128)(2,1)} %heads_up.1), custom_call_target="tpu_custom_call" | custom-call | tf_op jit(solution)/shard_map/factors/pallas_call | solution.py:439
  64.4 0.0 copy-done.1
  64.4 4.4 %apply_rows.2.refs_0_ = bf16[256,1920]{1,0:T(8,128)(2,1)} custom-call(s32[1,1]{1,0:T(1,128)} %bitcast.me, s32[96,1]{1,0:T(8,128)} %get-tuple-element.21.tags, bf16[128,5120]{1,0:T(8,128)(2,1)} %get-tuple-element.17.down, bf16[128,5120]{1,0:T(8,128)(2,1)} %get-tuple-element.18.up, bf16[256,1920]{1,0:T(8,128)(2,1)} %bitcast.17), custom_call_target="tpu_custom_call" | custom-call | tf_op jit(solution)/shard_map/apply_rows/pallas_call | solution.py:455
  68.9 6.5 %all-to-all-done = bf16[32,8,2560]{2,1,0:T(8,128)(2,1)S(1)} async-done(((bf16[32,8,2560]{2,1,0:T(8,128)(2,1)}), bf16[32,8,2560]{2,1,0:T(8,128)(2,1)S(1)}, u32[]{:S(2)}, u32[]{:S(2)}) %all-to-all-start) | async-done | bytes 1310752 | tf_op jit(solution)/shard_map/all_to_all | solution.py:375
  75.4 0.0 copy-start
  75.4 1.1 copy-done
  76.4 5.6 %apply_rows.3 = bf16[256,4480]{1,0:T(8,128)(2,1)} custom-call(s32[1,1]{1,0:T(1,128)} %bitcast.me, s32[128,1]{1,0:T(8,128)} %get-tuple-element.16.tags, bf16[128,5120]{1,0:T(8,128)(2,1)} %get-tuple-element.17.down, bf16[128,5120]{1,0:T(8,128)(2,1)} %get-tuple-element.18.up, bf16[256,2560]{1,0:T(8,128)(2,1)} %bitcast.16, bf16[256,1920]{1,0:T(8,128)(2,1)} %apply_rows.2.refs_0_), custom_call_target="tpu_custom_call" | custom-call | tf_op jit(solution)/shard_map/apply_rows/pallas_call | solution.py:455
  82.0 58.1 %all_to_all.15 = bf16[32,8,4480]{2,1,0:T(8,128)(2,1)} all-to-all(bf16[32,8,4480]{2,1,0:T(8,128)(2,1)} %bitcast.14), channel_id=1, replica_groups=mesh['doc'=8,'ctx'=4] {'doc','ctx'}, dimensions={0} | all-to-all | bytes 4587520 | tf_op jit(solution)/shard_map/all_to_all | solution.py:375
  140.1 5.3 %finish_rows.1 = bf16[192,5120]{1,0:T(8,128)(2,1)} custom-call(bf16[256,4480]{1,0:T(8,128)(2,1)} %bitcast.15, s32[1,192]{1,0:T(1,128)} %get-tuple-element.24.slots, bf16[192,5120]{1,0:T(8,128)(2,1)} %requests.3), custom_call_target="tpu_custom_call" | custom-call | tf_op jit(solution)/shard_map/finish_rows/pallas_call | solution.py:466
  (1 shorter events, 0.0 us)
Async XLA Ops:
  4.7 32.1 %all-to-all-start.1 = ((bf16[32,8,1920]{2,1,0:T(8,128)(2,1)}), bf16[32,8,1920]{2,1,0:T(8,128)(2,1)S(1)}, u32[]{:S(2)}, u32[]{:S(2)}) async-start(bf16[32,8,1920]{2,1,0:T(8,128)(2,1)} %bitcast.19), calls=%async_computation.1 | async-start | bytes 1966080 | tf_op jit(solution)/shard_map/all_to_all | solution.py:375
  30.0 4.6 %collective-permute-start.1 = (bf16[32,512]{1,0:T(8,128)(2,1)}, bf16[32,512]{1,0:T(8,128)(2,1)S(1)}, u32[]{:S(2)}, u32[]{:S(2)}) collective-permute-start(bf16[32,512]{1,0:T(8,128)(2,1)} %summarize.1), channel_id=1, source_target_pairs={{0,4},{1,13},{2,22},{3,31},{4,0},{5,9},{6,18},{7,27},{8,12},{9,5},... | collective-permute-start | bytes 98312 | tf_op jit(solution)/shard_map/ppermute | solution.py:429
  31.5 3.2 %collective-permute-start = (bf16[32,512]{1,0:T(8,128)(2,1)}, bf16[32,512]{1,0:T(8,128)(2,1)S(1)}, u32[]{:S(2)}, u32[]{:S(2)}) collective-permute-start(bf16[32,512]{1,0:T(8,128)(2,1)} %summarize.1), channel_id=1, source_target_pairs={{0,0},{1,9},{2,18},{3,27},{4,4},{5,13},{6,22},{7,31},{8,8},{9,1},{... | collective-permute-start | bytes 98312 | tf_op jit(solution)/shard_map/ppermute | solution.py:429
  36.8 27.6 %copy-start.1 = (bf16[32,8,1920]{2,1,0:T(8,128)(2,1)}, bf16[32,8,1920]{2,1,0:T(8,128)(2,1)S(1)}, u32[]{:S(2)}) copy-start(bf16[32,8,1920]{2,1,0:T(8,128)(2,1)S(1)} %all-to-all-done.1) | copy-start | bytes 2949124
  36.8 38.6 %all-to-all-start = ((bf16[32,8,2560]{2,1,0:T(8,128)(2,1)}), bf16[32,8,2560]{2,1,0:T(8,128)(2,1)S(1)}, u32[]{:S(2)}, u32[]{:S(2)}) async-start(bf16[32,8,2560]{2,1,0:T(8,128)(2,1)} %bitcast.18), calls=%async_computation | async-start | bytes 2621440 | tf_op jit(solution)/shard_map/all_to_all | solution.py:375
  75.4 1.1 copy-start

commit v3 on v2

--- a/solution.py
+++ b/solution.py
@@ -11,15 +11,14 @@
 HEADS = 4
 SUB = 8
 LANES = 128
-VMEM_LIMIT = 60 * 1024 * 1024
 ALL = ("doc", "ctx")
 
 
-def call(kernel, name, **options):
+def call(kernel, name, vmem=32, **options):
     return pl.pallas_call(
         kernel,
         name=name,
-        compiler_params=pltpu.CompilerParams(vmem_limit_bytes=VMEM_LIMIT),
+        compiler_params=pltpu.CompilerParams(vmem_limit_bytes=vmem * 1024 * 1024),
         **options,
     )
 
@@ -281,10 +280,24 @@
 
 
 def apply_kernel(blocks, capacity, latent_count, members, me, tags, down, up, arrived, *refs):
-    *ready, update, stage = refs
+    *ready, update, arrived_in, stage, done = refs
     width = down.shape[1]
     piece = width // SUB
-    fill_stage(stage, (arrived,))
+    start = sum(part.shape[1] for part in ready)
+    incoming = [
+        pltpu.make_async_copy(
+            arrived.at[:, pl.ds(slot * piece, piece)], arrived_in.at[slot], done.at[slot]
+        )
+        for slot in range(capacity)
+    ] + [pltpu.make_async_copy(part, update.at[:, pl.ds(0, start)], done.at[capacity]) for part in ready]
+    for copy in incoming:
+        copy.start()
+    for slot in range(capacity):
+        incoming[slot].wait()
+        for lane in range(piece // LANES):
+            stage[slot * (piece // LANES) + lane] = arrived_in[
+                slot, :, lane * LANES : (lane + 1) * LANES
+            ].astype(jnp.float32)
     coeff = None
     for index in range(SUB):
         part = lax.dot_general(
@@ -304,19 +317,18 @@
             coeff, up[:, index * piece : (index + 1) * piece], preferred_element_type=jnp.float32
         ) * (1.0 / math.sqrt(latent_count))
         scatter_pieces(stage, index, moved, blocks, capacity, piece)
-    start = 0
-    for part in ready:
-        start = part.shape[1]
-        update[:, :start] = part[...]
     drain_stage(stage, (update.at[:, start:],))
-
-
-def finish_kernel(blocks, capacity, returned, slots, requests, adapted, stage):
+    for copy in incoming[capacity:]:
+        copy.wait()
+
+
+def finish_kernel(blocks, capacity, returned, slots, requests, adapted, adapted_out, stage, done):
     rows, width = requests.shape
     piece = width // SUB
     fill_stage(stage, (returned,))
     placed = lax.broadcasted_iota(jnp.int32, (capacity * blocks, rows), 0) == slots[...]
     placer = placed.astype(jnp.float32).astype(jnp.bfloat16)
+    leaving = []
     for index in range(SUB):
         gathered = lax.dot_general(
             placer,
@@ -324,10 +336,17 @@
             (((0,), (0,)), ((), ())),
             preferred_element_type=jnp.float32,
         )
-        columns = slice(index * piece, (index + 1) * piece)
-        adapted[:, columns] = (requests[:, columns].astype(jnp.float32) + gathered).astype(
-            adapted.dtype
-        )
+        adapted_out[index] = (
+            requests[:, index * piece : (index + 1) * piece].astype(jnp.float32) + gathered
+        ).astype(adapted.dtype)
+        leaving.append(
+            pltpu.make_async_copy(
+                adapted_out.at[index], adapted.at[:, pl.ds(index * piece, piece)], done.at[index]
+            )
+        )
+        leaving[index].start()
+    for copy in leaving:
+        copy.wait()
 
 
 def on_device(
@@ -361,6 +380,7 @@
     in_smem = pl.BlockSpec(memory_space=pltpu.SMEM)
     in_vmem = pl.BlockSpec(memory_space=pltpu.VMEM)
     in_hbm = pl.BlockSpec(memory_space=pl.ANY)
+    outside = pl.BlockSpec(memory_space=pltpu.HBM)
 
     def after(values, *others):
         return lax.optimization_barrier((values, *others))[0]
@@ -379,6 +399,7 @@
     first_sent, second_sent, tags, slots = call(
         functools.partial(place_kernel, blocks, capacity),
         "place_rows",
+        vmem=60,
         out_shape=(
             block_type(early),
             block_type(late),
@@ -402,6 +423,7 @@
     partial = call(
         functools.partial(attend_kernel, chunks),
         "attend",
+        vmem=60,
         in_specs=[in_hbm] * 3 + [in_vmem] * 2,
         out_shape=jax.ShapeDtypeStruct((partial_rows, head_dim), jnp.float32),
         scratch_shapes=[
@@ -439,6 +461,7 @@
     down_factor, up_factor, first_tags, second_tags = call(
         functools.partial(factor_kernel, blocks, capacity, early, latent_count, chunks),
         "factors",
+        vmem=60,
         in_specs=[in_smem, in_vmem, in_hbm, in_hbm],
         out_specs=(in_hbm, in_hbm, in_vmem, in_vmem),
         out_shape=(factor_type, factor_type, tag_type(early), tag_type(late)),
@@ -455,9 +478,13 @@
         return call(
             functools.partial(apply_kernel, blocks, slot_count, latent_count, ctx_count),
             "apply_rows",
-            in_specs=[in_smem] + [in_vmem] * (4 + len(ready)),
+            in_specs=[in_smem] + [in_vmem] * 3 + [outside] * (1 + len(ready)),
             out_shape=block_type(total),
-            scratch_shapes=[stage_type(slot_count)],
+            scratch_shapes=[
+                pltpu.VMEM((slot_count, blocks * SUB, piece), jnp.bfloat16),
+                stage_type(slot_count),
+                pltpu.SemaphoreType.DMA((slot_count + len(ready),)),
+            ],
         )(me, tag_column, down_factor, up_factor, arrived, *ready)
 
     first_update = apply(first_tags, early, first_arrived)
@@ -466,8 +493,13 @@
     return call(
         functools.partial(finish_kernel, blocks, capacity),
         "finish_rows",
+        out_specs=outside,
         out_shape=jax.ShapeDtypeStruct((rows, width), jnp.bfloat16),
-        scratch_shapes=[stage_type(capacity)],
+        scratch_shapes=[
+            pltpu.VMEM((SUB, rows, piece), jnp.bfloat16),
+            stage_type(capacity),
+            pltpu.SemaphoreType.DMA((SUB,)),
+        ],
     )(returned, slots, requests)
 
 

time: 146 us -> 141 us (0.966)
  Pallas kernels: 37.6 us -> 27.8 us
  local copies, waits for them, and re-layouts: 1.06 us -> 6.81 us
  blocking collectives: 79.7 us -> 77.8 us
    unnamed x4 -> x30, local copies, waits for them, and re-layouts: 1.06 us -> 6.81 us
    pallas_call x2, Pallas kernels: 10 us -> 4.62 us  [apply(): call(functools.partial(apply_kernel, blocks, slot_count, latent_count, ct...]
    pallas_call x1, Pallas kernels: 5.28 us -> 2.5 us  [on_device(): call(functools.partial(finish_kernel, blocks, capacity), 'finish_rows', o...]
    pallas_call x1, Pallas kernels: 2.1 us -> 0.36 us  [on_device(): call(functools.partial(summary_kernel, tag_parts), 'summarize', out_shape...]
  transfers between devices with their start and end apart: 4 -> 4, of which waited for: 3 -> 3; matrix products, arithmetic and copies ran while one was open for 0% -> 0% of each run, Pallas kernels for 15% -> 13%
where the time goes in v3:
time: 141 us; the launch traced here: 140 us
  blocking collectives  77.8 us (55%)
  Pallas kernels  27.8 us (20%)
  starting transfers between devices  15.7 us (11%)
  waiting for transfers between devices  11.8 us (8%)
  local copies, waits for them, and re-layouts  6.81 us (5%)
    all_to_all x1, blocking collectives, exchange(): lax.all_to_all(values.reshape(blocks, SUB, -1), ALL, split_axis=0, concat...  57.8 us
    all_to_all x2, starting transfers between devices, exchange(): lax.all_to_all(values.reshape(blocks, SUB, -1), ALL, split_axis=0, concat...  13.8 us
    all_gather x1, blocking collectives, on_device(): lax.all_gather(jnp.stack(fetched), 'ctx')  13.6 us
    all_to_all x2, waiting for transfers between devices, exchange(): lax.all_to_all(values.reshape(blocks, SUB, -1), ALL, split_axis=0, concat...  9.57 us
    pallas_call x1, Pallas kernels, on_device(): call(functools.partial(attend_kernel, chunks), 'attend', vmem=60, in_spec...  8.22 us
    pallas_call x1, Pallas kernels, on_device(): call(functools.partial(factor_kernel, blocks, capacity, early, latent_cou...  7.47 us
    unnamed x30, local copies, waits for them, and re-layouts  6.81 us
    all_gather x1, blocking collectives, on_device(): lax.all_gather(partial, 'ctx')  6.34 us
  transfers between devices with their start and end apart: 4, of which 3 were waited for; matrix products, arithmetic and copies ran while one was open for 0% of the time, Pallas kernels for 13%

profile of v3, /device:TPU:0, one launch (start us, length us, event | category | flops | bytes accessed | tf_op | source)
XLA Modules:
  0.0 140.0 jit_solution(14227937283656950631)
XLA Ops:
  0.0 4.7 %place_rows.1 = (bf16[256,1920]{1,0:T(8,128)(2,1)}, bf16[256,2560]{1,0:T(8,128)(2,1)}, f32[2,128]{1,0:T(2,128)}, s32[1,192]{1,0:T(1,128)}) custom-call(s32[1,32]{1,0:T(1,128)} %bitcast.24, s32[1,192]{1,0:T(1,128)} %bitcast.22, s32[1,192]{1,0:T(1,128)} %bitcast.23, bf16[192,5120]{1,0:T(8,128)(2,1)} %requests.3), custom_call_target="tpu_custom_call" | custom-call | tf_op jit(solution)/shard_map/place_rows/pallas_call | solution.py:399
  4.7 7.3 %all-to-all-start.1 = ((bf16[32,8,1920]{2,1,0:T(8,128)(2,1)}), bf16[32,8,1920]{2,1,0:T(8,128)(2,1)S(1)}, u32[]{:S(2)}, u32[]{:S(2)}) async-start(bf16[32,8,1920]{2,1,0:T(8,128)(2,1)} %bitcast.19), calls=%async_computation.1 | async-start | bytes 1966080 | tf_op jit(solution)/shard_map/all_to_all | solution.py:395
  12.0 0.0 copy-start.9
  12.0 0.0 copy-start.10
  12.0 0.0 copy-start.13
  12.0 8.2 %attend.1 = f32[72,128]{1,0:T(8,128)} custom-call(bf16[1,256,5120]{2,1,0:T(8,128)(2,1)} %tokens.1, bf16[5120,512]{1,0:T(8,128)(2,1)} %w_keys.1, bf16[5120,512]{1,0:T(8,128)(2,1)} %w_values.1, f32[16,512]{1,0:T(8,128)} %latents.3, f32[2,128]{1,0:T(2,128)} %get-tuple-element.15.tags), custom_call_target="tpu_custom_call" | custom-call | tf_op jit(solution)/shard_map/attend/pallas_call | solution.py:423
  20.2 6.3 %all-gather = f32[288,128]{1,0:T(8,128)S(1)} all-gather(f32[72,128]{1,0:T(8,128)} %attend.1), channel_id=2, replica_groups=mesh['doc'=8,'ctx'=4] {'ctx'}, dimensions={0}, use_global_device_ids=true | all-gather | bytes 184320 | tf_op jit(solution)/shard_map/all_gather | solution.py:441
  26.6 0.0 copy-done.9
  26.6 0.4 summarize.1
  26.9 1.2 collective-permute-start.1
  28.1 0.7 collective-permute-start
  28.8 2.2 %collective-permute-done.1 = bf16[32,512]{1,0:T(8,128)(2,1)S(1)} collective-permute-done((bf16[32,512]{1,0:T(8,128)(2,1)S(1)}, bf16[32,512]{1,0:T(8,128)(2,1)S(1)}, u32[]{:S(2)}, u32[]{:S(2)}) %collective-permute-start.1) | collective-permute-done | bytes 32800 | tf_op jit(solution)/shard_map/ppermute | solution.py:451
  31.0 0.0 collective-permute-done
  31.0 5.8 %all-to-all-done.1 = bf16[32,8,1920]{2,1,0:T(8,128)(2,1)S(1)} async-done(((bf16[32,8,1920]{2,1,0:T(8,128)(2,1)}), bf16[32,8,1920]{2,1,0:T(8,128)(2,1)S(1)}, u32[]{:S(2)}, u32[]{:S(2)}) %all-to-all-start.1) | async-done | bytes 983072 | tf_op jit(solution)/shard_map/all_to_all | solution.py:395
  36.8 6.5 %all-to-all-start = ((bf16[32,8,2560]{2,1,0:T(8,128)(2,1)}), bf16[32,8,2560]{2,1,0:T(8,128)(2,1)}, u32[]{:S(2)}, u32[]{:S(2)}) async-start(bf16[32,8,2560]{2,1,0:T(8,128)(2,1)} %bitcast.8), calls=%async_computation | async-start | bytes 2621440 | tf_op jit(solution)/shard_map/all_to_all | solution.py:395
  43.4 13.6 %all-gather.1.everyone = bf16[8,32,512]{2,1,0:T(8,128)(2,1)} all-gather(bf16[2,32,512]{2,1,0:T(8,128)(2,1)S(1)} %pad_maximum_fusion), channel_id=3, replica_groups=mesh['doc'=8,'ctx'=4] {'ctx'}, dimensions={0}, use_global_device_ids=true | all-gather | bytes 327680 | tf_op jit(solution)/shard_map/all_gather | solution.py:453
  57.0 7.5 %factors.1 = (bf16[128,5120]{1,0:T(8,128)(2,1)}, bf16[128,5120]{1,0:T(8,128)(2,1)}, s32[96,1]{1,0:T(8,128)}, s32[128,1]{1,0:T(8,128)}) custom-call(s32[1,1]{1,0:T(1,128)} %bitcast.me, bf16[8,32,512]{2,1,0:T(8,128)(2,1)} %all-gather.1.everyone, bf16[1,512,5120]{2,1,0:T(8,128)(2,1)} %heads_down.1, bf16[1,512,5120]{2,1,0:T(8,128)(2,1)} %heads_up.1), custom_call_target="tpu_custom_call" | custom-call | tf_op jit(solution)/shard_map/factors/pallas_call | solution.py:461
  64.5 1.3 copy-done.1
  65.8 1.3 copy-done.3
  67.1 1.2 copy-done.8
  68.3 0.8 copy-done.12
  69.2 1.6 %apply_rows.2.refs_0_ = bf16[256,1920]{1,0:T(8,128)(2,1)S(1)} custom-call(s32[1,1]{1,0:T(1,128)} %bitcast.me, s32[96,1]{1,0:T(8,128)S(1)} %copy-done.12, bf16[128,5120]{1,0:T(8,128)(2,1)S(1)} %copy-done.1, bf16[128,5120]{1,0:T(8,128)(2,1)S(1)} %copy-done.3, bf16[256,1920]{1,0:T(8,128)(2,1)S(1)} %bitcast.16), custom_call_target="tpu_custom_call" | custom-call | tf_op jit(solution)/shard_map/apply_rows/pallas_call | solution.py:478
  70.8 0.9 copy-done.5
  71.7 3.7 %all-to-all-done = bf16[32,8,2560]{2,1,0:T(8,128)(2,1)} async-done(((bf16[32,8,2560]{2,1,0:T(8,128)(2,1)}), bf16[32,8,2560]{2,1,0:T(8,128)(2,1)}, u32[]{:S(2)}, u32[]{:S(2)}) %all-to-all-start) | async-done | bytes 1310752 | tf_op jit(solution)/shard_map/all_to_all | solution.py:395
  75.5 0.0 copy-done.2
  75.5 0.0 copy-done.11
  75.5 1.2 copy-done.6
  76.7 3.0 %apply_rows.3 = bf16[256,4480]{1,0:T(8,128)(2,1)S(1)} custom-call(s32[1,1]{1,0:T(1,128)} %bitcast.me, s32[128,1]{1,0:T(8,128)S(1)} %copy-done.11, bf16[128,5120]{1,0:T(8,128)(2,1)S(1)} %copy-done.2, bf16[128,5120]{1,0:T(8,128)(2,1)S(1)} %copy-done.4, bf16[256,2560]{1,0:T(8,128)(2,1)} %bitcast.9.arrived, bf16[256,1920]{1,0:T(8,128)(2,1)S(1)} %copy-done.6), custom_call_target="tpu_custom_call" | custom-call | tf_op jit(solution)/shard_map/apply_rows/pallas_call | solution.py:478
  79.7 0.0 copy-start
  79.7 0.0 copy-start.14
  79.7 57.8 %all_to_all.15 = bf16[32,8,4480]{2,1,0:T(8,128)(2,1)S(1)} all-to-all(bf16[32,8,4480]{2,1,0:T(8,128)(2,1)S(1)} %bitcast.14), channel_id=1, replica_groups=mesh['doc'=8,'ctx'=4] {'doc','ctx'}, dimensions={0} | all-to-all | bytes 4587520 | tf_op jit(solution)/shard_map/all_to_all | solution.py:395
  137.5 2.5 %finish_rows.1 = bf16[192,5120]{1,0:T(8,128)(2,1)} custom-call(bf16[256,4480]{1,0:T(8,128)(2,1)S(1)} %bitcast.15, s32[1,192]{1,0:T(1,128)S(1)} %copy-done.14, bf16[192,5120]{1,0:T(8,128)(2,1)S(1)} %copy-done), custom_call_target="tpu_custom_call" | custom-call | tf_op jit(solution)/shard_map/finish_rows/pallas_call | solution.py:493
  (17 shorter events, 0.0 us)
Async XLA Ops:
  4.7 32.1 %all-to-all-start.1 = ((bf16[32,8,1920]{2,1,0:T(8,128)(2,1)}), bf16[32,8,1920]{2,1,0:T(8,128)(2,1)S(1)}, u32[]{:S(2)}, u32[]{:S(2)}) async-start(bf16[32,8,1920]{2,1,0:T(8,128)(2,1)} %bitcast.19), calls=%async_computation.1 | async-start | bytes 1966080 | tf_op jit(solution)/shard_map/all_to_all | solution.py:395
  12.0 14.6 %copy-start.9 = (bf16[512,512]{1,0:T(8,128)(2,1)S(1)}, bf16[512,512]{1,0:T(8,128)(2,1)}, u32[]{:S(2)}) copy-start(bf16[512,512]{1,0:T(8,128)(2,1)} %w_out.1) | copy-start | bytes 1572868
  12.0 14.6 %copy-start.10 = (f32[16,512]{1,0:T(8,128)S(1)}, f32[16,512]{1,0:T(8,128)}, u32[]{:S(2)}) copy-start(f32[16,512]{1,0:T(8,128)} %latents.3) | copy-start | bytes 98308
  12.0 14.6 %copy-start.13 = (f32[512]{0:T(512)S(1)}, f32[512]{0:T(512)}, u32[]{:S(2)}) copy-start(f32[512]{0:T(512)} %param.17) | copy-start | bytes 6148
  26.9 4.0 %collective-permute-start.1 = (bf16[32,512]{1,0:T(8,128)(2,1)S(1)}, bf16[32,512]{1,0:T(8,128)(2,1)S(1)}, u32[]{:S(2)}, u32[]{:S(2)}) collective-permute-start(bf16[32,512]{1,0:T(8,128)(2,1)S(1)} %summarize.1), channel_id=1, source_target_pairs={{0,4},{1,13},{2,22},{3,31},{4,0},{5,9},{6,18},{7,27},{8,12},{9,5},... | collective-permute-start | bytes 98312 | tf_op jit(solution)/shard_map/ppermute | solution.py:451
  28.1 2.8 %collective-permute-start = (bf16[32,512]{1,0:T(8,128)(2,1)S(1)}, bf16[32,512]{1,0:T(8,128)(2,1)S(1)}, u32[]{:S(2)}, u32[]{:S(2)}) collective-permute-start(bf16[32,512]{1,0:T(8,128)(2,1)S(1)} %summarize.1), channel_id=1, source_target_pairs={{0,0},{1,9},{2,18},{3,27},{4,4},{5,13},{6,22},{7,31},{8,8},{9,1},{... | collective-permute-start | bytes 98312 | tf_op jit(solution)/shard_map/ppermute | solution.py:451
  36.8 27.7 %copy-start.7 = (bf16[32,8,1920]{2,1,0:T(8,128)(2,1)}, bf16[32,8,1920]{2,1,0:T(8,128)(2,1)S(1)}, u32[]{:S(2)}) copy-start(bf16[32,8,1920]{2,1,0:T(8,128)(2,1)S(1)} %all-to-all-done.1) | copy-start | bytes 2949124
  36.8 38.7 %all-to-all-start = ((bf16[32,8,2560]{2,1,0:T(8,128)(2,1)}), bf16[32,8,2560]{2,1,0:T(8,128)(2,1)}, u32[]{:S(2)}, u32[]{:S(2)}) async-start(bf16[32,8,2560]{2,1,0:T(8,128)(2,1)} %bitcast.8), calls=%async_computation | async-start | bytes 2621440 | tf_op jit(solution)/shard_map/all_to_all | solution.py:395
  64.5 1.3 copy-start.1
  65.8 1.3 copy-start.3
  67.1 1.2 copy-start.8
  68.3 0.8 copy-start.12
  69.1 6.3 %copy-start.2 = (bf16[128,5120]{1,0:T(8,128)(2,1)S(1)}, bf16[128,5120]{1,0:T(8,128)(2,1)}, u32[]{:S(2)}) copy-start(bf16[128,5120]{1,0:T(8,128)(2,1)} %get-tuple-element.17.down) | copy-start | bytes 3932164
  69.1 6.3 %copy-start.4 = (bf16[128,5120]{1,0:T(8,128)(2,1)S(1)}, bf16[128,5120]{1,0:T(8,128)(2,1)}, u32[]{:S(2)}) copy-start(bf16[128,5120]{1,0:T(8,128)(2,1)} %get-tuple-element.18.up) | copy-start | bytes 3932164
  69.2 6.3 %copy-start.11 = (s32[128,1]{1,0:T(8,128)S(1)}, s32[128,1]{1,0:T(8,128)}, u32[]{:S(2)}) copy-start(s32[128,1]{1,0:T(8,128)} %get-tuple-element.16.tags) | copy-start | bytes 1540
  70.8 1.0 copy-start.5
  75.5 1.2 copy-start.6
  79.7 57.8 %copy-start = (bf16[192,5120]{1,0:T(8,128)(2,1)S(1)}, bf16[192,5120]{1,0:T(8,128)(2,1)}, u32[]{:S(2)}) copy-start(bf16[192,5120]{1,0:T(8,128)(2,1)} %requests.3) | copy-start | bytes 5898244
  79.7 57.8 %copy-start.14 = (s32[1,192]{1,0:T(1,128)S(1)}, s32[1,192]{1,0:T(1,128)}, u32[]{:S(2)}) copy-start(s32[1,192]{1,0:T(1,128)} %get-tuple-element.24.slots) | copy-start | bytes 2308

commit v4 on v3

--- a/solution.py
+++ b/solution.py
@@ -11,6 +11,7 @@
 HEADS = 4
 SUB = 8
 LANES = 128
+LONG = 20 * 1024 * 1024
 ALL = ("doc", "ctx")
 
 
@@ -254,7 +255,10 @@
     device = me[0, 0]
     my_doc = device // members
     by_entry = jnp.concatenate(
-        [everyone[x, latent_count:, :].astype(jnp.float32)[:members] for x in range(documents)],
+        [
+            everyone[x, latent_count : latent_count + members, :].astype(jnp.float32)
+            for x in range(documents)
+        ],
         axis=0,
     ).astype(jnp.bfloat16)
     source = lax.broadcasted_iota(jnp.int32, (blocks, blocks), 0)
@@ -279,18 +283,25 @@
         job[3].wait()
 
 
-def apply_kernel(blocks, capacity, latent_count, members, me, tags, down, up, arrived, *refs):
-    *ready, update, arrived_in, stage, done = refs
+def coeff_kernel(blocks, capacity, latent_count, members, me, tags, down, arrived, *refs):
+    coeff_out, arrived_in, stage, done = refs
+    coeff_out[...] = coefficients(
+        blocks, capacity, latent_count, members, me, tags, down, arrived, arrived_in, stage, done
+    )
+
+
+def coefficients(
+    blocks, capacity, latent_count, members, me, tags, down, arrived, arrived_in, stage, done, *later
+):
     width = down.shape[1]
     piece = width // SUB
-    start = sum(part.shape[1] for part in ready)
     incoming = [
         pltpu.make_async_copy(
             arrived.at[:, pl.ds(slot * piece, piece)], arrived_in.at[slot], done.at[slot]
         )
         for slot in range(capacity)
-    ] + [pltpu.make_async_copy(part, update.at[:, pl.ds(0, start)], done.at[capacity]) for part in ready]
-    for copy in incoming:
+    ]
+    for copy in incoming + list(later):
         copy.start()
     for slot in range(capacity):
         incoming[slot].wait()
@@ -298,28 +309,39 @@
             stage[slot * (piece // LANES) + lane] = arrived_in[
                 slot, :, lane * LANES : (lane + 1) * LANES
             ].astype(jnp.float32)
-    coeff = None
+    coeff = 0.0
     for index in range(SUB):
-        part = lax.dot_general(
+        coeff = coeff + lax.dot_general(
             gather_pieces(stage, index, blocks, capacity, piece),
             down[:, index * piece : (index + 1) * piece],
             (((1,), (1,)), ((), ())),
             preferred_element_type=jnp.float32,
         )
-        coeff = part if coeff is None else coeff + part
     column_doc = (
         lax.broadcasted_iota(jnp.int32, coeff.shape, 1) // latent_count
     ) ^ (me[0, 0] // members)
     matched = tags[...] - 1 == column_doc
-    coeff = jnp.where(matched, coeff / math.sqrt(width), 0.0).astype(jnp.bfloat16)
+    return jnp.where(matched, coeff / math.sqrt(width), 0.0).astype(jnp.bfloat16)
+
+
+def update_kernel(
+    blocks, capacity, latent_count, members, me, tags, down, up, first_coeff, arrived, *refs
+):
+    update, arrived_in, stage, done, up_in, up_done = refs
+    piece = down.shape[1] // SUB
+    late = arrived.shape[1] // piece
+    up_copy = pltpu.make_async_copy(up.at[:, pl.ds(0, down.shape[1])], up_in, up_done)
+    coeff = coefficients(
+        blocks, late, latent_count, members, me, tags, down, arrived, arrived_in, stage, done, up_copy
+    )
+    coeff = jnp.concatenate([first_coeff[...], coeff], axis=0)
+    up_copy.wait()
     for index in range(SUB):
         moved = jnp.dot(
-            coeff, up[:, index * piece : (index + 1) * piece], preferred_element_type=jnp.float32
+            coeff, up_in[:, index * piece : (index + 1) * piece], preferred_element_type=jnp.float32
         ) * (1.0 / math.sqrt(latent_count))
         scatter_pieces(stage, index, moved, blocks, capacity, piece)
-    drain_stage(stage, (update.at[:, start:],))
-    for copy in incoming[capacity:]:
-        copy.wait()
+    drain_stage(stage, (update,))
 
 
 def finish_kernel(blocks, capacity, returned, slots, requests, adapted, adapted_out, stage, done):
@@ -433,7 +455,7 @@
             pltpu.SemaphoreType.DMA((chunks, 3)),
         ],
     )(tokens, w_keys, w_values, latents, tags)
-    packet_rows = latent_count + 16
+    packet_rows = latent_count + -(-ctx_count // SUB) * SUB
     packet = call(
         functools.partial(summary_kernel, tag_parts),
         "summarize",
@@ -458,13 +480,17 @@
         return jax.ShapeDtypeStruct((slot_count * blocks, 1), jnp.int32)
 
     factor_type = jax.ShapeDtypeStruct((doc_count * latent_count, width), jnp.bfloat16)
+    long_columns = -(-LONG // (doc_count * latent_count) // LANES) * LANES
+    long_type = jax.ShapeDtypeStruct(
+        (doc_count * latent_count, max(width, long_columns)), jnp.bfloat16
+    )
     down_factor, up_factor, first_tags, second_tags = call(
         functools.partial(factor_kernel, blocks, capacity, early, latent_count, chunks),
         "factors",
         vmem=60,
         in_specs=[in_smem, in_vmem, in_hbm, in_hbm],
         out_specs=(in_hbm, in_hbm, in_vmem, in_vmem),
-        out_shape=(factor_type, factor_type, tag_type(early), tag_type(late)),
+        out_shape=(factor_type, long_type, tag_type(early), tag_type(late)),
         scratch_shapes=[
             pltpu.VMEM((chunks, 2, latent_width, depth), jnp.bfloat16),
             pltpu.VMEM((chunks, 2, doc_count * latent_count, depth), jnp.bfloat16),
@@ -473,22 +499,30 @@
         ],
     )(me, everyone, heads_down, heads_up)
 
-    def apply(tag_column, slot_count, arrived, *ready):
-        total = slot_count + sum(part.shape[1] for part in ready) // piece
-        return call(
-            functools.partial(apply_kernel, blocks, slot_count, latent_count, ctx_count),
-            "apply_rows",
-            in_specs=[in_smem] + [in_vmem] * 3 + [outside] * (1 + len(ready)),
-            out_shape=block_type(total),
-            scratch_shapes=[
-                pltpu.VMEM((slot_count, blocks * SUB, piece), jnp.bfloat16),
-                stage_type(slot_count),
-                pltpu.SemaphoreType.DMA((slot_count + len(ready),)),
-            ],
-        )(me, tag_column, down_factor, up_factor, arrived, *ready)
-
-    first_update = apply(first_tags, early, first_arrived)
-    update = apply(second_tags, late, after(second_arrived, first_update), first_update)
+    def row_scratch(slot_count, stage_count):
+        return [
+            pltpu.VMEM((slot_count, blocks * SUB, piece), jnp.bfloat16),
+            stage_type(stage_count),
+            pltpu.SemaphoreType.DMA((slot_count,)),
+        ]
+
+    first_coeff = call(
+        functools.partial(coeff_kernel, blocks, early, latent_count, ctx_count),
+        "coefficients",
+        in_specs=[in_smem] + [in_vmem] * 2 + [outside],
+        out_shape=jax.ShapeDtypeStruct(
+            (early * blocks, doc_count * latent_count), jnp.bfloat16
+        ),
+        scratch_shapes=row_scratch(early, early),
+    )(me, first_tags, down_factor, first_arrived)
+    update = call(
+        functools.partial(update_kernel, blocks, capacity, latent_count, ctx_count),
+        "update",
+        in_specs=[in_smem] + [in_vmem] * 2 + [outside, in_vmem, outside],
+        out_shape=block_type(capacity),
+        scratch_shapes=row_scratch(late, capacity)
+        + [pltpu.VMEM(factor_type.shape, factor_type.dtype), pltpu.SemaphoreType.DMA],
+    )(me, second_tags, down_factor, up_factor, first_coeff, second_arrived)
     returned = exchange(update)
     return call(
         functools.partial(finish_kernel, blocks, capacity),

time: 141 us -> 139 us (0.986)
  waiting for transfers between devices: 11.8 us -> 15.5 us
  local copies, waits for them, and re-layouts: 6.81 us -> 3.35 us
    all_to_all x2, waiting for transfers between devices: 9.57 us -> 13.3 us  [exchange(): lax.all_to_all(values.reshape(blocks, SUB, -1), ALL, split_axis=0, concat...]
    unnamed x30 -> x22, local copies, waits for them, and re-layouts: 6.81 us -> 3.35 us
  transfers between devices with their start and end apart: 4 -> 4, of which waited for: 3 -> 3; matrix products, arithmetic and copies ran while one was open for 0% -> 0% of each run, Pallas kernels for 13% -> 12%
where the time goes in v4:
time: 139 us; the launch traced here: 138 us
  blocking collectives  77.4 us (56%)
  Pallas kernels  27 us (19%)
  waiting for transfers between devices  15.5 us (11%)
  starting transfers between devices  14.7 us (11%)
  local copies, waits for them, and re-layouts  3.35 us (2%)
    all_to_all x1, blocking collectives, exchange(): lax.all_to_all(values.reshape(blocks, SUB, -1), ALL, split_axis=0, concat...  57.8 us
    all_to_all x2, waiting for transfers between devices, exchange(): lax.all_to_all(values.reshape(blocks, SUB, -1), ALL, split_axis=0, concat...  13.3 us
    all_gather x1, blocking collectives, on_device(): lax.all_gather(jnp.stack(fetched), 'ctx')  13.2 us
    all_to_all x2, starting transfers between devices, exchange(): lax.all_to_all(values.reshape(blocks, SUB, -1), ALL, split_axis=0, concat...  13 us
    pallas_call x1, Pallas kernels, on_device(): call(functools.partial(attend_kernel, chunks), 'attend', vmem=60, in_spec...  8.13 us
    pallas_call x1, Pallas kernels, on_device(): call(functools.partial(factor_kernel, blocks, capacity, early, latent_cou...  7.41 us
    all_gather x1, blocking collectives, on_device(): lax.all_gather(partial, 'ctx')  6.43 us
    pallas_call x1, Pallas kernels, on_device(): call(functools.partial(place_kernel, blocks, capacity), 'place_rows', vme...  4.65 us
  transfers between devices with their start and end apart: 4, of which 3 were waited for; matrix products, arithmetic and copies ran while one was open for 0% of the time, Pallas kernels for 12%

profile of v4, /device:TPU:0, one launch (start us, length us, event | category | flops | bytes accessed | tf_op | source)
XLA Modules:
  0.0 138.1 jit_solution(12771328751707853437)
XLA Ops:
  0.0 4.7 %place_rows.1 = (bf16[256,1920]{1,0:T(8,128)(2,1)}, bf16[256,2560]{1,0:T(8,128)(2,1)}, f32[2,128]{1,0:T(2,128)}, s32[1,192]{1,0:T(1,128)}) custom-call(s32[1,32]{1,0:T(1,128)} %bitcast.26, s32[1,192]{1,0:T(1,128)} %bitcast.24, s32[1,192]{1,0:T(1,128)} %bitcast.25, bf16[192,5120]{1,0:T(8,128)(2,1)} %requests.3), custom_call_target="tpu_custom_call" | custom-call | tf_op jit(solution)/shard_map/place_rows/pallas_call | solution.py:421
  4.7 7.3 %all-to-all-start = ((bf16[32,8,1920]{2,1,0:T(8,128)(2,1)}), bf16[32,8,1920]{2,1,0:T(8,128)(2,1)S(1)}, u32[]{:S(2)}, u32[]{:S(2)}) async-start(bf16[32,8,1920]{2,1,0:T(8,128)(2,1)} %bitcast.21), calls=%async_computation | async-start | bytes 1966080 | tf_op jit(solution)/shard_map/all_to_all | solution.py:417
  12.0 0.0 copy-start.5
  12.0 0.0 copy-start.6
  12.0 0.0 copy-start.9
  12.0 8.1 %attend.1 = f32[72,128]{1,0:T(8,128)} custom-call(bf16[1,256,5120]{2,1,0:T(8,128)(2,1)} %tokens.1, bf16[5120,512]{1,0:T(8,128)(2,1)} %w_keys.1, bf16[5120,512]{1,0:T(8,128)(2,1)} %w_values.1, f32[16,512]{1,0:T(8,128)} %latents.3, f32[2,128]{1,0:T(2,128)} %get-tuple-element.14.tags), custom_call_target="tpu_custom_call" | custom-call | tf_op jit(solution)/shard_map/attend/pallas_call | solution.py:445
  20.1 6.4 %all-gather = f32[288,128]{1,0:T(8,128)S(1)} all-gather(f32[72,128]{1,0:T(8,128)} %attend.1), channel_id=2, replica_groups=mesh['doc'=8,'ctx'=4] {'ctx'}, dimensions={0}, use_global_device_ids=true | all-gather | bytes 184320 | tf_op jit(solution)/shard_map/all_gather | solution.py:463
  26.6 0.0 copy-done.5
  26.6 0.0 copy-done.6
  26.6 0.0 copy-done.9
  26.6 0.4 summarize.1
  26.9 1.0 collective-permute-start.1
  28.0 0.7 collective-permute-start
  28.6 2.1 %collective-permute-done.1 = bf16[24,512]{1,0:T(8,128)(2,1)S(1)} collective-permute-done((bf16[24,512]{1,0:T(8,128)(2,1)S(1)}, bf16[24,512]{1,0:T(8,128)(2,1)S(1)}, u32[]{:S(2)}, u32[]{:S(2)}) %collective-permute-start.1) | collective-permute-done | bytes 24608 | tf_op jit(solution)/shard_map/ppermute | solution.py:473
  30.8 0.0 collective-permute-done
  30.8 6.0 %all-to-all-done = bf16[32,8,1920]{2,1,0:T(8,128)(2,1)S(1)} async-done(((bf16[32,8,1920]{2,1,0:T(8,128)(2,1)}), bf16[32,8,1920]{2,1,0:T(8,128)(2,1)S(1)}, u32[]{:S(2)}, u32[]{:S(2)}) %all-to-all-start) | async-done | bytes 983072 | tf_op jit(solution)/shard_map/all_to_all | solution.py:417
  36.8 5.7 %all-to-all-start.1 = ((bf16[32,8,2560]{2,1,0:T(8,128)(2,1)}), bf16[32,8,2560]{2,1,0:T(8,128)(2,1)S(1)}, u32[]{:S(2)}, u32[]{:S(2)}) async-start(bf16[32,8,2560]{2,1,0:T(8,128)(2,1)} %bitcast.20), calls=%async_computation.1 | async-start | bytes 2621440 | tf_op jit(solution)/shard_map/all_to_all | solution.py:417
  42.6 13.2 %all-gather.1.everyone = bf16[8,24,512]{2,1,0:T(8,128)(2,1)} all-gather(bf16[2,24,512]{2,1,0:T(8,128)(2,1)S(1)} %pad_maximum_fusion), channel_id=3, replica_groups=mesh['doc'=8,'ctx'=4] {'ctx'}, dimensions={0}, use_global_device_ids=true | all-gather | bytes 245760 | tf_op jit(solution)/shard_map/all_gather | solution.py:475
  55.7 7.4 %factors.1 = (bf16[128,5120]{1,0:T(8,128)(2,1)}, bf16[128,163840]{1,0:T(8,128)(2,1)}, s32[96,1]{1,0:T(8,128)}, s32[128,1]{1,0:T(8,128)}) custom-call(s32[1,1]{1,0:T(1,128)} %bitcast.me, bf16[8,24,512]{2,1,0:T(8,128)(2,1)} %all-gather.1.everyone, bf16[1,512,5120]{2,1,0:T(8,128)(2,1)} %heads_down.1, bf16[1,512,5120]{2,1,0:T(8,128)(2,1)} %heads_up.1), custom_call_target="tpu_custom_call" | custom-call | tf_op jit(solution)/shard_map/factors/pallas_call | solution.py:487
  63.1 0.0 copy-done.3
  63.1 0.0 copy-start.1
  63.2 1.3 copy-done.1
  64.5 1.2 copy-done.4
  65.7 0.8 copy-done.8
  66.5 0.9 coefficients.1.first_coeff
  67.4 7.3 %all-to-all-done.1 = bf16[32,8,2560]{2,1,0:T(8,128)(2,1)S(1)} async-done(((bf16[32,8,2560]{2,1,0:T(8,128)(2,1)}), bf16[32,8,2560]{2,1,0:T(8,128)(2,1)S(1)}, u32[]{:S(2)}, u32[]{:S(2)}) %all-to-all-start.1) | async-done | bytes 1310752 | tf_op jit(solution)/shard_map/all_to_all | solution.py:417
  74.7 0.0 copy-done.7
  74.7 3.1 %update.1 = bf16[256,4480]{1,0:T(8,128)(2,1)S(1)} custom-call(s32[1,1]{1,0:T(1,128)} %bitcast.me, s32[128,1]{1,0:T(8,128)S(1)} %copy-done.7, bf16[128,5120]{1,0:T(8,128)(2,1)S(1)} %copy-done.2, bf16[128,163840]{1,0:T(8,128)(2,1)} %get-tuple-element.17.up, bf16[96,128]{1,0:T(8,128)(2,1)S(1)} %coefficients.1.first_coeff, bf16[256,2560]{1,0:T(8,128)(2,1)S(1)} %bitcast.16), custom_call_target="tpu_custom_call" | custom-call | tf_op jit(solution)/shard_map/update/pallas_call | solution.py:518
  77.8 0.0 copy-start
  77.8 57.8 %all_to_all.15 = bf16[32,8,4480]{2,1,0:T(8,128)(2,1)S(1)} all-to-all(bf16[32,8,4480]{2,1,0:T(8,128)(2,1)S(1)} %bitcast.14), channel_id=1, replica_groups=mesh['doc'=8,'ctx'=4] {'doc','ctx'}, dimensions={0} | all-to-all | bytes 4587520 | tf_op jit(solution)/shard_map/all_to_all | solution.py:417
  135.6 0.0 copy-done.10
  135.6 2.5 %finish_rows.1 = bf16[192,5120]{1,0:T(8,128)(2,1)} custom-call(bf16[256,4480]{1,0:T(8,128)(2,1)S(1)} %bitcast.15, s32[1,192]{1,0:T(1,128)S(1)} %copy-done.10, bf16[192,5120]{1,0:T(8,128)(2,1)S(1)} %copy-done), custom_call_target="tpu_custom_call" | custom-call | tf_op jit(solution)/shard_map/finish_rows/pallas_call | solution.py:527
  (9 shorter events, 0.0 us)
Async XLA Ops:
  4.7 32.1 %all-to-all-start = ((bf16[32,8,1920]{2,1,0:T(8,128)(2,1)}), bf16[32,8,1920]{2,1,0:T(8,128)(2,1)S(1)}, u32[]{:S(2)}, u32[]{:S(2)}) async-start(bf16[32,8,1920]{2,1,0:T(8,128)(2,1)} %bitcast.21), calls=%async_computation | async-start | bytes 1966080 | tf_op jit(solution)/shard_map/all_to_all | solution.py:417
  12.0 14.6 %copy-start.5 = (bf16[512,512]{1,0:T(8,128)(2,1)S(1)}, bf16[512,512]{1,0:T(8,128)(2,1)}, u32[]{:S(2)}) copy-start(bf16[512,512]{1,0:T(8,128)(2,1)} %w_out.1) | copy-start | bytes 1572868
  12.0 14.6 %copy-start.6 = (f32[16,512]{1,0:T(8,128)S(1)}, f32[16,512]{1,0:T(8,128)}, u32[]{:S(2)}) copy-start(f32[16,512]{1,0:T(8,128)} %latents.3) | copy-start | bytes 98308
  12.0 14.6 %copy-start.9 = (f32[512]{0:T(512)S(1)}, f32[512]{0:T(512)}, u32[]{:S(2)}) copy-start(f32[512]{0:T(512)} %param.17) | copy-start | bytes 6148
  26.9 3.9 %collective-permute-start.1 = (bf16[24,512]{1,0:T(8,128)(2,1)S(1)}, bf16[24,512]{1,0:T(8,128)(2,1)S(1)}, u32[]{:S(2)}, u32[]{:S(2)}) collective-permute-start(bf16[24,512]{1,0:T(8,128)(2,1)S(1)} %summarize.1), channel_id=1, source_target_pairs={{0,4},{1,13},{2,22},{3,31},{4,0},{5,9},{6,18},{7,27},{8,12},{9,5},... | collective-permute-start | bytes 73736 | tf_op jit(solution)/shard_map/ppermute | solution.py:473
  28.0 2.8 %collective-permute-start = (bf16[24,512]{1,0:T(8,128)(2,1)S(1)}, bf16[24,512]{1,0:T(8,128)(2,1)S(1)}, u32[]{:S(2)}, u32[]{:S(2)}) collective-permute-start(bf16[24,512]{1,0:T(8,128)(2,1)S(1)} %summarize.1), channel_id=1, source_target_pairs={{0,0},{1,9},{2,18},{3,27},{4,4},{5,13},{6,22},{7,31},{8,8},{9,1},{... | collective-permute-start | bytes 73736 | tf_op jit(solution)/shard_map/ppermute | solution.py:473
  36.8 26.3 %copy-start.3 = (bf16[32,8,1920]{2,1,0:T(8,128)(2,1)}, bf16[32,8,1920]{2,1,0:T(8,128)(2,1)S(1)}, u32[]{:S(2)}) copy-start(bf16[32,8,1920]{2,1,0:T(8,128)(2,1)S(1)} %all-to-all-done) | copy-start | bytes 2949124
  36.8 37.9 %all-to-all-start.1 = ((bf16[32,8,2560]{2,1,0:T(8,128)(2,1)}), bf16[32,8,2560]{2,1,0:T(8,128)(2,1)S(1)}, u32[]{:S(2)}, u32[]{:S(2)}) async-start(bf16[32,8,2560]{2,1,0:T(8,128)(2,1)} %bitcast.20), calls=%async_computation.1 | async-start | bytes 2621440 | tf_op jit(solution)/shard_map/all_to_all | solution.py:417
  63.1 1.3 copy-start.1
  64.5 1.2 copy-start.4
  65.7 0.8 copy-start.8
  66.5 8.2 %copy-start.2 = (bf16[128,5120]{1,0:T(8,128)(2,1)S(1)}, bf16[128,5120]{1,0:T(8,128)(2,1)}, u32[]{:S(2)}) copy-start(bf16[128,5120]{1,0:T(8,128)(2,1)} %get-tuple-element.16.down) | copy-start | bytes 3932164
  66.5 8.2 %copy-start.7 = (s32[128,1]{1,0:T(8,128)S(1)}, s32[128,1]{1,0:T(8,128)}, u32[]{:S(2)}) copy-start(s32[128,1]{1,0:T(8,128)} %get-tuple-element.15.tags) | copy-start | bytes 1540
  77.8 57.8 %copy-start = (bf16[192,5120]{1,0:T(8,128)(2,1)S(1)}, bf16[192,5120]{1,0:T(8,128)(2,1)}, u32[]{:S(2)}) copy-start(bf16[192,5120]{1,0:T(8,128)(2,1)} %requests.3) | copy-start | bytes 5898244
  77.8 57.8 %copy-start.10 = (s32[1,192]{1,0:T(1,128)S(1)}, s32[1,192]{1,0:T(1,128)}, u32[]{:S(2)}) copy-start(s32[1,192]{1,0:T(1,128)} %get-tuple-element.22.slots) | copy-start | bytes 2308

commit v5 on v4

--- a/solution.py
+++ b/solution.py
@@ -284,31 +284,19 @@
 
 
 def coeff_kernel(blocks, capacity, latent_count, members, me, tags, down, arrived, *refs):
-    coeff_out, arrived_in, stage, done = refs
+    coeff_out, stage = refs
     coeff_out[...] = coefficients(
-        blocks, capacity, latent_count, members, me, tags, down, arrived, arrived_in, stage, done
+        blocks, capacity, latent_count, members, me, tags, down, arrived, stage
     )
 
 
 def coefficients(
-    blocks, capacity, latent_count, members, me, tags, down, arrived, arrived_in, stage, done, *later
+    blocks, capacity, latent_count, members, me, tags, down, arrived, stage
 ):
     width = down.shape[1]
     piece = width // SUB
-    incoming = [
-        pltpu.make_async_copy(
-            arrived.at[:, pl.ds(slot * piece, piece)], arrived_in.at[slot], done.at[slot]
-        )
-        for slot in range(capacity)
-    ]
-    for copy in incoming + list(later):
-        copy.start()
-    for slot in range(capacity):
-        incoming[slot].wait()
-        for lane in range(piece // LANES):
-            stage[slot * (piece // LANES) + lane] = arrived_in[
-                slot, :, lane * LANES : (lane + 1) * LANES
-            ].astype(jnp.float32)
+    for lane in range(capacity * piece // LANES):
+        stage[lane] = arrived[:, lane * LANES : (lane + 1) * LANES].astype(jnp.float32)
     coeff = 0.0
     for index in range(SUB):
         coeff = coeff + lax.dot_general(
@@ -327,12 +315,13 @@
 def update_kernel(
     blocks, capacity, latent_count, members, me, tags, down, up, first_coeff, arrived, *refs
 ):
-    update, arrived_in, stage, done, up_in, up_done = refs
+    update, stage, up_in, up_done = refs
     piece = down.shape[1] // SUB
     late = arrived.shape[1] // piece
     up_copy = pltpu.make_async_copy(up.at[:, pl.ds(0, down.shape[1])], up_in, up_done)
+    up_copy.start()
     coeff = coefficients(
-        blocks, late, latent_count, members, me, tags, down, arrived, arrived_in, stage, done, up_copy
+        blocks, late, latent_count, members, me, tags, down, arrived, stage
     )
     coeff = jnp.concatenate([first_coeff[...], coeff], axis=0)
     up_copy.wait()
@@ -348,14 +337,14 @@
     rows, width = requests.shape
     piece = width // SUB
     fill_stage(stage, (returned,))
-    placed = lax.broadcasted_iota(jnp.int32, (capacity * blocks, rows), 0) == slots[...]
-    placer = placed.astype(jnp.float32).astype(jnp.bfloat16)
+    slot_column = as_column(slots[...])
+    wanted = lax.broadcasted_iota(jnp.int32, (rows, capacity * blocks), 1) == slot_column
+    picker = wanted.astype(jnp.float32).astype(jnp.bfloat16)
     leaving = []
     for index in range(SUB):
-        gathered = lax.dot_general(
-            placer,
+        gathered = jnp.dot(
+            picker,
             gather_pieces(stage, index, blocks, capacity, piece),
-            (((0,), (0,)), ((), ())),
             preferred_element_type=jnp.float32,
         )
         adapted_out[index] = (
@@ -463,16 +452,19 @@
     )(lax.all_gather(partial, "ctx"), latents, w_out, latent_gain.reshape(1, latent_width))
 
     share = doc_count // ctx_count
+    half = max(1, ctx_count // 2)
+    order = [ctx // 2 + ctx % 2 * half for ctx in range(ctx_count)]
     fetched = []
     for turn in range(share):
         pairs = [
-            (doc * ctx_count + ctx, (doc ^ (ctx * share + turn)) * ctx_count + ctx)
+            (doc * ctx_count + ctx, (doc ^ (order[ctx] * share + turn)) * ctx_count + ctx)
             for doc in range(doc_count)
             for ctx in range(ctx_count)
         ]
         fetched.append(lax.ppermute(packet, ALL, pairs))
     second_arrived = exchange(after(second_sent, *fetched))
-    everyone = lax.all_gather(jnp.stack(fetched), "ctx").reshape(
+    gathered = lax.all_gather(jnp.stack(fetched), "ctx")
+    everyone = jnp.stack([gathered[order.index(part)] for part in range(ctx_count)]).reshape(
         doc_count, packet_rows, latent_width
     )
 
@@ -499,29 +491,25 @@
         ],
     )(me, everyone, heads_down, heads_up)
 
-    def row_scratch(slot_count, stage_count):
-        return [
-            pltpu.VMEM((slot_count, blocks * SUB, piece), jnp.bfloat16),
-            stage_type(stage_count),
-            pltpu.SemaphoreType.DMA((slot_count,)),
-        ]
-
     first_coeff = call(
         functools.partial(coeff_kernel, blocks, early, latent_count, ctx_count),
         "coefficients",
-        in_specs=[in_smem] + [in_vmem] * 2 + [outside],
+        in_specs=[in_smem] + [in_vmem] * 3,
         out_shape=jax.ShapeDtypeStruct(
             (early * blocks, doc_count * latent_count), jnp.bfloat16
         ),
-        scratch_shapes=row_scratch(early, early),
+        scratch_shapes=[stage_type(early)],
     )(me, first_tags, down_factor, first_arrived)
     update = call(
         functools.partial(update_kernel, blocks, capacity, latent_count, ctx_count),
         "update",
-        in_specs=[in_smem] + [in_vmem] * 2 + [outside, in_vmem, outside],
+        in_specs=[in_smem] + [in_vmem] * 2 + [outside, in_vmem, in_vmem],
         out_shape=block_type(capacity),
-        scratch_shapes=row_scratch(late, capacity)
-        + [pltpu.VMEM(factor_type.shape, factor_type.dtype), pltpu.SemaphoreType.DMA],
+        scratch_shapes=[
+            stage_type(capacity),
+            pltpu.VMEM(factor_type.shape, factor_type.dtype),
+            pltpu.SemaphoreType.DMA,
+        ],
     )(me, second_tags, down_factor, up_factor, first_coeff, second_arrived)
     returned = exchange(update)
     return call(

time: 139 us -> 137 us (0.986)
  starting transfers between devices: 14.7 us -> 12.2 us
    all_to_all x2, starting transfers between devices: 13 us -> 10.5 us  [exchange(): lax.all_to_all(values.reshape(blocks, SUB, -1), ALL, split_axis=0, concat...]
  transfers between devices with their start and end apart: 4 -> 4, of which waited for: 3 -> 3; matrix products, arithmetic and copies ran while one was open for 0% -> 1% of each run, Pallas kernels for 12% -> 12%
where the time goes in v5:
time: 137 us
  blocking collectives  77 us (56%)
  Pallas kernels  27 us (20%)
  waiting for transfers between devices  16.3 us (12%)
  starting transfers between devices  12.2 us (9%)
  local copies, waits for them, and re-layouts  3.36 us (2%)
    all_to_all x1, blocking collectives, exchange(): lax.all_to_all(values.reshape(blocks, SUB, -1), ALL, split_axis=0, concat...  57.8 us
    all_to_all x2, waiting for transfers between devices, exchange(): lax.all_to_all(values.reshape(blocks, SUB, -1), ALL, split_axis=0, concat...  14.2 us
    all_gather x1, blocking collectives, on_device(): gathered = lax.all_gather(jnp.stack(fetched), 'ctx')  12.7 us
    all_to_all x2, starting transfers between devices, exchange(): lax.all_to_all(values.reshape(blocks, SUB, -1), ALL, split_axis=0, concat...  10.5 us
    pallas_call x1, Pallas kernels, on_device(): call(functools.partial(attend_kernel, chunks), 'attend', vmem=60, in_spec...  8.12 us
    pallas_call x1, Pallas kernels, on_device(): call(functools.partial(factor_kernel, blocks, capacity, early, latent_cou...  7.45 us
    all_gather x1, blocking collectives, on_device(): lax.all_gather(partial, 'ctx')  6.44 us
    pallas_call x1, Pallas kernels, on_device(): call(functools.partial(place_kernel, blocks, capacity), 'place_rows', vme...  4.65 us
  transfers between devices with their start and end apart: 4, of which 3 were waited for; matrix products, arithmetic and copies ran while one was open for 1% of the time, Pallas kernels for 12%

profile of v5, /device:TPU:0, one launch (start us, length us, event | category | flops | bytes accessed | tf_op | source)
XLA Modules:
  0.0 136.7 jit_solution(7126901975831394157)
XLA Ops:
  0.0 4.7 %place_rows.1 = (bf16[256,1920]{1,0:T(8,128)(2,1)}, bf16[256,2560]{1,0:T(8,128)(2,1)}, f32[2,128]{1,0:T(2,128)}, s32[1,192]{1,0:T(1,128)}) custom-call(s32[1,32]{1,0:T(1,128)} %bitcast.36, s32[1,192]{1,0:T(1,128)} %bitcast.34, s32[1,192]{1,0:T(1,128)} %bitcast.35, bf16[192,5120]{1,0:T(8,128)(2,1)} %requests.3), custom_call_target="tpu_custom_call" | custom-call | tf_op jit(solution)/shard_map/place_rows/pallas_call | solution.py:410
  4.7 7.3 %all-to-all-start = ((bf16[32,8,1920]{2,1,0:T(8,128)(2,1)}), bf16[32,8,1920]{2,1,0:T(8,128)(2,1)S(1)}, u32[]{:S(2)}, u32[]{:S(2)}) async-start(bf16[32,8,1920]{2,1,0:T(8,128)(2,1)} %bitcast.30), calls=%async_computation | async-start | bytes 1966080 | tf_op jit(solution)/shard_map/all_to_all | solution.py:406
  12.0 0.0 copy-start.5
  12.0 0.0 copy-start.6
  12.0 0.0 copy-start.9
  12.0 8.1 %attend.1 = f32[72,128]{1,0:T(8,128)} custom-call(bf16[1,256,5120]{2,1,0:T(8,128)(2,1)} %tokens.1, bf16[5120,512]{1,0:T(8,128)(2,1)} %w_keys.1, bf16[5120,512]{1,0:T(8,128)(2,1)} %w_values.1, f32[16,512]{1,0:T(8,128)} %latents.3, f32[2,128]{1,0:T(2,128)} %get-tuple-element.14.tags), custom_call_target="tpu_custom_call" | custom-call | tf_op jit(solution)/shard_map/attend/pallas_call | solution.py:434
  20.1 6.4 %all-gather = f32[288,128]{1,0:T(8,128)S(1)} all-gather(f32[72,128]{1,0:T(8,128)} %attend.1), channel_id=2, replica_groups=mesh['doc'=8,'ctx'=4] {'ctx'}, dimensions={0}, use_global_device_ids=true | all-gather | bytes 184320 | tf_op jit(solution)/shard_map/all_gather | solution.py:452
  26.6 0.0 copy-done.5
  26.6 0.0 copy-done.6
  26.6 0.0 copy-done.9
  26.6 0.4 summarize.1
  26.9 1.0 collective-permute-start.1
  28.0 0.7 collective-permute-start
  28.6 2.2 %collective-permute-done.1 = bf16[24,512]{1,0:T(8,128)(2,1)S(1)} collective-permute-done((bf16[24,512]{1,0:T(8,128)(2,1)S(1)}, bf16[24,512]{1,0:T(8,128)(2,1)S(1)}, u32[]{:S(2)}, u32[]{:S(2)}) %collective-permute-start.1) | collective-permute-done | bytes 24608 | tf_op jit(solution)/shard_map/ppermute | solution.py:464
  30.8 0.0 collective-permute-done
  30.8 7.0 %all-to-all-done = bf16[32,8,1920]{2,1,0:T(8,128)(2,1)S(1)} async-done(((bf16[32,8,1920]{2,1,0:T(8,128)(2,1)}), bf16[32,8,1920]{2,1,0:T(8,128)(2,1)S(1)}, u32[]{:S(2)}, u32[]{:S(2)}) %all-to-all-start) | async-done | bytes 983072 | tf_op jit(solution)/shard_map/all_to_all | solution.py:406
  37.8 3.2 %all-to-all-start.1 = ((bf16[32,8,2560]{2,1,0:T(8,128)(2,1)}), bf16[32,8,2560]{2,1,0:T(8,128)(2,1)S(1)}, u32[]{:S(2)}, u32[]{:S(2)}) async-start(bf16[32,8,2560]{2,1,0:T(8,128)(2,1)} %bitcast.29), calls=%async_computation.1 | async-start | bytes 2621440 | tf_op jit(solution)/shard_map/all_to_all | solution.py:406
  41.0 12.7 %all-gather.1 = bf16[8,24,512]{2,1,0:T(8,128)(2,1)S(1)} all-gather(bf16[2,24,512]{2,1,0:T(8,128)(2,1)S(1)} %pad_maximum_fusion.1), channel_id=3, replica_groups=mesh['doc'=8,'ctx'=4] {'ctx'}, dimensions={0}, use_global_device_ids=true | all-gather | bytes 245760 | tf_op jit(solution)/shard_map/all_gather | solution.py:466
  53.7 0.7 pad_maximum_fusion
  54.4 7.4 %factors.1 = (bf16[128,5120]{1,0:T(8,128)(2,1)}, bf16[128,163840]{1,0:T(8,128)(2,1)}, s32[96,1]{1,0:T(8,128)}, s32[128,1]{1,0:T(8,128)}) custom-call(s32[1,1]{1,0:T(1,128)} %bitcast.me, bf16[8,24,512]{2,1,0:T(8,128)(2,1)} %bitcast.31, bf16[1,512,5120]{2,1,0:T(8,128)(2,1)} %heads_down.1, bf16[1,512,5120]{2,1,0:T(8,128)(2,1)} %heads_up.1), custom_call_target="tpu_custom_call" | custom-call | tf_op jit(solution)/shard_map/factors/pallas_call | solution.py:479
  61.9 0.0 copy-done.3
  61.9 1.3 copy-done.1
  63.2 1.2 copy-done.4
  64.4 0.8 copy-done.8
  65.2 0.7 coefficients.1.first_coeff
  65.9 7.2 %all-to-all-done.1 = bf16[32,8,2560]{2,1,0:T(8,128)(2,1)S(1)} async-done(((bf16[32,8,2560]{2,1,0:T(8,128)(2,1)}), bf16[32,8,2560]{2,1,0:T(8,128)(2,1)S(1)}, u32[]{:S(2)}, u32[]{:S(2)}) %all-to-all-start.1) | async-done | bytes 1310752 | tf_op jit(solution)/shard_map/all_to_all | solution.py:406
  73.1 0.0 copy-done.7
  73.1 3.2 %update.1 = bf16[256,4480]{1,0:T(8,128)(2,1)S(1)} custom-call(s32[1,1]{1,0:T(1,128)} %bitcast.me, s32[128,1]{1,0:T(8,128)S(1)} %copy-done.7, bf16[128,5120]{1,0:T(8,128)(2,1)S(1)} %copy-done.2, bf16[128,163840]{1,0:T(8,128)(2,1)} %get-tuple-element.17.up, bf16[96,128]{1,0:T(8,128)(2,1)S(1)} %coefficients.1.first_coeff, bf16[256,2560]{1,0:T(8,128)(2,1)S(1)} %bitcast.25), custom_call_target="tpu_custom_call" | custom-call | tf_op jit(solution)/shard_map/update/pallas_call | solution.py:503
  76.3 0.0 copy-start
  76.3 57.8 %all_to_all.15 = bf16[32,8,4480]{2,1,0:T(8,128)(2,1)S(1)} all-to-all(bf16[32,8,4480]{2,1,0:T(8,128)(2,1)S(1)} %bitcast.23), channel_id=1, replica_groups=mesh['doc'=8,'ctx'=4] {'doc','ctx'}, dimensions={0} | all-to-all | bytes 4587520 | tf_op jit(solution)/shard_map/all_to_all | solution.py:406
  134.1 0.0 copy-done
  134.1 2.6 %finish_rows.1 = bf16[192,5120]{1,0:T(8,128)(2,1)} custom-call(bf16[256,4480]{1,0:T(8,128)(2,1)S(1)} %bitcast.24, s32[1,192]{1,0:T(1,128)S(1)} %copy-done.10, bf16[192,5120]{1,0:T(8,128)(2,1)S(1)} %copy-done), custom_call_target="tpu_custom_call" | custom-call | tf_op jit(solution)/shard_map/finish_rows/pallas_call | solution.py:515
  (11 shorter events, 0.0 us)
Async XLA Ops:
  4.7 33.1 %all-to-all-start = ((bf16[32,8,1920]{2,1,0:T(8,128)(2,1)}), bf16[32,8,1920]{2,1,0:T(8,128)(2,1)S(1)}, u32[]{:S(2)}, u32[]{:S(2)}) async-start(bf16[32,8,1920]{2,1,0:T(8,128)(2,1)} %bitcast.30), calls=%async_computation | async-start | bytes 1966080 | tf_op jit(solution)/shard_map/all_to_all | solution.py:406
  12.0 14.6 %copy-start.5 = (bf16[512,512]{1,0:T(8,128)(2,1)S(1)}, bf16[512,512]{1,0:T(8,128)(2,1)}, u32[]{:S(2)}) copy-start(bf16[512,512]{1,0:T(8,128)(2,1)} %w_out.1) | copy-start | bytes 1572868
  12.0 14.6 %copy-start.6 = (f32[16,512]{1,0:T(8,128)S(1)}, f32[16,512]{1,0:T(8,128)}, u32[]{:S(2)}) copy-start(f32[16,512]{1,0:T(8,128)} %latents.3) | copy-start | bytes 98308
  12.0 14.6 %copy-start.9 = (f32[512]{0:T(512)S(1)}, f32[512]{0:T(512)}, u32[]{:S(2)}) copy-start(f32[512]{0:T(512)} %param.17) | copy-start | bytes 6148
  26.9 3.9 %collective-permute-start.1 = (bf16[24,512]{1,0:T(8,128)(2,1)S(1)}, bf16[24,512]{1,0:T(8,128)(2,1)S(1)}, u32[]{:S(2)}, u32[]{:S(2)}) collective-permute-start(bf16[24,512]{1,0:T(8,128)(2,1)S(1)} %summarize.1), channel_id=1, source_target_pairs={{0,4},{1,21},{2,14},{3,31},{4,0},{5,17},{6,10},{7,27},{8,12},{9,29... | collective-permute-start | bytes 73736 | tf_op jit(solution)/shard_map/ppermute | solution.py:464
  28.0 2.8 %collective-permute-start = (bf16[24,512]{1,0:T(8,128)(2,1)S(1)}, bf16[24,512]{1,0:T(8,128)(2,1)S(1)}, u32[]{:S(2)}, u32[]{:S(2)}) collective-permute-start(bf16[24,512]{1,0:T(8,128)(2,1)S(1)} %summarize.1), channel_id=1, source_target_pairs={{0,0},{1,17},{2,10},{3,27},{4,4},{5,21},{6,14},{7,31},{8,8},{9,25}... | collective-permute-start | bytes 73736 | tf_op jit(solution)/shard_map/ppermute | solution.py:464
  37.8 24.1 %copy-start.3 = (bf16[32,8,1920]{2,1,0:T(8,128)(2,1)}, bf16[32,8,1920]{2,1,0:T(8,128)(2,1)S(1)}, u32[]{:S(2)}) copy-start(bf16[32,8,1920]{2,1,0:T(8,128)(2,1)S(1)} %all-to-all-done) | copy-start | bytes 2949124
  37.8 35.3 %all-to-all-start.1 = ((bf16[32,8,2560]{2,1,0:T(8,128)(2,1)}), bf16[32,8,2560]{2,1,0:T(8,128)(2,1)S(1)}, u32[]{:S(2)}, u32[]{:S(2)}) async-start(bf16[32,8,2560]{2,1,0:T(8,128)(2,1)} %bitcast.29), calls=%async_computation.1 | async-start | bytes 2621440 | tf_op jit(solution)/shard_map/all_to_all | solution.py:406
  61.9 1.3 copy-start.1
  63.2 1.2 copy-start.4
  64.4 0.8 copy-start.8
  65.2 7.9 %copy-start.2 = (bf16[128,5120]{1,0:T(8,128)(2,1)S(1)}, bf16[128,5120]{1,0:T(8,128)(2,1)}, u32[]{:S(2)}) copy-start(bf16[128,5120]{1,0:T(8,128)(2,1)} %get-tuple-element.16.down) | copy-start | bytes 3932164
  65.2 7.9 %copy-start.7 = (s32[128,1]{1,0:T(8,128)S(1)}, s32[128,1]{1,0:T(8,128)}, u32[]{:S(2)}) copy-start(s32[128,1]{1,0:T(8,128)} %get-tuple-element.15.tags) | copy-start | bytes 1540
  76.3 57.8 %copy-start = (bf16[192,5120]{1,0:T(8,128)(2,1)S(1)}, bf16[192,5120]{1,0:T(8,128)(2,1)}, u32[]{:S(2)}) copy-start(bf16[192,5120]{1,0:T(8,128)(2,1)} %requests.3) | copy-start | bytes 5898244
  76.3 57.8 %copy-start.10 = (s32[1,192]{1,0:T(1,128)S(1)}, s32[1,192]{1,0:T(1,128)}, u32[]{:S(2)}) copy-start(s32[1,192]{1,0:T(1,128)} %get-tuple-element.22.slots) | copy-start | bytes 2308

commit v6 on v5

--- a/solution.py
+++ b/solution.py
@@ -81,10 +81,35 @@
 
 
 def place_kernel(
-    blocks, capacity, owner_row, module_row, doc_row, requests, first_sent, second_sent, tags, slots, stage
+    blocks,
+    capacity,
+    owners_outside,
+    modules_outside,
+    requests_outside,
+    sent,
+    slots,
+    owner_row,
+    module_row,
+    requests,
+    stage,
+    done,
 ):
     rows, width = requests.shape
     piece = width // SUB
+    copies = [
+        pltpu.make_async_copy(source, target, done.at[number])
+        for number, (source, target) in enumerate(
+            (
+                (owners_outside, owner_row),
+                (modules_outside, module_row),
+                (requests_outside, requests),
+            )
+        )
+    ]
+    for copy in copies:
+        copy.start()
+    copies[0].wait()
+    copies[1].wait()
     modules = module_row[...]
     owners = as_column(owner_row[...])
     named = lax.broadcasted_iota(jnp.int32, (blocks, rows), 0) == modules
@@ -95,15 +120,9 @@
     rank = jnp.sum(ahead.astype(jnp.int32), axis=0, keepdims=True)
     slot_row = rank * blocks + target
     slots[...] = slot_row
-    slot_column = as_column(slot_row)
-    documents = as_column(doc_row[...] + 1)
-    for part in range(tags.shape[0]):
-        lanes = lax.broadcasted_iota(jnp.int32, (rows, LANES), 1) + part * LANES
-        tags[part : part + 1, :] = jnp.sum(
-            jnp.where(lanes == slot_column, documents, 0), axis=0, keepdims=True
-        ).astype(jnp.float32)
     slot_ids = lax.broadcasted_iota(jnp.int32, (capacity * blocks, rows), 0)
     placer = (slot_ids == slot_row).astype(jnp.float32).astype(jnp.bfloat16)
+    copies[2].wait()
     for index in range(SUB):
         moved = jnp.dot(
             placer,
@@ -111,11 +130,38 @@
             preferred_element_type=jnp.float32,
         )
         scatter_pieces(stage, index, moved, blocks, capacity, piece)
-    drain_stage(stage, (first_sent, second_sent))
+    drain_stage(stage, (sent,))
+
+
+def place_more_kernel(blocks, start, capacity, slots, requests, sent, stage):
+    rows, width = requests.shape
+    piece = width // SUB
+    slot_ids = start * blocks + lax.broadcasted_iota(jnp.int32, (capacity * blocks, rows), 0)
+    placer = (slot_ids == slots[...]).astype(jnp.float32).astype(jnp.bfloat16)
+    for index in range(SUB):
+        moved = jnp.dot(
+            placer,
+            requests[:, index * piece : (index + 1) * piece],
+            preferred_element_type=jnp.float32,
+        )
+        scatter_pieces(stage, index, moved, blocks, capacity, piece)
+    drain_stage(stage, (sent,))
 
 
 def attend_kernel(
-    chunks, tokens, w_keys, w_values, latents, tags, partial, tokens_in, keys_in, values_in, done
+    chunks,
+    tag_parts,
+    tokens,
+    w_keys,
+    w_values,
+    latents,
+    slots,
+    doc_row,
+    partial,
+    tokens_in,
+    keys_in,
+    values_in,
+    done,
 ):
     depth = w_keys.shape[0] // chunks
     copies = []
@@ -171,7 +217,13 @@
     partial[entries:, :] = jnp.zeros_like(partial[entries:, :])
     partial[entries : entries + 1, :entries] = as_row(jnp.concatenate(peaks, axis=0))
     partial[entries + 1 : entries + 2, :entries] = as_row(jnp.concatenate(sums, axis=0))
-    partial[entries + 2 : entries + 2 + tags.shape[0], :] = tags[...]
+    slot_column = as_column(slots[...])
+    documents = as_column(doc_row[...] + 1)
+    for part in range(tag_parts):
+        lanes = lax.broadcasted_iota(jnp.int32, (slot_column.shape[0], LANES), 1) + part * LANES
+        partial[entries + 2 + part : entries + 3 + part, :] = jnp.sum(
+            jnp.where(lanes == slot_column, documents, 0), axis=0, keepdims=True
+        ).astype(jnp.float32)
 
 
 def summary_kernel(tag_parts, pieces, latents, w_out, gain, packet):
@@ -407,21 +459,25 @@
             values.reshape(blocks, SUB, -1), ALL, split_axis=0, concat_axis=0, tiled=True
         ).reshape(values.shape)
 
-    first_sent, second_sent, tags, slots = call(
-        functools.partial(place_kernel, blocks, capacity),
+    first_sent, slots = call(
+        functools.partial(place_kernel, blocks, early),
         "place_rows",
         vmem=60,
+        in_specs=[outside] * 3,
         out_shape=(
             block_type(early),
-            block_type(late),
-            jax.ShapeDtypeStruct((tag_parts, LANES), jnp.float32),
             jax.ShapeDtypeStruct((1, rows), jnp.int32),
         ),
-        scratch_shapes=[stage_type(capacity)],
+        scratch_shapes=[
+            pltpu.VMEM((1, blocks), jnp.int32),
+            pltpu.VMEM((1, rows), jnp.int32),
+            pltpu.VMEM((rows, width), jnp.bfloat16),
+            stage_type(early),
+            pltpu.SemaphoreType.DMA((3,)),
+        ],
     )(
         owner.reshape(1, blocks),
         req_module.reshape(1, rows),
-        req_doc.reshape(1, rows),
         requests,
     )
     first_arrived = exchange(first_sent)
@@ -432,10 +488,10 @@
     chunks = width // (SUB * LANES)
     depth = width // chunks
     partial = call(
-        functools.partial(attend_kernel, chunks),
+        functools.partial(attend_kernel, chunks, tag_parts),
         "attend",
         vmem=60,
-        in_specs=[in_hbm] * 3 + [in_vmem] * 2,
+        in_specs=[in_hbm] * 3 + [in_vmem] * 3,
         out_shape=jax.ShapeDtypeStruct((partial_rows, head_dim), jnp.float32),
         scratch_shapes=[
             pltpu.VMEM((chunks, token_count, depth), jnp.bfloat16),
@@ -443,7 +499,7 @@
             pltpu.VMEM((chunks, depth, latent_width), jnp.bfloat16),
             pltpu.SemaphoreType.DMA((chunks, 3)),
         ],
-    )(tokens, w_keys, w_values, latents, tags)
+    )(tokens, w_keys, w_values, latents, slots, req_doc.reshape(1, rows))
     packet_rows = latent_count + -(-ctx_count // SUB) * SUB
     packet = call(
         functools.partial(summary_kernel, tag_parts),
@@ -462,6 +518,13 @@
             for ctx in range(ctx_count)
         ]
         fetched.append(lax.ppermute(packet, ALL, pairs))
+    second_sent = call(
+        functools.partial(place_more_kernel, blocks, early, late),
+        "place_more",
+        vmem=60,
+        out_shape=block_type(late),
+        scratch_shapes=[stage_type(late)],
+    )(after(slots, packet), requests)
     second_arrived = exchange(after(second_sent, *fetched))
     gathered = lax.all_gather(jnp.stack(fetched), "ctx")
     everyone = jnp.stack([gathered[order.index(part)] for part in range(ctx_count)]).reshape(

time: 137 us -> 136 us (level)
  waiting for transfers between devices: 16.3 us -> 12.6 us
  Pallas kernels: 27 us -> 29.5 us
    pallas_call x2 -> x3, Pallas kernels: 12.8 us -> 15.2 us  [the longest x1 8.19 us: on_device(): call(functools.partial(attend_kernel, chunks, tag_parts), 'attend', vmem=...]
    ppermute x2, waiting for transfers between devices: 2.16 us -> 0.01 us  [on_device(): fetched.append(lax.ppermute(packet, ALL, pairs))]
    all_to_all x2, waiting for transfers between devices: 14.2 us -> 12.6 us  [exchange(): lax.all_to_all(values.reshape(blocks, SUB, -1), ALL, split_axis=0, concat...]
  transfers between devices with their start and end apart: 4 -> 4, of which waited for: 3 -> 2; matrix products, arithmetic and copies ran while one was open for 1% -> 1% of each run, Pallas kernels for 12% -> 15%
where the time goes in v6:
time: 136 us
  blocking collectives  76.9 us (57%)
  Pallas kernels  29.5 us (22%)
  waiting for transfers between devices  12.6 us (9%)
  starting transfers between devices  12.4 us (9%)
  local copies, waits for them, and re-layouts  3.36 us (2%)
    all_to_all x1, blocking collectives, exchange(): lax.all_to_all(values.reshape(blocks, SUB, -1), ALL, split_axis=0, concat...  57.8 us
    all_gather x1, blocking collectives, on_device(): gathered = lax.all_gather(jnp.stack(fetched), 'ctx')  12.7 us
    all_to_all x2, waiting for transfers between devices, exchange(): lax.all_to_all(values.reshape(blocks, SUB, -1), ALL, split_axis=0, concat...  12.6 us
    all_to_all x2, starting transfers between devices, exchange(): lax.all_to_all(values.reshape(blocks, SUB, -1), ALL, split_axis=0, concat...  10.7 us
    pallas_call x1, Pallas kernels, on_device(): call(functools.partial(attend_kernel, chunks, tag_parts), 'attend', vmem=...  8.19 us
    pallas_call x1, Pallas kernels, on_device(): call(functools.partial(factor_kernel, blocks, capacity, early, latent_cou...  7.45 us
    all_gather x1, blocking collectives, on_device(): lax.all_gather(partial, 'ctx')  6.37 us
    pallas_call x1, Pallas kernels, on_device(): call(functools.partial(place_more_kernel, blocks, early, late), 'place_mo...  3.64 us
  transfers between devices with their start and end apart: 4, of which 2 were waited for; matrix products, arithmetic and copies ran while one was open for 1% of the time, Pallas kernels for 15%

profile of v6, /device:TPU:0, one launch (start us, length us, event | category | flops | bytes accessed | tf_op | source)
XLA Modules:
  0.0 135.6 jit_solution(470004231252122196)
XLA Ops:
  0.0 3.4 %place_rows.1 = (bf16[256,1920]{1,0:T(8,128)(2,1)}, s32[1,192]{1,0:T(1,128)}) custom-call(s32[1,32]{1,0:T(1,128)} %bitcast.36, s32[1,192]{1,0:T(1,128)} %bitcast.34, bf16[192,5120]{1,0:T(8,128)(2,1)} %requests.3), custom_call_target="tpu_custom_call" | custom-call | tf_op jit(solution)/shard_map/place_rows/pallas_call | solution.py:462
  3.4 7.3 %all-to-all-start = ((bf16[32,8,1920]{2,1,0:T(8,128)(2,1)}), bf16[32,8,1920]{2,1,0:T(8,128)(2,1)S(1)}, u32[]{:S(2)}, u32[]{:S(2)}) async-start(bf16[32,8,1920]{2,1,0:T(8,128)(2,1)} %bitcast.30), calls=%async_computation | async-start | bytes 1966080 | tf_op jit(solution)/shard_map/all_to_all | solution.py:458
  10.7 0.0 copy-start.5
  10.7 0.0 copy-start.6
  10.7 0.0 copy-start.10
  10.7 8.2 %attend.1 = f32[72,128]{1,0:T(8,128)} custom-call(bf16[1,256,5120]{2,1,0:T(8,128)(2,1)} %tokens.1, bf16[5120,512]{1,0:T(8,128)(2,1)} %w_keys.1, bf16[5120,512]{1,0:T(8,128)(2,1)} %w_values.1, f32[16,512]{1,0:T(8,128)} %latents.3, s32[1,192]{1,0:T(1,128)} %get-tuple-element.19.slots, s32[1,192]{1,0:T(1,128)} %bitcast.35), custom_call_target="tpu_custom_call" | custom-call | tf_op jit(solution)/shard_map/attend/pallas_call | solution.py:490
  18.9 6.4 %all-gather = f32[288,128]{1,0:T(8,128)S(1)} all-gather(f32[72,128]{1,0:T(8,128)} %attend.1), channel_id=2, replica_groups=mesh['doc'=8,'ctx'=4] {'ctx'}, dimensions={0}, use_global_device_ids=true | all-gather | bytes 184320 | tf_op jit(solution)/shard_map/all_gather | solution.py:508
  25.3 0.0 copy-done.5
  25.3 0.0 copy-done.6
  25.3 0.0 copy-done.10
  25.3 0.4 summarize.1
  25.6 1.1 collective-permute-start.1
  26.8 0.7 collective-permute-start
  27.4 3.6 %place_more.1 = bf16[256,2560]{1,0:T(8,128)(2,1)} custom-call(s32[1,192]{1,0:T(1,128)} %get-tuple-element.19.slots, bf16[192,5120]{1,0:T(8,128)(2,1)} %requests.3), custom_call_target="tpu_custom_call" | custom-call | tf_op jit(solution)/shard_map/place_more/pallas_call | solution.py:521
  31.1 0.0 collective-permute-done.1
  31.1 0.0 collective-permute-done
  31.1 5.4 %all-to-all-done = bf16[32,8,1920]{2,1,0:T(8,128)(2,1)S(1)} async-done(((bf16[32,8,1920]{2,1,0:T(8,128)(2,1)}), bf16[32,8,1920]{2,1,0:T(8,128)(2,1)S(1)}, u32[]{:S(2)}, u32[]{:S(2)}) %all-to-all-start) | async-done | bytes 983072 | tf_op jit(solution)/shard_map/all_to_all | solution.py:458
  36.5 3.4 %all-to-all-start.1 = ((bf16[32,8,2560]{2,1,0:T(8,128)(2,1)}), bf16[32,8,2560]{2,1,0:T(8,128)(2,1)S(1)}, u32[]{:S(2)}, u32[]{:S(2)}) async-start(bf16[32,8,2560]{2,1,0:T(8,128)(2,1)} %bitcast.29), calls=%async_computation.1 | async-start | bytes 2621440 | tf_op jit(solution)/shard_map/all_to_all | solution.py:458
  39.9 12.7 %all-gather.1 = bf16[8,24,512]{2,1,0:T(8,128)(2,1)S(1)} all-gather(bf16[2,24,512]{2,1,0:T(8,128)(2,1)S(1)} %pad_maximum_fusion.1), channel_id=3, replica_groups=mesh['doc'=8,'ctx'=4] {'ctx'}, dimensions={0}, use_global_device_ids=true | all-gather | bytes 245760 | tf_op jit(solution)/shard_map/all_gather | solution.py:529
  52.6 0.7 pad_maximum_fusion
  53.3 7.4 %factors.1 = (bf16[128,5120]{1,0:T(8,128)(2,1)}, bf16[128,163840]{1,0:T(8,128)(2,1)}, s32[96,1]{1,0:T(8,128)}, s32[128,1]{1,0:T(8,128)}) custom-call(s32[1,1]{1,0:T(1,128)} %bitcast.me, bf16[8,24,512]{2,1,0:T(8,128)(2,1)} %bitcast.31, bf16[1,512,5120]{2,1,0:T(8,128)(2,1)} %heads_down.1, bf16[1,512,5120]{2,1,0:T(8,128)(2,1)} %heads_up.1), custom_call_target="tpu_custom_call" | custom-call | tf_op jit(solution)/shard_map/factors/pallas_call | solution.py:542
  60.8 0.0 copy-start.1
  60.8 1.3 copy-done.1
  62.1 1.2 copy-done.4
  63.3 0.8 copy-done.8
  64.1 0.7 coefficients.1.first_coeff
  64.8 7.2 %all-to-all-done.1 = bf16[32,8,2560]{2,1,0:T(8,128)(2,1)S(1)} async-done(((bf16[32,8,2560]{2,1,0:T(8,128)(2,1)}), bf16[32,8,2560]{2,1,0:T(8,128)(2,1)S(1)}, u32[]{:S(2)}, u32[]{:S(2)}) %all-to-all-start.1) | async-done | bytes 1310752 | tf_op jit(solution)/shard_map/all_to_all | solution.py:458
  72.0 3.2 %update.1 = bf16[256,4480]{1,0:T(8,128)(2,1)S(1)} custom-call(s32[1,1]{1,0:T(1,128)} %bitcast.me, s32[128,1]{1,0:T(8,128)S(1)} %copy-done.7, bf16[128,5120]{1,0:T(8,128)(2,1)S(1)} %copy-done.2, bf16[128,163840]{1,0:T(8,128)(2,1)} %get-tuple-element.16.up, bf16[96,128]{1,0:T(8,128)(2,1)S(1)} %coefficients.1.first_coeff, bf16[256,2560]{1,0:T(8,128)(2,1)S(1)} %bitcast.25), custom_call_target="tpu_custom_call" | custom-call | tf_op jit(solution)/shard_map/update/pallas_call | solution.py:566
  75.2 0.0 copy-start
  75.2 57.8 %all_to_all.15 = bf16[32,8,4480]{2,1,0:T(8,128)(2,1)S(1)} all-to-all(bf16[32,8,4480]{2,1,0:T(8,128)(2,1)S(1)} %bitcast.23), channel_id=1, replica_groups=mesh['doc'=8,'ctx'=4] {'doc','ctx'}, dimensions={0} | all-to-all | bytes 4587520 | tf_op jit(solution)/shard_map/all_to_all | solution.py:458
  133.0 0.0 copy-done
  133.0 2.6 %finish_rows.1 = bf16[192,5120]{1,0:T(8,128)(2,1)} custom-call(bf16[256,4480]{1,0:T(8,128)(2,1)S(1)} %bitcast.24, s32[1,192]{1,0:T(1,128)S(1)} %copy-done.9, bf16[192,5120]{1,0:T(8,128)(2,1)S(1)} %copy-done), custom_call_target="tpu_custom_call" | custom-call | tf_op jit(solution)/shard_map/finish_rows/pallas_call | solution.py:578
  (12 shorter events, 0.0 us)
Async XLA Ops:
  3.4 33.1 %all-to-all-start = ((bf16[32,8,1920]{2,1,0:T(8,128)(2,1)}), bf16[32,8,1920]{2,1,0:T(8,128)(2,1)S(1)}, u32[]{:S(2)}, u32[]{:S(2)}) async-start(bf16[32,8,1920]{2,1,0:T(8,128)(2,1)} %bitcast.30), calls=%async_computation | async-start | bytes 1966080 | tf_op jit(solution)/shard_map/all_to_all | solution.py:458
  10.7 14.6 %copy-start.5 = (bf16[512,512]{1,0:T(8,128)(2,1)S(1)}, bf16[512,512]{1,0:T(8,128)(2,1)}, u32[]{:S(2)}) copy-start(bf16[512,512]{1,0:T(8,128)(2,1)} %w_out.1) | copy-start | bytes 1572868
  10.7 14.6 %copy-start.6 = (f32[16,512]{1,0:T(8,128)S(1)}, f32[16,512]{1,0:T(8,128)}, u32[]{:S(2)}) copy-start(f32[16,512]{1,0:T(8,128)} %latents.3) | copy-start | bytes 98308
  10.7 14.6 %copy-start.10 = (f32[512]{0:T(512)S(1)}, f32[512]{0:T(512)}, u32[]{:S(2)}) copy-start(f32[512]{0:T(512)} %param.17) | copy-start | bytes 6148
  25.6 5.4 %collective-permute-start.1 = (bf16[24,512]{1,0:T(8,128)(2,1)S(1)}, bf16[24,512]{1,0:T(8,128)(2,1)S(1)}, u32[]{:S(2)}, u32[]{:S(2)}) collective-permute-start(bf16[24,512]{1,0:T(8,128)(2,1)S(1)} %summarize.1), channel_id=1, source_target_pairs={{0,4},{1,21},{2,14},{3,31},{4,0},{5,17},{6,10},{7,27},{8,12},{9,29... | collective-permute-start | bytes 73736 | tf_op jit(solution)/shard_map/ppermute | solution.py:520
  26.8 4.3 %collective-permute-start = (bf16[24,512]{1,0:T(8,128)(2,1)S(1)}, bf16[24,512]{1,0:T(8,128)(2,1)S(1)}, u32[]{:S(2)}, u32[]{:S(2)}) collective-permute-start(bf16[24,512]{1,0:T(8,128)(2,1)S(1)} %summarize.1), channel_id=1, source_target_pairs={{0,0},{1,17},{2,10},{3,27},{4,4},{5,21},{6,14},{7,31},{8,8},{9,25}... | collective-permute-start | bytes 73736 | tf_op jit(solution)/shard_map/ppermute | solution.py:520
  36.5 24.3 %copy-start.3 = (bf16[32,8,1920]{2,1,0:T(8,128)(2,1)}, bf16[32,8,1920]{2,1,0:T(8,128)(2,1)S(1)}, u32[]{:S(2)}) copy-start(bf16[32,8,1920]{2,1,0:T(8,128)(2,1)S(1)} %all-to-all-done) | copy-start | bytes 2949124
  36.5 35.5 %all-to-all-start.1 = ((bf16[32,8,2560]{2,1,0:T(8,128)(2,1)}), bf16[32,8,2560]{2,1,0:T(8,128)(2,1)S(1)}, u32[]{:S(2)}, u32[]{:S(2)}) async-start(bf16[32,8,2560]{2,1,0:T(8,128)(2,1)} %bitcast.29), calls=%async_computation.1 | async-start | bytes 2621440 | tf_op jit(solution)/shard_map/all_to_all | solution.py:458
  60.8 1.3 copy-start.1
  62.1 1.2 copy-start.4
  63.3 0.8 copy-start.8
  64.1 7.9 %copy-start.2 = (bf16[128,5120]{1,0:T(8,128)(2,1)S(1)}, bf16[128,5120]{1,0:T(8,128)(2,1)}, u32[]{:S(2)}) copy-start(bf16[128,5120]{1,0:T(8,128)(2,1)} %get-tuple-element.15.down) | copy-start | bytes 3932164
  64.1 7.9 %copy-start.7 = (s32[128,1]{1,0:T(8,128)S(1)}, s32[128,1]{1,0:T(8,128)}, u32[]{:S(2)}) copy-start(s32[128,1]{1,0:T(8,128)} %get-tuple-element.14.tags) | copy-start | bytes 1540
  75.2 57.8 %copy-start = (bf16[192,5120]{1,0:T(8,128)(2,1)S(1)}, bf16[192,5120]{1,0:T(8,128)(2,1)}, u32[]{:S(2)}) copy-start(bf16[192,5120]{1,0:T(8,128)(2,1)} %requests.3) | copy-start | bytes 5898244
  75.2 57.8 %copy-start.9 = (s32[1,192]{1,0:T(1,128)S(1)}, s32[1,192]{1,0:T(1,128)}, u32[]{:S(2)}) copy-start(s32[1,192]{1,0:T(1,128)} %get-tuple-element.19.slots) | copy-start | bytes 2308

commit v7 on v6

--- a/solution.py
+++ b/solution.py
@@ -307,10 +307,7 @@
     device = me[0, 0]
     my_doc = device // members
     by_entry = jnp.concatenate(
-        [
-            everyone[x, latent_count : latent_count + members, :].astype(jnp.float32)
-            for x in range(documents)
-        ],
+        [everyone[x, latent_count:, :].astype(jnp.float32)[:members] for x in range(documents)],
         axis=0,
     ).astype(jnp.bfloat16)
     source = lax.broadcasted_iota(jnp.int32, (blocks, blocks), 0)
@@ -500,7 +497,7 @@
             pltpu.SemaphoreType.DMA((chunks, 3)),
         ],
     )(tokens, w_keys, w_values, latents, slots, req_doc.reshape(1, rows))
-    packet_rows = latent_count + -(-ctx_count // SUB) * SUB
+    packet_rows = latent_count + -(-ctx_count // 16) * 16
     packet = call(
         functools.partial(summary_kernel, tag_parts),
         "summarize",

time: 136 us -> 136 us (level)
  no operation moved by 1% of the time
where the time goes in v7:
time: 136 us
  blocking collectives  77.5 us (57%)
  Pallas kernels  29.5 us (22%)
  starting transfers between devices  12.3 us (9%)
  waiting for transfers between devices  12.2 us (9%)
  local copies, waits for them, and re-layouts  3.37 us (2%)
    all_to_all x1, blocking collectives, exchange(): lax.all_to_all(values.reshape(blocks, SUB, -1), ALL, split_axis=0, concat...  57.8 us
    all_gather x1, blocking collectives, on_device(): gathered = lax.all_gather(jnp.stack(fetched), 'ctx')  13.3 us
    all_to_all x2, waiting for transfers between devices, exchange(): lax.all_to_all(values.reshape(blocks, SUB, -1), ALL, split_axis=0, concat...  12.2 us
    all_to_all x2, starting transfers between devices, exchange(): lax.all_to_all(values.reshape(blocks, SUB, -1), ALL, split_axis=0, concat...  10.5 us
    pallas_call x1, Pallas kernels, on_device(): call(functools.partial(attend_kernel, chunks, tag_parts), 'attend', vmem=...  8.19 us
    pallas_call x1, Pallas kernels, on_device(): call(functools.partial(factor_kernel, blocks, capacity, early, latent_cou...  7.43 us
    all_gather x1, blocking collectives, on_device(): lax.all_gather(partial, 'ctx')  6.37 us
    pallas_call x1, Pallas kernels, on_device(): call(functools.partial(place_more_kernel, blocks, early, late), 'place_mo...  3.64 us
  transfers between devices with their start and end apart: 4, of which 2 were waited for; matrix products, arithmetic and copies ran while one was open for 1% of the time, Pallas kernels for 15%

profile of v7, /device:TPU:0, one launch (start us, length us, event | category | flops | bytes accessed | tf_op | source)
XLA Modules:
  0.0 135.7 jit_solution(5505409673795782647)
XLA Ops:
  0.0 3.4 %place_rows.1 = (bf16[256,1920]{1,0:T(8,128)(2,1)}, s32[1,192]{1,0:T(1,128)}) custom-call(s32[1,32]{1,0:T(1,128)} %bitcast.36, s32[1,192]{1,0:T(1,128)} %bitcast.34, bf16[192,5120]{1,0:T(8,128)(2,1)} %requests.3), custom_call_target="tpu_custom_call" | custom-call | tf_op jit(solution)/shard_map/place_rows/pallas_call | solution.py:459
  3.4 7.3 %all-to-all-start = ((bf16[32,8,1920]{2,1,0:T(8,128)(2,1)}), bf16[32,8,1920]{2,1,0:T(8,128)(2,1)S(1)}, u32[]{:S(2)}, u32[]{:S(2)}) async-start(bf16[32,8,1920]{2,1,0:T(8,128)(2,1)} %bitcast.31), calls=%async_computation | async-start | bytes 1966080 | tf_op jit(solution)/shard_map/all_to_all | solution.py:455
  10.7 0.0 copy-start.5
  10.7 0.0 copy-start.6
  10.7 0.0 copy-start.10
  10.7 8.2 %attend.1 = f32[72,128]{1,0:T(8,128)} custom-call(bf16[1,256,5120]{2,1,0:T(8,128)(2,1)} %tokens.1, bf16[5120,512]{1,0:T(8,128)(2,1)} %w_keys.1, bf16[5120,512]{1,0:T(8,128)(2,1)} %w_values.1, f32[16,512]{1,0:T(8,128)} %latents.3, s32[1,192]{1,0:T(1,128)} %get-tuple-element.19.slots, s32[1,192]{1,0:T(1,128)} %bitcast.35), custom_call_target="tpu_custom_call" | custom-call | tf_op jit(solution)/shard_map/attend/pallas_call | solution.py:487
  18.9 6.4 %all-gather = f32[288,128]{1,0:T(8,128)S(1)} all-gather(f32[72,128]{1,0:T(8,128)} %attend.1), channel_id=2, replica_groups=mesh['doc'=8,'ctx'=4] {'ctx'}, dimensions={0}, use_global_device_ids=true | all-gather | bytes 184320 | tf_op jit(solution)/shard_map/all_gather | solution.py:505
  25.3 0.0 copy-done.5
  25.3 0.0 copy-done.6
  25.3 0.4 summarize.1
  25.6 1.1 collective-permute-start.1
  26.8 0.7 collective-permute-start
  27.4 3.6 %place_more.1 = bf16[256,2560]{1,0:T(8,128)(2,1)} custom-call(s32[1,192]{1,0:T(1,128)} %get-tuple-element.19.slots, bf16[192,5120]{1,0:T(8,128)(2,1)} %requests.3), custom_call_target="tpu_custom_call" | custom-call | tf_op jit(solution)/shard_map/place_more/pallas_call | solution.py:518
  31.1 0.0 collective-permute-done.1
  31.1 0.0 collective-permute-done
  31.1 5.6 %all-to-all-done = bf16[32,8,1920]{2,1,0:T(8,128)(2,1)S(1)} async-done(((bf16[32,8,1920]{2,1,0:T(8,128)(2,1)}), bf16[32,8,1920]{2,1,0:T(8,128)(2,1)S(1)}, u32[]{:S(2)}, u32[]{:S(2)}) %all-to-all-start) | async-done | bytes 983072 | tf_op jit(solution)/shard_map/all_to_all | solution.py:455
  36.7 3.2 %all-to-all-start.1 = ((bf16[32,8,2560]{2,1,0:T(8,128)(2,1)}), bf16[32,8,2560]{2,1,0:T(8,128)(2,1)S(1)}, u32[]{:S(2)}, u32[]{:S(2)}) async-start(bf16[32,8,2560]{2,1,0:T(8,128)(2,1)} %bitcast.29), calls=%async_computation.1 | async-start | bytes 2621440 | tf_op jit(solution)/shard_map/all_to_all | solution.py:455
  40.0 13.3 %all-gather.1 = bf16[8,32,512]{2,1,0:T(8,128)(2,1)S(1)} all-gather(bf16[2,32,512]{2,1,0:T(8,128)(2,1)S(1)} %pad_maximum_fusion.1), channel_id=3, replica_groups=mesh['doc'=8,'ctx'=4] {'ctx'}, dimensions={0}, use_global_device_ids=true | all-gather | bytes 327680 | tf_op jit(solution)/shard_map/all_gather | solution.py:526
  53.3 0.7 pad_maximum_fusion
  54.0 7.4 %factors.1 = (bf16[128,5120]{1,0:T(8,128)(2,1)}, bf16[128,163840]{1,0:T(8,128)(2,1)}, s32[96,1]{1,0:T(8,128)}, s32[128,1]{1,0:T(8,128)}) custom-call(s32[1,1]{1,0:T(1,128)} %bitcast.me, bf16[8,32,512]{2,1,0:T(8,128)(2,1)} %bitcast.30, bf16[1,512,5120]{2,1,0:T(8,128)(2,1)} %heads_down.1, bf16[1,512,5120]{2,1,0:T(8,128)(2,1)} %heads_up.1), custom_call_target="tpu_custom_call" | custom-call | tf_op jit(solution)/shard_map/factors/pallas_call | solution.py:539
  61.5 0.0 copy-start.1
  61.5 1.3 copy-done.1
  62.8 1.2 copy-done.4
  64.0 0.8 copy-done.8
  64.8 0.7 coefficients.1.first_coeff
  65.5 6.6 %all-to-all-done.1 = bf16[32,8,2560]{2,1,0:T(8,128)(2,1)S(1)} async-done(((bf16[32,8,2560]{2,1,0:T(8,128)(2,1)}), bf16[32,8,2560]{2,1,0:T(8,128)(2,1)S(1)}, u32[]{:S(2)}, u32[]{:S(2)}) %all-to-all-start.1) | async-done | bytes 1310752 | tf_op jit(solution)/shard_map/all_to_all | solution.py:455
  72.1 0.0 copy-done.7
  72.1 3.2 %update.1 = bf16[256,4480]{1,0:T(8,128)(2,1)S(1)} custom-call(s32[1,1]{1,0:T(1,128)} %bitcast.me, s32[128,1]{1,0:T(8,128)S(1)} %copy-done.7, bf16[128,5120]{1,0:T(8,128)(2,1)S(1)} %copy-done.2, bf16[128,163840]{1,0:T(8,128)(2,1)} %get-tuple-element.16.up, bf16[96,128]{1,0:T(8,128)(2,1)S(1)} %coefficients.1.first_coeff, bf16[256,2560]{1,0:T(8,128)(2,1)S(1)} %bitcast.25), custom_call_target="tpu_custom_call" | custom-call | tf_op jit(solution)/shard_map/update/pallas_call | solution.py:563
  75.2 0.0 copy-start
  75.3 57.8 %all_to_all.15 = bf16[32,8,4480]{2,1,0:T(8,128)(2,1)S(1)} all-to-all(bf16[32,8,4480]{2,1,0:T(8,128)(2,1)S(1)} %bitcast.23), channel_id=1, replica_groups=mesh['doc'=8,'ctx'=4] {'doc','ctx'}, dimensions={0} | all-to-all | bytes 4587520 | tf_op jit(solution)/shard_map/all_to_all | solution.py:455
  133.1 0.0 copy-done.9
  133.1 2.6 %finish_rows.1 = bf16[192,5120]{1,0:T(8,128)(2,1)} custom-call(bf16[256,4480]{1,0:T(8,128)(2,1)S(1)} %bitcast.24, s32[1,192]{1,0:T(1,128)S(1)} %copy-done.9, bf16[192,5120]{1,0:T(8,128)(2,1)S(1)} %copy-done), custom_call_target="tpu_custom_call" | custom-call | tf_op jit(solution)/shard_map/finish_rows/pallas_call | solution.py:575
  (12 shorter events, 0.0 us)
Async XLA Ops:
  3.4 33.3 %all-to-all-start = ((bf16[32,8,1920]{2,1,0:T(8,128)(2,1)}), bf16[32,8,1920]{2,1,0:T(8,128)(2,1)S(1)}, u32[]{:S(2)}, u32[]{:S(2)}) async-start(bf16[32,8,1920]{2,1,0:T(8,128)(2,1)} %bitcast.31), calls=%async_computation | async-start | bytes 1966080 | tf_op jit(solution)/shard_map/all_to_all | solution.py:455
  10.7 14.6 %copy-start.5 = (bf16[512,512]{1,0:T(8,128)(2,1)S(1)}, bf16[512,512]{1,0:T(8,128)(2,1)}, u32[]{:S(2)}) copy-start(bf16[512,512]{1,0:T(8,128)(2,1)} %w_out.1) | copy-start | bytes 1572868
  10.7 14.6 %copy-start.6 = (f32[16,512]{1,0:T(8,128)S(1)}, f32[16,512]{1,0:T(8,128)}, u32[]{:S(2)}) copy-start(f32[16,512]{1,0:T(8,128)} %latents.3) | copy-start | bytes 98308
  10.7 14.6 %copy-start.10 = (f32[512]{0:T(512)S(1)}, f32[512]{0:T(512)}, u32[]{:S(2)}) copy-start(f32[512]{0:T(512)} %param.17) | copy-start | bytes 6148
  25.6 5.4 %collective-permute-start.1 = (bf16[32,512]{1,0:T(8,128)(2,1)S(1)}, bf16[32,512]{1,0:T(8,128)(2,1)S(1)}, u32[]{:S(2)}, u32[]{:S(2)}) collective-permute-start(bf16[32,512]{1,0:T(8,128)(2,1)S(1)} %summarize.1), channel_id=1, source_target_pairs={{0,4},{1,21},{2,14},{3,31},{4,0},{5,17},{6,10},{7,27},{8,12},{9,29... | collective-permute-start | bytes 98312 | tf_op jit(solution)/shard_map/ppermute | solution.py:517
  26.8 4.3 %collective-permute-start = (bf16[32,512]{1,0:T(8,128)(2,1)S(1)}, bf16[32,512]{1,0:T(8,128)(2,1)S(1)}, u32[]{:S(2)}, u32[]{:S(2)}) collective-permute-start(bf16[32,512]{1,0:T(8,128)(2,1)S(1)} %summarize.1), channel_id=1, source_target_pairs={{0,0},{1,17},{2,10},{3,27},{4,4},{5,21},{6,14},{7,31},{8,8},{9,25}... | collective-permute-start | bytes 98312 | tf_op jit(solution)/shard_map/ppermute | solution.py:517
  36.7 24.8 %copy-start.3 = (bf16[32,8,1920]{2,1,0:T(8,128)(2,1)}, bf16[32,8,1920]{2,1,0:T(8,128)(2,1)S(1)}, u32[]{:S(2)}) copy-start(bf16[32,8,1920]{2,1,0:T(8,128)(2,1)S(1)} %all-to-all-done) | copy-start | bytes 2949124
  36.7 35.4 %all-to-all-start.1 = ((bf16[32,8,2560]{2,1,0:T(8,128)(2,1)}), bf16[32,8,2560]{2,1,0:T(8,128)(2,1)S(1)}, u32[]{:S(2)}, u32[]{:S(2)}) async-start(bf16[32,8,2560]{2,1,0:T(8,128)(2,1)} %bitcast.29), calls=%async_computation.1 | async-start | bytes 2621440 | tf_op jit(solution)/shard_map/all_to_all | solution.py:455
  61.5 1.3 copy-start.1
  62.8 1.2 copy-start.4
  64.0 0.8 copy-start.8
  64.8 7.3 %copy-start.2 = (bf16[128,5120]{1,0:T(8,128)(2,1)S(1)}, bf16[128,5120]{1,0:T(8,128)(2,1)}, u32[]{:S(2)}) copy-start(bf16[128,5120]{1,0:T(8,128)(2,1)} %get-tuple-element.15.down) | copy-start | bytes 3932164
  64.8 7.3 %copy-start.7 = (s32[128,1]{1,0:T(8,128)S(1)}, s32[128,1]{1,0:T(8,128)}, u32[]{:S(2)}) copy-start(s32[128,1]{1,0:T(8,128)} %get-tuple-element.14.tags) | copy-start | bytes 1540
  75.2 57.8 %copy-start = (bf16[192,5120]{1,0:T(8,128)(2,1)S(1)}, bf16[192,5120]{1,0:T(8,128)(2,1)}, u32[]{:S(2)}) copy-start(bf16[192,5120]{1,0:T(8,128)(2,1)} %requests.3) | copy-start | bytes 5898244
  75.2 57.8 %copy-start.9 = (s32[1,192]{1,0:T(1,128)S(1)}, s32[1,192]{1,0:T(1,128)}, u32[]{:S(2)}) copy-start(s32[1,192]{1,0:T(1,128)} %get-tuple-element.19.slots) | copy-start | bytes 2308

commit v8 on v7

--- a/solution.py
+++ b/solution.py
@@ -11,6 +11,7 @@
 HEADS = 4
 SUB = 8
 LANES = 128
+CHUNKS = 4
 LONG = 20 * 1024 * 1024
 ALL = ("doc", "ctx")
 
@@ -367,14 +368,24 @@
     update, stage, up_in, up_done = refs
     piece = down.shape[1] // SUB
     late = arrived.shape[1] // piece
-    up_copy = pltpu.make_async_copy(up.at[:, pl.ds(0, down.shape[1])], up_in, up_done)
-    up_copy.start()
+    span = down.shape[1] // CHUNKS
+    up_copies = [
+        pltpu.make_async_copy(
+            up.at[:, pl.ds(chunk * span, span)],
+            up_in.at[:, pl.ds(chunk * span, span)],
+            up_done.at[chunk],
+        )
+        for chunk in range(CHUNKS)
+    ]
+    for copy in up_copies:
+        copy.start()
     coeff = coefficients(
         blocks, late, latent_count, members, me, tags, down, arrived, stage
     )
     coeff = jnp.concatenate([first_coeff[...], coeff], axis=0)
-    up_copy.wait()
     for index in range(SUB):
+        if index % (SUB // CHUNKS) == 0:
+            up_copies[index // (SUB // CHUNKS)].wait()
         moved = jnp.dot(
             coeff, up_in[:, index * piece : (index + 1) * piece], preferred_element_type=jnp.float32
         ) * (1.0 / math.sqrt(latent_count))
@@ -568,7 +579,7 @@
         scratch_shapes=[
             stage_type(capacity),
             pltpu.VMEM(factor_type.shape, factor_type.dtype),
-            pltpu.SemaphoreType.DMA,
+            pltpu.SemaphoreType.DMA((CHUNKS,)),
         ],
     )(me, second_tags, down_factor, up_factor, first_coeff, second_arrived)
     returned = exchange(update)

time: 136 us -> 136 us (level)
  no operation moved by 1% of the time
where the time goes in v8:
time: 136 us
  blocking collectives  77.5 us (57%)
  Pallas kernels  29.5 us (22%)
  starting transfers between devices  12.3 us (9%)
  waiting for transfers between devices  12.2 us (9%)
  local copies, waits for them, and re-layouts  3.37 us (2%)
    all_to_all x1, blocking collectives, exchange(): lax.all_to_all(values.reshape(blocks, SUB, -1), ALL, split_axis=0, concat...  57.8 us
    all_gather x1, blocking collectives, on_device(): gathered = lax.all_gather(jnp.stack(fetched), 'ctx')  13.3 us
    all_to_all x2, waiting for transfers between devices, exchange(): lax.all_to_all(values.reshape(blocks, SUB, -1), ALL, split_axis=0, concat...  12.2 us
    all_to_all x2, starting transfers between devices, exchange(): lax.all_to_all(values.reshape(blocks, SUB, -1), ALL, split_axis=0, concat...  10.5 us
    pallas_call x1, Pallas kernels, on_device(): call(functools.partial(attend_kernel, chunks, tag_parts), 'attend', vmem=...  8.19 us
    pallas_call x1, Pallas kernels, on_device(): call(functools.partial(factor_kernel, blocks, capacity, early, latent_cou...  7.43 us
    all_gather x1, blocking collectives, on_device(): lax.all_gather(partial, 'ctx')  6.37 us
    pallas_call x1, Pallas kernels, on_device(): call(functools.partial(place_more_kernel, blocks, early, late), 'place_mo...  3.64 us
  transfers between devices with their start and end apart: 4, of which 2 were waited for; matrix products, arithmetic and copies ran while one was open for 1% of the time, Pallas kernels for 15%

profile of v8, /device:TPU:0, one launch (start us, length us, event | category | flops | bytes accessed | tf_op | source)
XLA Modules:
  0.0 135.8 jit_solution(4805034007380123268)
XLA Ops:
  0.0 3.4 %place_rows.1 = (bf16[256,1920]{1,0:T(8,128)(2,1)}, s32[1,192]{1,0:T(1,128)}) custom-call(s32[1,32]{1,0:T(1,128)} %bitcast.36, s32[1,192]{1,0:T(1,128)} %bitcast.34, bf16[192,5120]{1,0:T(8,128)(2,1)} %requests.3), custom_call_target="tpu_custom_call" | custom-call | tf_op jit(solution)/shard_map/place_rows/pallas_call | solution.py:470
  3.4 7.3 %all-to-all-start = ((bf16[32,8,1920]{2,1,0:T(8,128)(2,1)}), bf16[32,8,1920]{2,1,0:T(8,128)(2,1)S(1)}, u32[]{:S(2)}, u32[]{:S(2)}) async-start(bf16[32,8,1920]{2,1,0:T(8,128)(2,1)} %bitcast.31), calls=%async_computation | async-start | bytes 1966080 | tf_op jit(solution)/shard_map/all_to_all | solution.py:466
  10.7 0.0 copy-start.5
  10.7 0.0 copy-start.6
  10.7 0.0 copy-start.10
  10.7 8.2 %attend.1 = f32[72,128]{1,0:T(8,128)} custom-call(bf16[1,256,5120]{2,1,0:T(8,128)(2,1)} %tokens.1, bf16[5120,512]{1,0:T(8,128)(2,1)} %w_keys.1, bf16[5120,512]{1,0:T(8,128)(2,1)} %w_values.1, f32[16,512]{1,0:T(8,128)} %latents.3, s32[1,192]{1,0:T(1,128)} %get-tuple-element.19.slots, s32[1,192]{1,0:T(1,128)} %bitcast.35), custom_call_target="tpu_custom_call" | custom-call | tf_op jit(solution)/shard_map/attend/pallas_call | solution.py:498
  18.9 6.4 %all-gather = f32[288,128]{1,0:T(8,128)S(1)} all-gather(f32[72,128]{1,0:T(8,128)} %attend.1), channel_id=2, replica_groups=mesh['doc'=8,'ctx'=4] {'ctx'}, dimensions={0}, use_global_device_ids=true | all-gather | bytes 184320 | tf_op jit(solution)/shard_map/all_gather | solution.py:516
  25.3 0.0 copy-done.5
  25.3 0.0 copy-done.6
  25.3 0.4 summarize.1
  25.6 1.1 collective-permute-start.1
  26.8 0.7 collective-permute-start
  27.4 3.6 %place_more.1 = bf16[256,2560]{1,0:T(8,128)(2,1)} custom-call(s32[1,192]{1,0:T(1,128)} %get-tuple-element.19.slots, bf16[192,5120]{1,0:T(8,128)(2,1)} %requests.3), custom_call_target="tpu_custom_call" | custom-call | tf_op jit(solution)/shard_map/place_more/pallas_call | solution.py:529
  31.1 0.0 collective-permute-done.1
  31.1 0.0 collective-permute-done
  31.1 5.6 %all-to-all-done = bf16[32,8,1920]{2,1,0:T(8,128)(2,1)S(1)} async-done(((bf16[32,8,1920]{2,1,0:T(8,128)(2,1)}), bf16[32,8,1920]{2,1,0:T(8,128)(2,1)S(1)}, u32[]{:S(2)}, u32[]{:S(2)}) %all-to-all-start) | async-done | bytes 983072 | tf_op jit(solution)/shard_map/all_to_all | solution.py:466
  36.7 3.2 %all-to-all-start.1 = ((bf16[32,8,2560]{2,1,0:T(8,128)(2,1)}), bf16[32,8,2560]{2,1,0:T(8,128)(2,1)S(1)}, u32[]{:S(2)}, u32[]{:S(2)}) async-start(bf16[32,8,2560]{2,1,0:T(8,128)(2,1)} %bitcast.29), calls=%async_computation.1 | async-start | bytes 2621440 | tf_op jit(solution)/shard_map/all_to_all | solution.py:466
  40.0 13.3 %all-gather.1 = bf16[8,32,512]{2,1,0:T(8,128)(2,1)S(1)} all-gather(bf16[2,32,512]{2,1,0:T(8,128)(2,1)S(1)} %pad_maximum_fusion.1), channel_id=3, replica_groups=mesh['doc'=8,'ctx'=4] {'ctx'}, dimensions={0}, use_global_device_ids=true | all-gather | bytes 327680 | tf_op jit(solution)/shard_map/all_gather | solution.py:537
  53.3 0.7 pad_maximum_fusion
  54.0 7.4 %factors.1 = (bf16[128,5120]{1,0:T(8,128)(2,1)}, bf16[128,163840]{1,0:T(8,128)(2,1)}, s32[96,1]{1,0:T(8,128)}, s32[128,1]{1,0:T(8,128)}) custom-call(s32[1,1]{1,0:T(1,128)} %bitcast.me, bf16[8,32,512]{2,1,0:T(8,128)(2,1)} %bitcast.30, bf16[1,512,5120]{2,1,0:T(8,128)(2,1)} %heads_down.1, bf16[1,512,5120]{2,1,0:T(8,128)(2,1)} %heads_up.1), custom_call_target="tpu_custom_call" | custom-call | tf_op jit(solution)/shard_map/factors/pallas_call | solution.py:550
  61.5 0.0 copy-start.1
  61.5 1.3 copy-done.1
  62.8 1.2 copy-done.4
  64.0 0.8 copy-done.8
  64.8 0.7 coefficients.1.first_coeff
  65.5 6.6 %all-to-all-done.1 = bf16[32,8,2560]{2,1,0:T(8,128)(2,1)S(1)} async-done(((bf16[32,8,2560]{2,1,0:T(8,128)(2,1)}), bf16[32,8,2560]{2,1,0:T(8,128)(2,1)S(1)}, u32[]{:S(2)}, u32[]{:S(2)}) %all-to-all-start.1) | async-done | bytes 1310752 | tf_op jit(solution)/shard_map/all_to_all | solution.py:466
  72.1 0.0 copy-done.7
  72.1 3.2 %update.1 = bf16[256,4480]{1,0:T(8,128)(2,1)S(1)} custom-call(s32[1,1]{1,0:T(1,128)} %bitcast.me, s32[128,1]{1,0:T(8,128)S(1)} %copy-done.7, bf16[128,5120]{1,0:T(8,128)(2,1)S(1)} %copy-done.2, bf16[128,163840]{1,0:T(8,128)(2,1)} %get-tuple-element.16.up, bf16[96,128]{1,0:T(8,128)(2,1)S(1)} %coefficients.1.first_coeff, bf16[256,2560]{1,0:T(8,128)(2,1)S(1)} %bitcast.25), custom_call_target="tpu_custom_call" | custom-call | tf_op jit(solution)/shard_map/update/pallas_call | solution.py:574
  75.3 0.0 copy-start
  75.3 57.8 %all_to_all.15 = bf16[32,8,4480]{2,1,0:T(8,128)(2,1)S(1)} all-to-all(bf16[32,8,4480]{2,1,0:T(8,128)(2,1)S(1)} %bitcast.23), channel_id=1, replica_groups=mesh['doc'=8,'ctx'=4] {'doc','ctx'}, dimensions={0} | all-to-all | bytes 4587520 | tf_op jit(solution)/shard_map/all_to_all | solution.py:466
  133.1 0.0 copy-done
  133.1 2.6 %finish_rows.1 = bf16[192,5120]{1,0:T(8,128)(2,1)} custom-call(bf16[256,4480]{1,0:T(8,128)(2,1)S(1)} %bitcast.24, s32[1,192]{1,0:T(1,128)S(1)} %copy-done.9, bf16[192,5120]{1,0:T(8,128)(2,1)S(1)} %copy-done), custom_call_target="tpu_custom_call" | custom-call | tf_op jit(solution)/shard_map/finish_rows/pallas_call | solution.py:586
  (12 shorter events, 0.0 us)
Async XLA Ops:
  3.4 33.3 %all-to-all-start = ((bf16[32,8,1920]{2,1,0:T(8,128)(2,1)}), bf16[32,8,1920]{2,1,0:T(8,128)(2,1)S(1)}, u32[]{:S(2)}, u32[]{:S(2)}) async-start(bf16[32,8,1920]{2,1,0:T(8,128)(2,1)} %bitcast.31), calls=%async_computation | async-start | bytes 1966080 | tf_op jit(solution)/shard_map/all_to_all | solution.py:466
  10.7 14.6 %copy-start.5 = (bf16[512,512]{1,0:T(8,128)(2,1)S(1)}, bf16[512,512]{1,0:T(8,128)(2,1)}, u32[]{:S(2)}) copy-start(bf16[512,512]{1,0:T(8,128)(2,1)} %w_out.1) | copy-start | bytes 1572868
  10.7 14.6 %copy-start.6 = (f32[16,512]{1,0:T(8,128)S(1)}, f32[16,512]{1,0:T(8,128)}, u32[]{:S(2)}) copy-start(f32[16,512]{1,0:T(8,128)} %latents.3) | copy-start | bytes 98308
  10.7 14.6 %copy-start.10 = (f32[512]{0:T(512)S(1)}, f32[512]{0:T(512)}, u32[]{:S(2)}) copy-start(f32[512]{0:T(512)} %param.17) | copy-start | bytes 6148
  25.6 5.4 %collective-permute-start.1 = (bf16[32,512]{1,0:T(8,128)(2,1)S(1)}, bf16[32,512]{1,0:T(8,128)(2,1)S(1)}, u32[]{:S(2)}, u32[]{:S(2)}) collective-permute-start(bf16[32,512]{1,0:T(8,128)(2,1)S(1)} %summarize.1), channel_id=1, source_target_pairs={{0,4},{1,21},{2,14},{3,31},{4,0},{5,17},{6,10},{7,27},{8,12},{9,29... | collective-permute-start | bytes 98312 | tf_op jit(solution)/shard_map/ppermute | solution.py:528
  26.8 4.3 %collective-permute-start = (bf16[32,512]{1,0:T(8,128)(2,1)S(1)}, bf16[32,512]{1,0:T(8,128)(2,1)S(1)}, u32[]{:S(2)}, u32[]{:S(2)}) collective-permute-start(bf16[32,512]{1,0:T(8,128)(2,1)S(1)} %summarize.1), channel_id=1, source_target_pairs={{0,0},{1,17},{2,10},{3,27},{4,4},{5,21},{6,14},{7,31},{8,8},{9,25}... | collective-permute-start | bytes 98312 | tf_op jit(solution)/shard_map/ppermute | solution.py:528
  36.7 24.8 %copy-start.3 = (bf16[32,8,1920]{2,1,0:T(8,128)(2,1)}, bf16[32,8,1920]{2,1,0:T(8,128)(2,1)S(1)}, u32[]{:S(2)}) copy-start(bf16[32,8,1920]{2,1,0:T(8,128)(2,1)S(1)} %all-to-all-done) | copy-start | bytes 2949124
  36.7 35.4 %all-to-all-start.1 = ((bf16[32,8,2560]{2,1,0:T(8,128)(2,1)}), bf16[32,8,2560]{2,1,0:T(8,128)(2,1)S(1)}, u32[]{:S(2)}, u32[]{:S(2)}) async-start(bf16[32,8,2560]{2,1,0:T(8,128)(2,1)} %bitcast.29), calls=%async_computation.1 | async-start | bytes 2621440 | tf_op jit(solution)/shard_map/all_to_all | solution.py:466
  61.5 1.3 copy-start.1
  62.8 1.2 copy-start.4
  64.0 0.8 copy-start.8
  64.8 7.3 %copy-start.2 = (bf16[128,5120]{1,0:T(8,128)(2,1)S(1)}, bf16[128,5120]{1,0:T(8,128)(2,1)}, u32[]{:S(2)}) copy-start(bf16[128,5120]{1,0:T(8,128)(2,1)} %get-tuple-element.15.down) | copy-start | bytes 3932164
  64.8 7.3 %copy-start.7 = (s32[128,1]{1,0:T(8,128)S(1)}, s32[128,1]{1,0:T(8,128)}, u32[]{:S(2)}) copy-start(s32[128,1]{1,0:T(8,128)} %get-tuple-element.14.tags) | copy-start | bytes 1540
  75.3 57.8 %copy-start = (bf16[192,5120]{1,0:T(8,128)(2,1)S(1)}, bf16[192,5120]{1,0:T(8,128)(2,1)}, u32[]{:S(2)}) copy-start(bf16[192,5120]{1,0:T(8,128)(2,1)} %requests.3) | copy-start | bytes 5898244
  75.3 57.8 %copy-start.9 = (s32[1,192]{1,0:T(1,128)S(1)}, s32[1,192]{1,0:T(1,128)}, u32[]{:S(2)}) copy-start(s32[1,192]{1,0:T(1,128)} %get-tuple-element.19.slots) | copy-start | bytes 2308
